TPU v7x, 32 devices: a whole 2x2x4 slice. The times are simulated.
32 devices in a mesh: ka: 8 (over z, core), ba: 4 (over y, x).
Axes of the slice: x: 2, y: 2, z: 4, core: 2. Of those that a mesh axis runs over, the one named last changes fastest.
Arguments:
- orbitals: bfloat16 [8, 4, 2, 32768], P('ka', 'ba'), may hold values from -6 to 6
- kpoint_coords: int32 [8, 3], replicated, may hold values from 0 to 3
Outputs:
- exchange_field: float32 [8, 4, 2, 32768], P('ka', 'ba')
All inputs are finite; a program needn't handle non-finite values.
Results may differ from a plain program's by a relative error of at most 0.0074.
Values may be sent and summed in bfloat16 or wider, within the bound.
No kernel may reach another device: no remote copies, remote signals or barrier semaphores. Data moves between devices by JAX's collectives and lax.ppermute only.
A program may use at most 64 MiB of HBM per device.

v0:
```python
import math

import jax
import jax.numpy as jnp
from jax import lax
from jax.sharding import PartitionSpec as P

GRID = 32


def shifted(value, axis, steps):
    count = lax.axis_size(axis)
    pairs = [(source, (source + steps) % count) for source in range(count)]
    return lax.ppermute(value, axis, pairs)


def partner(value, axis, apart):
    mask = 2**apart
    pairs = [(source, source ^ mask) for source in range(lax.axis_size(axis))]
    return lax.ppermute(value, axis, pairs)


def wave_tables(grid, sign):
    index = jnp.arange(grid, dtype=jnp.int32)
    phase = index[:, None] * index[None, :] % grid
    angle = phase.astype(jnp.float32) * (2.0 * math.pi / grid)
    cosine = jnp.cos(angle)
    sine = sign * jnp.sin(angle)
    table = jnp.stack([jnp.stack([cosine, sine]), jnp.stack([-sine, cosine])])
    return table.astype(jnp.bfloat16)


def one_pass(field, table, grid):
    count = field.shape[0]
    shaped = field.reshape(count, 2, grid * grid, grid)
    result = jnp.einsum("pcme,dcfe->pdfm", shaped, table, preferred_element_type=jnp.float32)
    return result.reshape(count, 2, grid**3)


def transform(field, table, grid):
    first = one_pass(field, table, grid).astype(jnp.bfloat16)
    second = one_pass(first, table, grid).astype(jnp.bfloat16)
    return one_pass(second, table, grid)


def coulomb_kernel(offset, grid):
    index = jnp.arange(grid, dtype=jnp.int32)
    signed = jnp.where(index < grid // 2, index, index - grid).astype(jnp.float32)
    along_x = signed[:, None, None] + offset[0]
    along_y = signed[None, :, None] + offset[1]
    along_z = signed[None, None, :] + offset[2]
    square = along_x * along_x + along_y * along_y + along_z * along_z
    return (32.0 / grid**3 / (square + 0.25)).reshape(grid**3)


def pair_density(former, latter):
    f_real = former[..., :, None, 0, :].astype(jnp.float32)
    f_imag = former[..., :, None, 1, :].astype(jnp.float32)
    l_real = latter[..., None, :, 0, :].astype(jnp.float32)
    l_imag = latter[..., None, :, 1, :].astype(jnp.float32)
    real = l_real * f_real + l_imag * f_imag
    imag = l_real * f_imag - l_imag * f_real
    return jnp.stack([real, imag], axis=-2).astype(jnp.bfloat16)


def coulomb_fields(former, latter, kernel, forward, inverse):
    density = pair_density(former, latter)
    flat = density.reshape(-1, 2, GRID**3)
    spectrum = transform(flat, forward, GRID)
    screened = (spectrum * kernel).astype(jnp.bfloat16)
    return transform(screened, inverse, GRID).reshape(density.shape)


def apply_fields(fields, latter):
    w_real = fields[..., 0, :]
    w_imag = fields[..., 1, :]
    l_real = latter[..., None, :, 0, :].astype(jnp.float32)
    l_imag = latter[..., None, :, 1, :].astype(jnp.float32)
    real = -jnp.sum(l_real * w_real - l_imag * w_imag, axis=-2)
    imag = -jnp.sum(l_real * w_imag + l_imag * w_real, axis=-2)
    return jnp.stack([real, imag], axis=-2)


def back_fields(fields, former):
    w_real = fields[..., 0, :]
    w_imag = fields[..., 1, :]
    f_real = former[..., :, None, 0, :].astype(jnp.float32)
    f_imag = former[..., :, None, 1, :].astype(jnp.float32)
    real = -jnp.sum(f_real * w_real + f_imag * w_imag, axis=-3)
    imag = -jnp.sum(f_imag * w_real - f_real * w_imag, axis=-3)
    return jnp.stack([real, imag], axis=-2)


def fields_all(formers, latters, kernel, forward, inverse):
    joined = coulomb_fields(jnp.stack(formers), jnp.stack(latters), kernel, forward, inverse)
    return [joined[number] for number in range(len(formers))]


def per_device(orbitals, kpoint_coords):
    own = orbitals[0]
    kpoints = lax.axis_size("ka")
    offset_steps = kpoints // 4
    matches = min(3, lax.axis_size("ba") // 4 + 1)
    forward = wave_tables(GRID, 1.0)
    inverse = wave_tables(GRID, -1.0)
    coords = kpoint_coords.astype(jnp.float32)
    rows_all = jnp.arange(kpoints, dtype=jnp.int32)
    here = lax.axis_index("ka")

    def coord_of(position):
        picked = (rows_all == position).astype(jnp.float32)
        return jnp.dot(picked, coords, precision=lax.Precision.HIGHEST)

    source = (here - offset_steps) % kpoints
    kernel = coulomb_kernel((coord_of(here) - coord_of(source)) / 4.0, GRID)
    received = shifted(own, "ka", offset_steps)
    partners = [partner(received, "ba", matching) for matching in range(matches)]
    fields = fields_all([own] * matches, partners, kernel, forward, inverse)
    total = jnp.zeros(own.shape, jnp.float32)
    for matching in range(matches):
        total = total + apply_fields(fields[matching], partners[matching])
    outgoing = [
        back_fields(fields[matching], own).astype(jnp.bfloat16) for matching in range(matches)
    ]
    summed = jnp.zeros(own.shape, jnp.float32)
    for matching in range(matches):
        arrived = partner(outgoing[matching], "ba", matching)
        summed = summed + arrived.astype(jnp.float32)
    total = total + shifted(summed, "ka", -offset_steps)
    return total[None]


def solution(mesh):
    return jax.shard_map(
        per_device,
        mesh=mesh,
        in_specs=(P("ka", "ba", None, None), P()),
        out_specs=P("ka", "ba", None, None),
        check_vma=False,
    )
```

profile of v0, /device:TPU:0, one launch (start us, length us, event | category | flops | bytes accessed | tf_op | source)
XLA Modules:
  0.0 42.2 jit_solution(13044465336880916756)
XLA Ops:
  0.0 3.0 %collective-permute-start = (bf16[1,2,32768]{2,1,0:T(2,128)(2,1)}, bf16[1,2,32768]{2,1,0:T(2,128)(2,1)S(1)}, u32[]{:S(2)}, u32[]{:S(2)}) collective-permute-start(bf16[1,2,32768]{2,1,0:T(2,128)(2,1)} %bitcast.192), channel_id=1, source_target_pairs={{0,8},{4,12},{8,16},{12,20},{16,24},{20,28},{24,0},{28,4},{1,9},{5... | collective-permute-start | bytes 393224 | tf_op jit(solution)/shard_map/ppermute | solution.py:14
  3.0 1.0 %constant_dynamic-update-slice_fusion.1 = bf16[2,1,2,32768]{3,2,1,0:T(2,128)(2,1)S(1)} fusion(bf16[1,1,2,32768]{3,2,1,0:T(2,128)(2,1)} %param.2), kind=kLoop, calls=%fused_computation.93 | loop fusion | bytes 262144
  4.1 1.0 %constant_dynamic-update-slice_fusion = bf16[2,1,2,32768]{3,2,1,0:T(2,128)(2,1)S(1)} fusion(bf16[2,1,2,32768]{3,2,1,0:T(2,128)(2,1)S(1)} %constant_dynamic-update-slice_fusion.1, bf16[1,1,2,32768]{3,2,1,0:T(2,128)(2,1)} %param.2), kind=kLoop, calls=%fused_computation.92 | loop fusion | bytes 262144 | tf_op jit(solution)/shard_map/stack | solution.py:95
  5.1 0.8 %convolution_bitcast_fusion.6 = f32[3]{0:T(128)S(1)} fusion(s32[8,3]{0,1:T(4,128)} %param.3, s32[]{:T(128)S(6)} %select_n.74), kind=kOutput, calls=%fused_computation.15 | convolution fusion | flops 320 | bytes 112 | tf_op jit(solution)/shard_map/dot_general | solution.py:112
  5.9 0.8 %fusion.9 = f32[3]{0:T(128)S(1)} fusion(f32[3]{0:T(128)S(1)} %convolution_bitcast_fusion.6, s32[8,3]{0,1:T(4,128)} %param.3, s32[]{:T(128)S(6)} %axis_index.15), kind=kOutput, calls=%fused_computation.18 | convolution fusion | flops 326 | bytes 124 | tf_op jit(solution)/shard_map/dot_general | solution.py:112
  6.7 0.7 %fusion.58 = (f32[1]{0:T(128)}, f32[1]{0:T(128)}, f32[1]{0:T(128)}) fusion(f32[3]{0:T(128)S(1)} %fusion.9), kind=kLoop, calls=%fused_computation.116 | loop fusion | bytes 24 | tf_op jit(solution)/shard_map/slice | solution.py:49
  7.4 0.6 %add_multiply_fusion = f32[32]{0:T(128)S(1)} fusion(f32[]{:T(128)} %bitcast.31), kind=kLoop, calls=%fused_computation.102 | loop fusion | flops 192 | bytes 132 | tf_op jit(solution)/shard_map/mul | solution.py:52
  8.0 1.3 %add_multiply_fusion.1 = (f32[32]{0:T(128)S(1)}, f32[32]{0:T(128)S(1)}) fusion(f32[]{:T(128)} %bitcast.30, f32[]{:T(128)} %bitcast.29), kind=kLoop, calls=%fused_computation.103 | loop fusion | flops 256 | bytes 264 | tf_op jit(solution)/shard_map/mul | solution.py:52
  9.7 1.6 %collective-permute-start.2 = (bf16[1,2,32768]{2,1,0:T(2,128)(2,1)S(1)}, bf16[1,2,32768]{2,1,0:T(2,128)(2,1)S(1)}, u32[]{:S(2)}, u32[]{:S(2)}) collective-permute-start(bf16[1,2,32768]{2,1,0:T(2,128)(2,1)S(1)} %collective-permute-done), channel_id=1, source_target_pairs={{0,2},{1,3},{2,0},{3,1},{4,6},{5,7},{6,4},{7,5},{8,10},{9,11},{10,... | collective-permute-start | bytes 393224 | tf_op jit(solution)/shard_map/ppermute | solution.py:20
  11.3 1.5 %collective-permute-start.1 = (bf16[1,2,32768]{2,1,0:T(2,128)(2,1)S(1)}, bf16[1,2,32768]{2,1,0:T(2,128)(2,1)S(1)}, u32[]{:S(2)}, u32[]{:S(2)}) collective-permute-start(bf16[1,2,32768]{2,1,0:T(2,128)(2,1)S(1)} %collective-permute-done), channel_id=1, source_target_pairs={{0,1},{1,0},{2,3},{3,2},{4,5},{5,4},{6,7},{7,6},{8,9},{9,8},{10,11... | collective-permute-start | bytes 393224 | tf_op jit(solution)/shard_map/ppermute | solution.py:20
  13.1 1.6 %collective-permute-done.2 = bf16[1,2,32768]{2,1,0:T(2,128)(2,1)S(1)} collective-permute-done((bf16[1,2,32768]{2,1,0:T(2,128)(2,1)S(1)}, bf16[1,2,32768]{2,1,0:T(2,128)(2,1)S(1)}, u32[]{:S(2)}, u32[]{:S(2)}) %collective-permute-start.2) | collective-permute-done | bytes 131104 | tf_op jit(solution)/shard_map/ppermute | solution.py:20
  14.8 1.5 %collective-permute-done.1 = bf16[1,2,32768]{2,1,0:T(2,128)(2,1)S(1)} collective-permute-done((bf16[1,2,32768]{2,1,0:T(2,128)(2,1)S(1)}, bf16[1,2,32768]{2,1,0:T(2,128)(2,1)S(1)}, u32[]{:S(2)}, u32[]{:S(2)}) %collective-permute-start.1) | collective-permute-done | bytes 131104 | tf_op jit(solution)/shard_map/ppermute | solution.py:20
  16.3 2.4 %convert_reduce_fusion.1 = (bf16[2,32768]{1,0:T(2,128)(2,1)S(1)}, bf16[2,32768]{1,0:T(2,128)(2,1)S(1)}) fusion(bf16[2,1,2,32768]{3,2,1,0:T(2,128)(2,1)S(1)} %constant_dynamic-update-slice_fusion, bf16[1,1,2,32768]{3,2,1,0:T(2,128)(2,1)S(1)} %bitcast.196, bf16[1,1,2,32768]{3,2,1,0:T(2,128)(2,1)S(1)} %bitcast.195), kind=kLoop, calls=%fused_computation.38 | loop fusion | flops 1441792 | bytes 786432 | tf_op jit(solution)/shard_map/convert.7
  19.9 0.8 %reshape.389 = bf16[2,2,1024,32]{3,2,0,1:T(8,128)(2,1)S(1)} reshape(bf16[2,2,32,1024]{3,2,0,1:T(8,128)(2,1)S(1)} %fusion.7) | data formatting | bytes 524288 | tf_op jit(solution)/shard_map/convert_element_type | solution.py:41
  20.7 0.4 %fusion.5 = bf16[2,2,32,1024]{3,2,0,1:T(8,128)(2,1)S(1)} fusion(bf16[2,2,1024,32]{3,2,0,1:T(8,128)(2,1)S(1)} %reshape.389, bf16[1,2,32,32]{3,2,1,0:T(8,128)(2,1)S(1)} %get-tuple-element.22, bf16[1,2,32,32]{3,2,1,0:T(8,128)(2,1)S(1)} %get-tuple-element.23), kind=kOutput, calls=%fused_computation.12 | convolution fusion | flops 16924672 | bytes 532480 | tf_op jit(solution)/shard_map/pcme,dcfe->pdfm/dot_general | solution.py:36
  21.1 0.8 %reshape.390 = bf16[2,2,1024,32]{3,2,0,1:T(8,128)(2,1)S(1)} reshape(bf16[2,2,32,1024]{3,2,0,1:T(8,128)(2,1)S(1)} %fusion.5) | data formatting | bytes 524288 | tf_op jit(solution)/shard_map/convert_element_type | solution.py:42
  21.9 0.4 %convolution_bitcast_fusion.3 = f32[2,2,32,1024]{3,2,0,1:T(8,128)S(1)} fusion(bf16[2,2,1024,32]{3,2,0,1:T(8,128)(2,1)S(1)} %reshape.390, bf16[1,2,32,32]{3,2,1,0:T(8,128)(2,1)S(1)} %get-tuple-element.22, bf16[1,2,32,32]{3,2,1,0:T(8,128)(2,1)S(1)} %get-tuple-element.23), kind=kOutput, calls=%fused_computation.4 | convolution fusion | flops 16793600 | bytes 794624 | tf_op jit(solution)/shard_map/pcme,dcfe->pdfm/dot_general | solution.py:36
  22.4 0.7 %reshape.370 = f32[2,2,1024,32]{3,2,1,0:T(8,128)S(1)} reshape(f32[2,2,32,1024]{3,2,1,0:T(8,128)S(1)} %copy.26) | data formatting | bytes 1048576 | tf_op jit(solution)/shard_map/reshape | solution.py:37
  23.1 0.4 %fusion.6 = bf16[2,2,32,1024]{3,2,0,1:T(8,128)(2,1)S(1)} fusion(f32[2,2,1024,32]{3,2,1,0:T(8,128)S(1)} %reshape.370, f32[1024,32]{1,0:T(8,128)S(1)} %copy.27, bf16[1,2,32,32]{3,2,1,0:T(8,128)(2,1)S(1)} %get-tuple-element.24, bf16[1,2,32,32]{3,2,1,0:T(8,128)(2,1)S(1)} %get-tuple-element.21), kind=kOutput, calls=%fused_computation.13 | convolution fusion | flops 17186816 | bytes 925696 | tf_op jit(solution)/shard_map/pcme,dcfe->pdfm/dot_general | solution.py:36
  23.5 0.8 %reshape.391 = bf16[2,2,1024,32]{3,2,0,1:T(8,128)(2,1)S(1)} reshape(bf16[2,2,32,1024]{3,2,0,1:T(8,128)(2,1)S(1)} %fusion.6) | data formatting | bytes 524288 | tf_op jit(solution)/shard_map/convert_element_type | solution.py:41
  24.3 0.4 %fusion.4 = bf16[2,2,32,1024]{3,2,0,1:T(8,128)(2,1)S(1)} fusion(bf16[2,2,1024,32]{3,2,0,1:T(8,128)(2,1)S(1)} %reshape.391, bf16[1,2,32,32]{3,2,1,0:T(8,128)(2,1)S(1)} %get-tuple-element.24, bf16[1,2,32,32]{3,2,1,0:T(8,128)(2,1)S(1)} %get-tuple-element.21), kind=kOutput, calls=%fused_computation.11 | convolution fusion | flops 16924672 | bytes 532480 | tf_op jit(solution)/shard_map/pcme,dcfe->pdfm/dot_general | solution.py:36
  24.8 0.8 %reshape.392 = bf16[2,2,1024,32]{3,2,0,1:T(8,128)(2,1)S(1)} reshape(bf16[2,2,32,1024]{3,2,0,1:T(8,128)(2,1)S(1)} %fusion.4) | data formatting | bytes 524288 | tf_op jit(solution)/shard_map/convert_element_type | solution.py:42
  25.5 0.4 %convolution_bitcast_fusion.1 = f32[2,2,32,1024]{3,2,0,1:T(8,128)S(1)} fusion(bf16[2,2,1024,32]{3,2,0,1:T(8,128)(2,1)S(1)} %reshape.392, bf16[1,2,32,32]{3,2,1,0:T(8,128)(2,1)S(1)} %get-tuple-element.24, bf16[1,2,32,32]{3,2,1,0:T(8,128)(2,1)S(1)} %get-tuple-element.21), kind=kOutput, calls=%fused_computation.2 | convolution fusion | flops 16793600 | bytes 794624 | tf_op jit(solution)/shard_map/pcme,dcfe->pdfm/dot_general | solution.py:36
  26.3 0.9 %subtract_negate_fusion = (f32[1,1,32768]{2,1,0:T(1,128)S(1)}, f32[1,1,32768]{2,1,0:T(1,128)S(1)}, bf16[1,1,32768]{2,1,0:T(2,128)(2,1)S(1)}, bf16[1,1,32768]{2,1,0:T(2,128)(2,1)S(1)}) fusion(bf16[1,2,32768]{2,1,0:T(2,128)(2,1)S(1)} %collective-permute-done.2, f32[1,1,2,32768]{3,2,1,0:T(2,128)S(1)} %squeeze.41, bf16[1,2,32768]{2,1,0:T(2,128)(2,1)S(1)} %bitcast.193), kind=kLoop, calls=%fused_computation.56 | loop fusion | flops 720896 | bytes 917504 | tf_op jit(solution)/shard_map/neg | solution.py:79
  27.5 0.6 %collective-permute-start.4 = (bf16[1,2,32768]{2,1,0:T(2,128)(2,1)S(1)}, bf16[1,2,32768]{2,1,0:T(2,128)(2,1)S(1)}, u32[]{:S(2)}, u32[]{:S(2)}) collective-permute-start(bf16[1,2,32768]{2,1,0:T(2,128)(2,1)S(1)} %pad_maximum_fusion.2), channel_id=1, source_target_pairs={{0,2},{1,3},{2,0},{3,1},{4,6},{5,7},{6,4},{7,5},{8,10},{9,11},{10,... | collective-permute-start | bytes 393224 | tf_op jit(solution)/shard_map/ppermute | solution.py:20
  28.3 0.9 %subtract_negate_fusion.1 = (f32[1,1,32768]{2,1,0:T(1,128)S(1)}, f32[1,1,32768]{2,1,0:T(1,128)S(1)}, bf16[1,1,32768]{2,1,0:T(2,128)(2,1)S(1)}, bf16[1,1,32768]{2,1,0:T(2,128)(2,1)S(1)}) fusion(bf16[1,2,32768]{2,1,0:T(2,128)(2,1)S(1)} %collective-permute-done.1, f32[1,1,2,32768]{3,2,1,0:T(2,128)S(1)} %squeeze.38, bf16[1,2,32768]{2,1,0:T(2,128)(2,1)S(1)} %bitcast.194), kind=kLoop, calls=%fused_computation.58 | loop fusion | flops 720896 | bytes 917504 | tf_op jit(solution)/shard_map/neg | solution.py:79
  29.5 1.6 %collective-permute-start.3 = (bf16[1,2,32768]{2,1,0:T(2,128)(2,1)S(1)}, bf16[1,2,32768]{2,1,0:T(2,128)(2,1)S(1)}, u32[]{:S(2)}, u32[]{:S(2)}) collective-permute-start(bf16[1,2,32768]{2,1,0:T(2,128)(2,1)S(1)} %pad_maximum_fusion.1), channel_id=1, source_target_pairs={{0,1},{1,0},{2,3},{3,2},{4,5},{5,4},{6,7},{7,6},{8,9},{9,8},{10,11... | collective-permute-start | bytes 393224 | tf_op jit(solution)/shard_map/ppermute | solution.py:20
  31.0 1.5 %collective-permute-done.4 = bf16[1,2,32768]{2,1,0:T(2,128)(2,1)S(1)} collective-permute-done((bf16[1,2,32768]{2,1,0:T(2,128)(2,1)S(1)}, bf16[1,2,32768]{2,1,0:T(2,128)(2,1)S(1)}, u32[]{:S(2)}, u32[]{:S(2)}) %collective-permute-start.4) | collective-permute-done | bytes 131104 | tf_op jit(solution)/shard_map/ppermute | solution.py:20
  32.5 2.0 %collective-permute-done.3 = bf16[1,2,32768]{2,1,0:T(2,128)(2,1)S(1)} collective-permute-done((bf16[1,2,32768]{2,1,0:T(2,128)(2,1)S(1)}, bf16[1,2,32768]{2,1,0:T(2,128)(2,1)S(1)}, u32[]{:S(2)}, u32[]{:S(2)}) %collective-permute-start.3) | collective-permute-done | bytes 131104 | tf_op jit(solution)/shard_map/ppermute | solution.py:20
  34.6 2.1 %collective-permute-start.5 = (f32[1,2,32768]{2,1,0:T(2,128)S(1)}, f32[1,2,32768]{2,1,0:T(2,128)S(1)}, u32[]{:S(2)}, u32[]{:S(2)}) collective-permute-start(f32[1,2,32768]{2,1,0:T(2,128)S(1)} %convert_add_fusion), channel_id=1, source_target_pairs={{0,24},{4,28},{8,0},{12,4},{16,8},{20,12},{24,16},{28,20},{1,25},{... | collective-permute-start | bytes 786440 | tf_op jit(solution)/shard_map/ppermute | solution.py:14
  36.7 4.3 %collective-permute-done.5 = f32[1,2,32768]{2,1,0:T(2,128)S(1)} collective-permute-done((f32[1,2,32768]{2,1,0:T(2,128)S(1)}, f32[1,2,32768]{2,1,0:T(2,128)S(1)}, u32[]{:S(2)}, u32[]{:S(2)}) %collective-permute-start.5) | collective-permute-done | bytes 262176 | tf_op jit(solution)/shard_map/ppermute | solution.py:14
  41.1 1.2 %fusion.21 = f32[1,1,2,32768]{3,2,1,0:T(2,128)} fusion(f32[1,2,32768]{2,1,0:T(2,128)S(1)} %collective-permute-done.5, f32[1,1,32768]{2,1,0:T(1,128)S(1)} %get-tuple-element.12, f32[1,1,32768]{2,1,0:T(1,128)S(1)} %get-tuple-element.11, f32[1,1,32768]{2,1,0:T(1,128)S(1)} %get-tuple-element.10, f32[1,1,32768]{2,1,0:T(1,128)S(1)} %get-tuple-element.9), kind=kLoop, calls=%fused_computation.35 | loop fusion | flops 262144 | bytes 1048576 | tf_op jit(solution)/shard_map/broadcast_in_dim | solution.py:130
  (23 shorter events, 3.2 us)
Async XLA Ops:
  0.0 9.7 %collective-permute-start = (bf16[1,2,32768]{2,1,0:T(2,128)(2,1)}, bf16[1,2,32768]{2,1,0:T(2,128)(2,1)S(1)}, u32[]{:S(2)}, u32[]{:S(2)}) collective-permute-start(bf16[1,2,32768]{2,1,0:T(2,128)(2,1)} %bitcast.192), channel_id=1, source_target_pairs={{0,8},{4,12},{8,16},{12,20},{16,24},{20,28},{24,0},{28,4},{1,9},{5... | collective-permute-start | bytes 393224 | tf_op jit(solution)/shard_map/ppermute | solution.py:14
  9.7 5.0 %collective-permute-start.2 = (bf16[1,2,32768]{2,1,0:T(2,128)(2,1)S(1)}, bf16[1,2,32768]{2,1,0:T(2,128)(2,1)S(1)}, u32[]{:S(2)}, u32[]{:S(2)}) collective-permute-start(bf16[1,2,32768]{2,1,0:T(2,128)(2,1)S(1)} %collective-permute-done), channel_id=1, source_target_pairs={{0,2},{1,3},{2,0},{3,1},{4,6},{5,7},{6,4},{7,5},{8,10},{9,11},{10,... | collective-permute-start | bytes 393224 | tf_op jit(solution)/shard_map/ppermute | solution.py:20
  11.3 5.0 %collective-permute-start.1 = (bf16[1,2,32768]{2,1,0:T(2,128)(2,1)S(1)}, bf16[1,2,32768]{2,1,0:T(2,128)(2,1)S(1)}, u32[]{:S(2)}, u32[]{:S(2)}) collective-permute-start(bf16[1,2,32768]{2,1,0:T(2,128)(2,1)S(1)} %collective-permute-done), channel_id=1, source_target_pairs={{0,1},{1,0},{2,3},{3,2},{4,5},{5,4},{6,7},{7,6},{8,9},{9,8},{10,11... | collective-permute-start | bytes 393224 | tf_op jit(solution)/shard_map/ppermute | solution.py:20
  24.8 1.5 %copy-start = (bf16[1,1,2,32768]{3,2,1,0:T(2,128)(2,1)S(1)}, bf16[1,1,2,32768]{3,2,1,0:T(2,128)(2,1)}, u32[]{:S(2)}) copy-start(bf16[1,1,2,32768]{3,2,1,0:T(2,128)(2,1)} %param.2) | copy-start | bytes 393220
  27.5 5.0 %collective-permute-start.4 = (bf16[1,2,32768]{2,1,0:T(2,128)(2,1)S(1)}, bf16[1,2,32768]{2,1,0:T(2,128)(2,1)S(1)}, u32[]{:S(2)}, u32[]{:S(2)}) collective-permute-start(bf16[1,2,32768]{2,1,0:T(2,128)(2,1)S(1)} %pad_maximum_fusion.2), channel_id=1, source_target_pairs={{0,2},{1,3},{2,0},{3,1},{4,6},{5,7},{6,4},{7,5},{8,10},{9,11},{10,... | collective-permute-start | bytes 393224 | tf_op jit(solution)/shard_map/ppermute | solution.py:20
  29.5 5.0 %collective-permute-start.3 = (bf16[1,2,32768]{2,1,0:T(2,128)(2,1)S(1)}, bf16[1,2,32768]{2,1,0:T(2,128)(2,1)S(1)}, u32[]{:S(2)}, u32[]{:S(2)}) collective-permute-start(bf16[1,2,32768]{2,1,0:T(2,128)(2,1)S(1)} %pad_maximum_fusion.1), channel_id=1, source_target_pairs={{0,1},{1,0},{2,3},{3,2},{4,5},{5,4},{6,7},{7,6},{8,9},{9,8},{10,11... | collective-permute-start | bytes 393224 | tf_op jit(solution)/shard_map/ppermute | solution.py:20
  34.6 6.4 %collective-permute-start.5 = (f32[1,2,32768]{2,1,0:T(2,128)S(1)}, f32[1,2,32768]{2,1,0:T(2,128)S(1)}, u32[]{:S(2)}, u32[]{:S(2)}) collective-permute-start(f32[1,2,32768]{2,1,0:T(2,128)S(1)} %convert_add_fusion), channel_id=1, source_target_pairs={{0,24},{4,28},{8,0},{12,4},{16,8},{20,12},{24,16},{28,20},{1,25},{... | collective-permute-start | bytes 786440 | tf_op jit(solution)/shard_map/ppermute | solution.py:14
where the time goes:
time: 42.5 us; the launch traced here: 42.2 us
  waiting for transfers between devices  11 us (26%)
  starting transfers between devices  10.3 us (24%)
  other arithmetic  8.47 us (20%)
  local copies, waits for them, and re-layouts  8.18 us (19%)
  matrix products  4.07 us (10%)
    ppermute x4, waiting for transfers between devices, partner(): return lax.ppermute(value, axis, pairs)  6.63 us
    ppermute x4, starting transfers between devices, partner(): return lax.ppermute(value, axis, pairs)  5.2 us
    ppermute x2, starting transfers between devices, shifted(): return lax.ppermute(value, axis, pairs)  5.11 us
    ppermute x2, waiting for transfers between devices, shifted(): return lax.ppermute(value, axis, pairs)  4.34 us
    another operation x4, other arithmetic  2.68 us
    dot_general x6, matrix products, one_pass(): jnp.einsum('pcme,dcfe->pdfm', shaped, table, preferred_element_type=jnp.f...  2.46 us
    mul x2, other arithmetic, coulomb_kernel(): square = along_x * along_x + along_y * along_y + along_z * along_z  1.91 us
    neg x2, other arithmetic, apply_fields(): real = -jnp.sum(l_real * w_real - l_imag * w_imag, axis=-2)  1.77 us
  transfers between devices with their start and end apart: 6, of which 5 were waited for; matrix products, arithmetic and copies ran while one was open for 20% of the time, Pallas kernels for 0%

commit v1 on v0

v1 whole, which is shorter than its diff:
```python
import math

import numpy as np
import jax
import jax.numpy as jnp
from jax import lax
from jax.experimental import pallas as pl
from jax.experimental.pallas import tpu as pltpu
from jax.sharding import PartitionSpec as P

LANES = 128


class Layout:
    def __init__(self, cells):
        self.grid = round(cells ** (1.0 / 3.0))
        self.low = LANES // self.grid
        self.high = self.grid // self.low
        self.rows = self.grid * self.high


def roots(exponents, grid):
    angle = (exponents % grid).astype(np.float64) * (2.0 * math.pi / grid)
    return np.cos(angle).astype(np.float32), np.sin(angle).astype(np.float32)


def tables(lay):
    grid, low, high = lay.grid, lay.low, lay.high
    row = np.arange(lay.rows)
    lane = np.arange(LANES)
    fx, f0 = row // high, row % high
    f1, fz = lane // grid, lane % grid
    cos, sin = roots(np.outer(fx, fx) + low * np.outer(f0, f0), grid)
    rows_table = np.concatenate([cos, sin], axis=0)
    tw_cos, tw_sin = roots(np.outer(f0, f1), grid)
    cos, sin = roots(high * np.outer(f1, f1) + np.outer(fz, fz), grid)
    forward = np.block([[cos, -sin], [sin, cos]])
    inverse = np.block([[cos, sin], [-sin, cos]])
    narrow = [jnp.asarray(t, jnp.bfloat16) for t in (rows_table, forward, inverse)]
    return narrow + [jnp.asarray(np.concatenate([tw_cos, tw_sin], axis=0))]


def coulomb_kernel(offset, lay):
    grid, high = lay.grid, lay.high
    shape = (lay.rows, LANES)
    row = lax.broadcasted_iota(jnp.int32, shape, 0)
    lane = lax.broadcasted_iota(jnp.int32, shape, 1)

    def signed(index):
        return jnp.where(index < grid // 2, index, index - grid).astype(jnp.float32)

    along_x = signed(row // high) + offset[0]
    along_y = signed(lane // grid * high + row % high) + offset[1]
    along_z = signed(lane % grid) + offset[2]
    square = along_x * along_x + along_y * along_y + along_z * along_z
    return 32.0 / grid**3 / (square + 0.25)


def interleaved(field, lay):
    return field.reshape(2, lay.rows, LANES).transpose(1, 0, 2).reshape(2 * lay.rows, LANES)


def split_parts(ref, scratch, rows):
    scratch[...] = ref[...].astype(jnp.float32)
    return scratch[pl.ds(0, rows, 2), :], scratch[pl.ds(1, rows, 2), :]


def exchange_kernel(rows, matches, *refs):
    source_ref, refs = refs[0], refs[1:]
    target_refs, refs = refs[:matches], refs[matches:]
    coulomb_ref, rows_ref, forward_ref, inverse_ref, twiddle_ref = refs[:5]
    own_refs, return_ref = refs[5 : 5 + matches], refs[5 + matches]
    scratch = refs[6 + matches :]
    f32, bf16 = jnp.float32, jnp.bfloat16

    def dot(a, b):
        return jnp.dot(a, b, preferred_element_type=f32)

    s_real, s_imag = split_parts(source_ref, scratch[0], rows)
    targets = [split_parts(target_refs[j], scratch[1 + j], rows) for j in range(matches)]
    coulomb = coulomb_ref[...]
    coulomb = jnp.concatenate([coulomb, coulomb], axis=1)
    tw_cos, tw_sin = twiddle_ref[:rows], twiddle_ref[rows:]

    stage = []
    for t_real, t_imag in targets:
        real = s_real * t_real + s_imag * t_imag
        imag = s_real * t_imag - s_imag * t_real
        stage.append(jnp.concatenate([real.astype(bf16), imag.astype(bf16)], axis=1))
    stage = [dot(rows_ref[...], pair) for pair in stage]
    after = []
    for both in stage:
        real = both[:rows, :LANES] + both[rows:, LANES:]
        imag = both[:rows, LANES:] - both[rows:, :LANES]
        turned_real = real * tw_cos + imag * tw_sin
        turned_imag = imag * tw_cos - real * tw_sin
        after.append(jnp.concatenate([turned_real.astype(bf16), turned_imag.astype(bf16)], axis=1))
    stage = [dot(field, forward_ref[...]) for field in after]
    stage = [(field * coulomb).astype(bf16) for field in stage]
    stage = [dot(field, inverse_ref[...]) for field in stage]
    after = []
    for both in stage:
        real, imag = both[:, :LANES], both[:, LANES:]
        turned_real = real * tw_cos - imag * tw_sin
        turned_imag = imag * tw_cos + real * tw_sin
        after.append(jnp.concatenate([turned_real.astype(bf16), turned_imag.astype(bf16)], axis=1))
    stage = [dot(rows_ref[...], field) for field in after]
    total_real, total_imag = None, None
    for j, both in enumerate(stage):
        v_real = both[:rows, :LANES] - both[rows:, LANES:]
        v_imag = both[:rows, LANES:] + both[rows:, :LANES]
        t_real, t_imag = targets[j]
        own_refs[j][:rows] = (s_imag * v_imag - s_real * v_real).astype(bf16)
        own_refs[j][rows:] = (-(s_real * v_imag + s_imag * v_real)).astype(bf16)
        real = -(t_real * v_real + t_imag * v_imag)
        imag = t_real * v_imag - t_imag * v_real
        total_real = real if total_real is None else total_real + real
        total_imag = imag if total_imag is None else total_imag + imag
    return_ref[:rows] = total_real.astype(bf16)
    return_ref[rows:] = total_imag.astype(bf16)


def sum_kernel(rows, *refs):
    out_ref = refs[-1]
    total = refs[0][...].astype(jnp.float32)
    for ref in refs[1:-1]:
        total = total + ref[...].astype(jnp.float32)
    out_ref[pl.ds(0, rows, 2), :] = total[:rows]
    out_ref[pl.ds(1, rows, 2), :] = total[rows:]


def in_vmem(count):
    return [pl.BlockSpec(memory_space=pltpu.VMEM)] * count


def per_device(orbitals, kpoint_coords):
    own = orbitals[0, 0]
    cells = own.shape[-1]
    lay = Layout(cells)
    rows = lay.rows
    kpoints, groups = lax.axis_size("ka"), lax.axis_size("ba")
    steps = kpoints // 4
    matches = min(3, groups // 4 + 1)

    def shifted(value, by):
        return lax.ppermute(value, "ka", [(k, (k + by) % kpoints) for k in range(kpoints)])

    def partner(value, apart):
        return lax.ppermute(value, "ba", [(b, b ^ 2**apart) for b in range(groups)])

    source = shifted(own, steps)
    targets = [partner(own, j) for j in range(matches)]

    coords = kpoint_coords.astype(jnp.float32)
    here = lax.axis_index("ka")
    there = (here - steps) % kpoints
    offset = (coords[here] - coords[there]) / 4.0
    coulomb = coulomb_kernel(offset, lay)

    field = jax.ShapeDtypeStruct((2 * rows, LANES), jnp.bfloat16)
    outs = pl.pallas_call(
        lambda *refs: exchange_kernel(rows, matches, *refs),
        out_shape=[field] * (matches + 1),
        in_specs=in_vmem(matches + 6),
        out_specs=in_vmem(matches + 1),
        scratch_shapes=[pltpu.VMEM((2 * rows, LANES), jnp.float32)] * (matches + 1),
        compiler_params=pltpu.CompilerParams(vmem_limit_bytes=32 * 1024 * 1024),
        name="exchange",
    )(interleaved(source, lay), *[interleaved(t, lay) for t in targets], coulomb, *tables(lay))
    arrived = [shifted(outs[matches], -steps)]
    arrived += [partner(outs[j], j) for j in range(matches)]
    total = pl.pallas_call(
        lambda *refs: sum_kernel(rows, *refs),
        out_shape=jax.ShapeDtypeStruct((2 * rows, LANES), jnp.float32),
        in_specs=in_vmem(matches + 1),
        out_specs=in_vmem(1)[0],
        compiler_params=pltpu.CompilerParams(vmem_limit_bytes=32 * 1024 * 1024),
        name="total",
    )(*arrived)
    return total.reshape(rows, 2, LANES).transpose(1, 0, 2).reshape(1, 1, 2, cells)


def solution(mesh):
    return jax.shard_map(
        per_device,
        mesh=mesh,
        in_specs=(P("ka", "ba", None, None), P()),
        out_specs=P("ka", "ba", None, None),
        check_vma=False,
    )
```

time: 42.5 us -> 23.6 us (0.56)
  other arithmetic: 8.47 us -> 2.95 us
  local copies, waits for them, and re-layouts: 8.18 us -> 3.41 us
  waiting for transfers between devices: 11 us -> 6.28 us
  matrix products: 4.07 us -> 0 us
  Pallas kernels: 0 us -> 1.77 us
  starting transfers between devices: 10.3 us -> 8.93 us
    ppermute x6, waiting for transfers between devices: 11 us -> 6.28 us  [the longest x2 3.92 us: shifted(): lax.ppermute(value, 'ka', [(k, (k + by) % kpoints) for k in range(kpoints)])]
    dot_general x8 -> x0, matrix products: 4.07 us -> none  [the longest x6 2.46 us: one_pass(): jnp.einsum('pcme,dcfe->pdfm', shaped, table, preferred_element_type=jnp.f...]
    another operation x7 -> x0, other arithmetic: 3.3 us -> none
    convert_element_type x4 -> x0, local copies, waits for them, and re-layouts: 3.1 us -> none  [the longest x2 1.55 us: transform(): first = one_pass(field, table, grid).astype(jnp.bfloat16)]
    div x1 -> x4, other arithmetic: 0.1 us -> 2.24 us  [the longest x1 2.16 us: coulomb_kernel(): return 32.0 / grid ** 3 / (square + 0.25)]
    mul x2 -> x0, other arithmetic: 1.91 us -> none  [coulomb_kernel(): square = along_x * along_x + along_y * along_y + along_z * along_z]
    another operation x5 -> x0, local copies, waits for them, and re-layouts: 1.91 us -> none  [the longest x1 1.02 us: fields_all(): jnp.stack(formers)]
    unnamed x3 -> x8, local copies, waits for them, and re-layouts: 1.04 us -> 2.81 us
  transfers between devices with their start and end apart: 6 -> 6, of which waited for: 5 -> 4; matrix products, arithmetic and copies ran while one was open for 20% -> 15% of each run, Pallas kernels for 0% -> 0%
where the time goes in v1:
time: 23.6 us; the launch traced here: 23.4 us
  starting transfers between devices  8.93 us (38%)
  waiting for transfers between devices  6.28 us (27%)
  local copies, waits for them, and re-layouts  3.41 us (14%)
  other arithmetic  2.95 us (12%)
  Pallas kernels  1.77 us (7%)
    ppermute x4, starting transfers between devices, partner(): lax.ppermute(value, 'ba', [(b, b ^ 2 ** apart) for b in range(groups)])  5.5 us
    ppermute x2, waiting for transfers between devices, shifted(): lax.ppermute(value, 'ka', [(k, (k + by) % kpoints) for k in range(kpoints)])  3.92 us
    ppermute x2, starting transfers between devices, shifted(): lax.ppermute(value, 'ka', [(k, (k + by) % kpoints) for k in range(kpoints)])  3.43 us
    unnamed x8, local copies, waits for them, and re-layouts  2.81 us
    ppermute x4, waiting for transfers between devices, partner(): lax.ppermute(value, 'ba', [(b, b ^ 2 ** apart) for b in range(groups)])  2.35 us
    div x1, other arithmetic, coulomb_kernel(): return 32.0 / grid ** 3 / (square + 0.25)  2.16 us
    pallas_call x1, Pallas kernels, per_device(): pl.pallas_call(lambda *refs: exchange_kernel(rows, matches, *refs), out_s...  1.02 us
    pallas_call x1, Pallas kernels, per_device(): pl.pallas_call(lambda *refs: sum_kernel(rows, *refs), out_shape=jax.Shape...  0.75 us
  transfers between devices with their start and end apart: 6, of which 4 were waited for; matrix products, arithmetic and copies ran while one was open for 15% of the time, Pallas kernels for 0%

profile of v1, /device:TPU:0, one launch (start us, length us, event | category | flops | bytes accessed | tf_op | source)
XLA Modules:
  0.0 23.4 jit_solution(4558177458904986365)
XLA Ops:
  0.0 0.0 copy-start.2
  0.0 3.0 %collective-permute-start.2 = (bf16[2,32768]{1,0:T(2,128)(2,1)}, bf16[2,32768]{1,0:T(2,128)(2,1)S(1)}, u32[]{:S(2)}, u32[]{:S(2)}) collective-permute-start(bf16[2,32768]{1,0:T(2,128)(2,1)} %bitcast.27), channel_id=1, source_target_pairs={{0,2},{1,3},{2,0},{3,1},{4,6},{5,7},{6,4},{7,5},{8,10},{9,11},{10,... | collective-permute-start | bytes 393224 | tf_op jit(solution)/shard_map/ppermute | solution.py:149
  3.0 1.5 %collective-permute-start.1 = (bf16[2,32768]{1,0:T(2,128)(2,1)}, bf16[2,32768]{1,0:T(2,128)(2,1)S(1)}, u32[]{:S(2)}, u32[]{:S(2)}) collective-permute-start(bf16[2,32768]{1,0:T(2,128)(2,1)} %bitcast.28), channel_id=1, source_target_pairs={{0,1},{1,0},{2,3},{3,2},{4,5},{5,4},{6,7},{7,6},{8,9},{9,8},{10,11... | collective-permute-start | bytes 393224 | tf_op jit(solution)/shard_map/ppermute | solution.py:149
  4.5 1.6 %collective-permute-start = (bf16[2,32768]{1,0:T(2,128)(2,1)}, bf16[2,32768]{1,0:T(2,128)(2,1)S(1)}, u32[]{:S(2)}, u32[]{:S(2)}) collective-permute-start(bf16[2,32768]{1,0:T(2,128)(2,1)} %bitcast.29), channel_id=1, source_target_pairs={{0,8},{4,12},{8,16},{12,20},{16,24},{20,28},{24,0},{28,4},{1,9},{5... | collective-permute-start | bytes 393224 | tf_op jit(solution)/shard_map/ppermute | solution.py:146
  6.1 0.7 %convert_element_type.13 = f32[8,3]{0,1:T(4,128)S(1)} convert(s32[8,3]{0,1:T(4,128)} %param.7) | non-fusion elementwise | flops 24 | bytes 192 | tf_op jit(solution)/shard_map/convert_element_type | solution.py:154
  6.8 0.1 subtract_multiply_fusion
  6.9 0.6 %fusion.15 = (f32[1,1]{0,1:T(1,128)}, f32[1,1]{0,1:T(1,128)}, f32[1,1]{0,1:T(1,128)}) fusion(f32[1,3]{0,1:T(4,128)S(1)} %subtract_multiply_fusion), kind=kLoop, calls=%fused_computation.32 | loop fusion | bytes 24 | tf_op jit(solution)/shard_map/slice | solution.py:52
  7.5 2.2 %fusion.6.refs_3_ = f32[256,128]{1,0:T(8,128)S(1)} fusion(f32[]{:T(128)} %bitcast.12, s32[128]{0:T(128)S(1)} %get-tuple-element.21, s32[128]{0:T(128)S(1)} %get-tuple-element.24, f32[]{:T(128)} %bitcast.11, s32[256]{0:T(256)S(1)} %get-tuple-element.17, s32[256]{0:T(256)S(1)} %get-tuple-element.22, s32[128]{0:T(128)S(1)} %get-tuple-element.20, ...), kind=kLoop, calls=%fused_computation.9 | loop fusion | flops 917504 | bytes 137996 | tf_op jit(solution)/shard_map/div | solution.py:56
  9.6 0.0 collective-permute-done.2
  9.6 0.0 collective-permute-done.1
  9.6 1.8 %collective-permute-done = bf16[2,32768]{1,0:T(2,128)(2,1)S(1)} collective-permute-done((bf16[2,32768]{1,0:T(2,128)(2,1)}, bf16[2,32768]{1,0:T(2,128)(2,1)S(1)}, u32[]{:S(2)}, u32[]{:S(2)}) %collective-permute-start) | collective-permute-done | bytes 131104 | tf_op jit(solution)/shard_map/ppermute | solution.py:146
  11.4 0.0 copy-done.2
  11.4 0.0 copy-start
  11.4 0.9 %copy-done = f32[512,128]{1,0:T(8,128)S(1)} copy-done((f32[512,128]{1,0:T(8,128)S(1)}, f32[512,128]{1,0:T(8,128)}, u32[]{:S(2)}) %copy-start) | copy-done | bytes 262168
  12.4 0.0 copy-start.1
  12.4 0.9 %copy-done.1 = bf16[512,256]{1,0:T(8,128)(2,1)S(1)} copy-done((bf16[512,256]{1,0:T(8,128)(2,1)S(1)}, bf16[512,256]{1,0:T(8,128)(2,1)}, u32[]{:S(2)}) %copy-start.1) | copy-done | bytes 262168
  13.3 0.0 copy-start.3
  13.3 0.9 %copy-done.3 = bf16[256,256]{1,0:T(8,128)(2,1)S(1)} copy-done((bf16[256,256]{1,0:T(8,128)(2,1)S(1)}, bf16[256,256]{1,0:T(8,128)(2,1)}, u32[]{:S(2)}) %copy-start.3) | copy-done | bytes 131096
  14.2 1.0 %exchange.1 = (bf16[512,128]{1,0:T(8,128)(2,1)S(1)}, bf16[512,128]{1,0:T(8,128)(2,1)S(1)}, bf16[512,128]{1,0:T(8,128)(2,1)S(1)}) custom-call(bf16[512,128]{1,0:T(8,128)(2,1)S(1)} %bitcast.26, bf16[512,128]{1,0:T(8,128)(2,1)S(1)} %bitcast.25, bf16[512,128]{1,0:T(8,128)(2,1)S(1)} %bitcast.24, f32[256,128]{1,0:T(8,128)S(1)} %fusion.6.refs_3_, ...), custom_call_target="tpu_custom_call" | custom-call | tf_op jit(solution)/shard_map/exchange/pallas_call | solution.py:161
  15.3 1.9 %collective-permute-start.3 = (bf16[512,128]{1,0:T(8,128)(2,1)S(1)}, bf16[512,128]{1,0:T(8,128)(2,1)S(1)}, u32[]{:S(2)}, u32[]{:S(2)}) collective-permute-start(bf16[512,128]{1,0:T(8,128)(2,1)S(1)} %get-tuple-element.8), channel_id=1, source_target_pairs={{0,24},{4,28},{8,0},{12,4},{16,8},{20,12},{24,16},{28,20},{1,25},{... | collective-permute-start | bytes 393224 | tf_op jit(solution)/shard_map/ppermute | solution.py:146
  17.1 0.5 %collective-permute-start.4 = (bf16[512,128]{1,0:T(8,128)(2,1)S(1)}, bf16[512,128]{1,0:T(8,128)(2,1)S(1)}, u32[]{:S(2)}, u32[]{:S(2)}) collective-permute-start(bf16[512,128]{1,0:T(8,128)(2,1)S(1)} %get-tuple-element.9), channel_id=1, source_target_pairs={{0,1},{1,0},{2,3},{3,2},{4,5},{5,4},{6,7},{7,6},{8,9},{9,8},{10,11... | collective-permute-start | bytes 393224 | tf_op jit(solution)/shard_map/ppermute | solution.py:149
  17.7 0.5 %collective-permute-start.5 = (bf16[512,128]{1,0:T(8,128)(2,1)S(1)}, bf16[512,128]{1,0:T(8,128)(2,1)S(1)}, u32[]{:S(2)}, u32[]{:S(2)}) collective-permute-start(bf16[512,128]{1,0:T(8,128)(2,1)S(1)} %get-tuple-element.10), channel_id=1, source_target_pairs={{0,2},{1,3},{2,0},{3,1},{4,6},{5,7},{6,4},{7,5},{8,10},{9,11},{10,... | collective-permute-start | bytes 393224 | tf_op jit(solution)/shard_map/ppermute | solution.py:149
  18.2 2.1 %collective-permute-done.3.refs_0_ = bf16[512,128]{1,0:T(8,128)(2,1)S(1)} collective-permute-done((bf16[512,128]{1,0:T(8,128)(2,1)S(1)}, bf16[512,128]{1,0:T(8,128)(2,1)S(1)}, u32[]{:S(2)}, u32[]{:S(2)}) %collective-permute-start.3) | collective-permute-done | bytes 131104 | tf_op jit(solution)/shard_map/ppermute | solution.py:146
  20.3 1.8 %collective-permute-done.4.refs_1_ = bf16[512,128]{1,0:T(8,128)(2,1)S(1)} collective-permute-done((bf16[512,128]{1,0:T(8,128)(2,1)S(1)}, bf16[512,128]{1,0:T(8,128)(2,1)S(1)}, u32[]{:S(2)}, u32[]{:S(2)}) %collective-permute-start.4) | collective-permute-done | bytes 131104 | tf_op jit(solution)/shard_map/ppermute | solution.py:149
  22.1 0.5 %collective-permute-done.5.refs_2_ = bf16[512,128]{1,0:T(8,128)(2,1)S(1)} collective-permute-done((bf16[512,128]{1,0:T(8,128)(2,1)S(1)}, bf16[512,128]{1,0:T(8,128)(2,1)S(1)}, u32[]{:S(2)}, u32[]{:S(2)}) %collective-permute-start.5) | collective-permute-done | bytes 131104 | tf_op jit(solution)/shard_map/ppermute | solution.py:149
  22.6 0.7 %total.1 = f32[512,128]{1,0:T(8,128)} custom-call(bf16[512,128]{1,0:T(8,128)(2,1)S(1)} %collective-permute-done.3.refs_0_, bf16[512,128]{1,0:T(8,128)(2,1)S(1)} %collective-permute-done.4.refs_1_, bf16[512,128]{1,0:T(8,128)(2,1)S(1)} %collective-permute-done.5.refs_2_), custom_call_target="tpu_custom_call" | custom-call | tf_op jit(solution)/shard_map/total/pallas_call | solution.py:172
  (6 shorter events, 0.0 us)
Async XLA Ops:
  0.0 11.4 %copy-start.2 = (bf16[256,256]{1,0:T(8,128)(2,1)S(1)}, bf16[256,256]{1,0:T(8,128)(2,1)}, u32[]{:S(2)}) copy-start(bf16[256,256]{1,0:T(8,128)(2,1)} %constant.98.clone.refs_6_) | copy-start | bytes 393220
  0.0 9.6 %collective-permute-start.2 = (bf16[2,32768]{1,0:T(2,128)(2,1)}, bf16[2,32768]{1,0:T(2,128)(2,1)S(1)}, u32[]{:S(2)}, u32[]{:S(2)}) collective-permute-start(bf16[2,32768]{1,0:T(2,128)(2,1)} %bitcast.27), channel_id=1, source_target_pairs={{0,2},{1,3},{2,0},{3,1},{4,6},{5,7},{6,4},{7,5},{8,10},{9,11},{10,... | collective-permute-start | bytes 393224 | tf_op jit(solution)/shard_map/ppermute | solution.py:149
  3.0 6.7 %collective-permute-start.1 = (bf16[2,32768]{1,0:T(2,128)(2,1)}, bf16[2,32768]{1,0:T(2,128)(2,1)S(1)}, u32[]{:S(2)}, u32[]{:S(2)}) collective-permute-start(bf16[2,32768]{1,0:T(2,128)(2,1)} %bitcast.28), channel_id=1, source_target_pairs={{0,1},{1,0},{2,3},{3,2},{4,5},{5,4},{6,7},{7,6},{8,9},{9,8},{10,11... | collective-permute-start | bytes 393224 | tf_op jit(solution)/shard_map/ppermute | solution.py:149
  4.5 7.0 %collective-permute-start = (bf16[2,32768]{1,0:T(2,128)(2,1)}, bf16[2,32768]{1,0:T(2,128)(2,1)S(1)}, u32[]{:S(2)}, u32[]{:S(2)}) collective-permute-start(bf16[2,32768]{1,0:T(2,128)(2,1)} %bitcast.29), channel_id=1, source_target_pairs={{0,8},{4,12},{8,16},{12,20},{16,24},{20,28},{24,0},{28,4},{1,9},{5... | collective-permute-start | bytes 393224 | tf_op jit(solution)/shard_map/ppermute | solution.py:146
  11.4 1.0 %copy-start = (f32[512,128]{1,0:T(8,128)S(1)}, f32[512,128]{1,0:T(8,128)}, u32[]{:S(2)}) copy-start(f32[512,128]{1,0:T(8,128)} %constant.99.clone.refs_7_) | copy-start | bytes 786436
  12.4 0.9 %copy-start.1 = (bf16[512,256]{1,0:T(8,128)(2,1)S(1)}, bf16[512,256]{1,0:T(8,128)(2,1)}, u32[]{:S(2)}) copy-start(bf16[512,256]{1,0:T(8,128)(2,1)} %constant.96.clone.refs_4_) | copy-start | bytes 786436
  13.3 0.9 %copy-start.3 = (bf16[256,256]{1,0:T(8,128)(2,1)S(1)}, bf16[256,256]{1,0:T(8,128)(2,1)}, u32[]{:S(2)}) copy-start(bf16[256,256]{1,0:T(8,128)(2,1)} %constant.97.clone.refs_5_) | copy-start | bytes 393220
  15.3 5.0 %collective-permute-start.3 = (bf16[512,128]{1,0:T(8,128)(2,1)S(1)}, bf16[512,128]{1,0:T(8,128)(2,1)S(1)}, u32[]{:S(2)}, u32[]{:S(2)}) collective-permute-start(bf16[512,128]{1,0:T(8,128)(2,1)S(1)} %get-tuple-element.8), channel_id=1, source_target_pairs={{0,24},{4,28},{8,0},{12,4},{16,8},{20,12},{24,16},{28,20},{1,25},{... | collective-permute-start | bytes 393224 | tf_op jit(solution)/shard_map/ppermute | solution.py:146
  17.1 5.0 %collective-permute-start.4 = (bf16[512,128]{1,0:T(8,128)(2,1)S(1)}, bf16[512,128]{1,0:T(8,128)(2,1)S(1)}, u32[]{:S(2)}, u32[]{:S(2)}) collective-permute-start(bf16[512,128]{1,0:T(8,128)(2,1)S(1)} %get-tuple-element.9), channel_id=1, source_target_pairs={{0,1},{1,0},{2,3},{3,2},{4,5},{5,4},{6,7},{7,6},{8,9},{9,8},{10,11... | collective-permute-start | bytes 393224 | tf_op jit(solution)/shard_map/ppermute | solution.py:149
  17.7 5.0 %collective-permute-start.5 = (bf16[512,128]{1,0:T(8,128)(2,1)S(1)}, bf16[512,128]{1,0:T(8,128)(2,1)S(1)}, u32[]{:S(2)}, u32[]{:S(2)}) collective-permute-start(bf16[512,128]{1,0:T(8,128)(2,1)S(1)} %get-tuple-element.10), channel_id=1, source_target_pairs={{0,2},{1,3},{2,0},{3,1},{4,6},{5,7},{6,4},{7,5},{8,10},{9,11},{10,... | collective-permute-start | bytes 393224 | tf_op jit(solution)/shard_map/ppermute | solution.py:149

commit v2 on v1

--- a/solution.py
+++ b/solution.py
@@ -1,6 +1,5 @@
 import math
 
-import numpy as np
 import jax
 import jax.numpy as jnp
 from jax import lax
@@ -19,41 +18,58 @@
         self.rows = self.grid * self.high
 
 
-def roots(exponents, grid):
-    angle = (exponents % grid).astype(np.float64) * (2.0 * math.pi / grid)
-    return np.cos(angle).astype(np.float32), np.sin(angle).astype(np.float32)
-
-
-def tables(lay):
-    grid, low, high = lay.grid, lay.low, lay.high
-    row = np.arange(lay.rows)
-    lane = np.arange(LANES)
-    fx, f0 = row // high, row % high
-    f1, fz = lane // grid, lane % grid
-    cos, sin = roots(np.outer(fx, fx) + low * np.outer(f0, f0), grid)
-    rows_table = np.concatenate([cos, sin], axis=0)
-    tw_cos, tw_sin = roots(np.outer(f0, f1), grid)
-    cos, sin = roots(high * np.outer(f1, f1) + np.outer(fz, fz), grid)
-    forward = np.block([[cos, -sin], [sin, cos]])
-    inverse = np.block([[cos, sin], [-sin, cos]])
-    narrow = [jnp.asarray(t, jnp.bfloat16) for t in (rows_table, forward, inverse)]
-    return narrow + [jnp.asarray(np.concatenate([tw_cos, tw_sin], axis=0))]
-
-
-def coulomb_kernel(offset, lay):
-    grid, high = lay.grid, lay.high
-    shape = (lay.rows, LANES)
-    row = lax.broadcasted_iota(jnp.int32, shape, 0)
-    lane = lax.broadcasted_iota(jnp.int32, shape, 1)
+def cosine(steps, grid):
+    folded = jnp.abs((steps & (grid - 1)) - grid // 2) - grid // 4
+    angle = folded.astype(jnp.float32) * (2.0 * math.pi / grid)
+    square = angle * angle
+    series = jnp.zeros_like(angle)
+    for order in range(13, 1, -2):
+        series = (series + (-1) ** (order // 2) / math.factorial(order)) * square
+    return angle + angle * series
+
+
+def sine(steps, grid):
+    return cosine(steps - grid // 4, grid)
+
+
+def setup_kernel(lay, by, coords_ref, rows_ref, forward_ref, inverse_ref, twiddle_ref, coulomb_ref):
+    grid, high, rows = lay.grid, lay.high, lay.rows
+    column = lax.broadcasted_iota(jnp.int32, (rows, 1), 0)
+    across = lax.broadcasted_iota(jnp.int32, (1, rows), 1)
+    steps = (column // high) * (across // high) + lay.low * (column % high) * (across % high)
+    rows_ref[:rows] = cosine(steps, grid).astype(jnp.bfloat16)
+    rows_ref[rows:] = sine(steps, grid).astype(jnp.bfloat16)
+
+    lane_row = lax.broadcasted_iota(jnp.int32, (LANES, 1), 0)
+    lane = lax.broadcasted_iota(jnp.int32, (1, LANES), 1)
+    steps = high * (lane_row // grid) * (lane // grid) + (lane_row % grid) * (lane % grid)
+    cos = cosine(steps, grid).astype(jnp.bfloat16)
+    sin = sine(steps, grid)
+    minus = (-sin).astype(jnp.bfloat16)
+    sin = sin.astype(jnp.bfloat16)
+    for ref, lower, upper in ((forward_ref, sin, minus), (inverse_ref, minus, sin)):
+        ref[:LANES, :LANES] = cos
+        ref[LANES:, LANES:] = cos
+        ref[LANES:, :LANES] = lower
+        ref[:LANES, LANES:] = upper
+
+    steps = (column % high) * (lane // grid)
+    twiddle_ref[:rows] = cosine(steps, grid)
+    twiddle_ref[rows:] = sine(steps, grid)
+
+    kpoints = coords_ref.shape[1]
+    here = lax.axis_index("ka")
+    there = lax.rem(here + kpoints - by, kpoints)
+    offset = [(coords_ref[d, here] - coords_ref[d, there]).astype(jnp.float32) / 4.0 for d in range(3)]
 
     def signed(index):
         return jnp.where(index < grid // 2, index, index - grid).astype(jnp.float32)
 
-    along_x = signed(row // high) + offset[0]
-    along_y = signed(lane // grid * high + row % high) + offset[1]
+    along_x = signed(column // high) + offset[0]
+    along_y = signed(lane // grid * high + column % high) + offset[1]
     along_z = signed(lane % grid) + offset[2]
     square = along_x * along_x + along_y * along_y + along_z * along_z
-    return 32.0 / grid**3 / (square + 0.25)
+    coulomb_ref[...] = 32.0 / grid**3 / (square + 0.25)
 
 
 def interleaved(field, lay):
@@ -68,7 +84,7 @@
 def exchange_kernel(rows, matches, *refs):
     source_ref, refs = refs[0], refs[1:]
     target_refs, refs = refs[:matches], refs[matches:]
-    coulomb_ref, rows_ref, forward_ref, inverse_ref, twiddle_ref = refs[:5]
+    rows_ref, forward_ref, inverse_ref, twiddle_ref, coulomb_ref = refs[:5]
     own_refs, return_ref = refs[5 : 5 + matches], refs[5 + matches]
     scratch = refs[6 + matches :]
     f32, bf16 = jnp.float32, jnp.bfloat16
@@ -151,30 +167,42 @@
     source = shifted(own, steps)
     targets = [partner(own, j) for j in range(matches)]
 
-    coords = kpoint_coords.astype(jnp.float32)
-    here = lax.axis_index("ka")
-    there = (here - steps) % kpoints
-    offset = (coords[here] - coords[there]) / 4.0
-    coulomb = coulomb_kernel(offset, lay)
-
-    field = jax.ShapeDtypeStruct((2 * rows, LANES), jnp.bfloat16)
+    def shape(*dims, dtype=jnp.bfloat16):
+        return jax.ShapeDtypeStruct(dims, dtype)
+
+    limits = pltpu.CompilerParams(vmem_limit_bytes=32 * 1024 * 1024)
+    tables = pl.pallas_call(
+        lambda *refs: setup_kernel(lay, steps, *refs),
+        out_shape=[
+            shape(2 * rows, rows),
+            shape(2 * LANES, 2 * LANES),
+            shape(2 * LANES, 2 * LANES),
+            shape(2 * rows, LANES, dtype=jnp.float32),
+            shape(rows, LANES, dtype=jnp.float32),
+        ],
+        in_specs=[pl.BlockSpec(memory_space=pltpu.SMEM)],
+        out_specs=in_vmem(5),
+        compiler_params=limits,
+        name="setup",
+    )(kpoint_coords.T)
+
     outs = pl.pallas_call(
         lambda *refs: exchange_kernel(rows, matches, *refs),
-        out_shape=[field] * (matches + 1),
+        out_shape=[shape(2 * rows, LANES)] * (matches + 1),
         in_specs=in_vmem(matches + 6),
         out_specs=in_vmem(matches + 1),
         scratch_shapes=[pltpu.VMEM((2 * rows, LANES), jnp.float32)] * (matches + 1),
-        compiler_params=pltpu.CompilerParams(vmem_limit_bytes=32 * 1024 * 1024),
+        compiler_params=limits,
         name="exchange",
-    )(interleaved(source, lay), *[interleaved(t, lay) for t in targets], coulomb, *tables(lay))
+    )(interleaved(source, lay), *[interleaved(t, lay) for t in targets], *tables)
     arrived = [shifted(outs[matches], -steps)]
     arrived += [partner(outs[j], j) for j in range(matches)]
     total = pl.pallas_call(
         lambda *refs: sum_kernel(rows, *refs),
-        out_shape=jax.ShapeDtypeStruct((2 * rows, LANES), jnp.float32),
+        out_shape=shape(2 * rows, LANES, dtype=jnp.float32),
         in_specs=in_vmem(matches + 1),
         out_specs=in_vmem(1)[0],
-        compiler_params=pltpu.CompilerParams(vmem_limit_bytes=32 * 1024 * 1024),
+        compiler_params=limits,
         name="total",
     )(*arrived)
     return total.reshape(rows, 2, LANES).transpose(1, 0, 2).reshape(1, 1, 2, cells)

time: 23.6 us -> 20.7 us (0.88)
  local copies, waits for them, and re-layouts: 3.41 us -> 0.01 us
  other arithmetic: 2.95 us -> 0 us
  waiting for transfers between devices: 6.28 us -> 8.45 us
  Pallas kernels: 1.77 us -> 3.2 us
    unnamed x8 -> x2, local copies, waits for them, and re-layouts: 2.81 us -> 0.01 us
    div x4 -> x0, other arithmetic: 2.24 us -> none  [the longest x1 2.16 us: coulomb_kernel(): return 32.0 / grid ** 3 / (square + 0.25)]
    ppermute x2, waiting for transfers between devices: 3.92 us -> 5.42 us  [shifted(): lax.ppermute(value, 'ka', [(k, (k + by) % kpoints) for k in range(kpoints)])]
    pallas_call x1 -> x2, Pallas kernels: 0.75 us -> 2.14 us  [the longest x1 1.4 us: per_device(): pl.pallas_call(lambda *refs: setup_kernel(lay, steps, *refs), out_shape=[...]
    convert_element_type x1 -> x0, other arithmetic: 0.69 us -> none  [per_device(): coords = kpoint_coords.astype(jnp.float32)]
    ppermute x4, waiting for transfers between devices: 2.35 us -> 3.03 us  [partner(): lax.ppermute(value, 'ba', [(b, b ^ 2 ** apart) for b in range(groups)])]
    slice x1 -> x0, local copies, waits for them, and re-layouts: 0.6 us -> none  [coulomb_kernel(): along_x = signed(row // high) + offset[0]]
  transfers between devices with their start and end apart: 6 -> 6, of which waited for: 4 -> 5; matrix products, arithmetic and copies ran while one was open for 15% -> 0% of each run, Pallas kernels for 0% -> 7%
where the time goes in v2:
time: 20.7 us; the launch traced here: 20.6 us
  starting transfers between devices  8.92 us (43%)
  waiting for transfers between devices  8.45 us (41%)
  Pallas kernels  3.2 us (15%)
    ppermute x4, starting transfers between devices, partner(): lax.ppermute(value, 'ba', [(b, b ^ 2 ** apart) for b in range(groups)])  5.49 us
    ppermute x2, waiting for transfers between devices, shifted(): lax.ppermute(value, 'ka', [(k, (k + by) % kpoints) for k in range(kpoints)])  5.42 us
    ppermute x2, starting transfers between devices, shifted(): lax.ppermute(value, 'ka', [(k, (k + by) % kpoints) for k in range(kpoints)])  3.43 us
    ppermute x4, waiting for transfers between devices, partner(): lax.ppermute(value, 'ba', [(b, b ^ 2 ** apart) for b in range(groups)])  3.03 us
    pallas_call x1, Pallas kernels, per_device(): pl.pallas_call(lambda *refs: setup_kernel(lay, steps, *refs), out_shape=[...  1.4 us
    pallas_call x1, Pallas kernels, per_device(): pl.pallas_call(lambda *refs: exchange_kernel(rows, matches, *refs), out_s...  1.05 us
    pallas_call x1, Pallas kernels, per_device(): pl.pallas_call(lambda *refs: sum_kernel(rows, *refs), out_shape=shape(2 *...  0.75 us
  transfers between devices with their start and end apart: 6, of which 5 were waited for; matrix products, arithmetic and copies ran while one was open for 0% of the time, Pallas kernels for 7%

profile of v2, /device:TPU:0, one launch (start us, length us, event | category | flops | bytes accessed | tf_op | source)
XLA Modules:
  0.0 20.6 jit_solution(9374023071408508066)
XLA Ops:
  0.0 0.0 copy-start
  0.0 3.0 %collective-permute-start.2 = (bf16[2,32768]{1,0:T(2,128)(2,1)}, bf16[2,32768]{1,0:T(2,128)(2,1)S(1)}, u32[]{:S(2)}, u32[]{:S(2)}) collective-permute-start(bf16[2,32768]{1,0:T(2,128)(2,1)} %bitcast.26), channel_id=1, source_target_pairs={{0,2},{1,3},{2,0},{3,1},{4,6},{5,7},{6,4},{7,5},{8,10},{9,11},{10,... | collective-permute-start | bytes 393224 | tf_op jit(solution)/shard_map/ppermute | solution.py:165
  3.0 1.5 %collective-permute-start.1 = (bf16[2,32768]{1,0:T(2,128)(2,1)}, bf16[2,32768]{1,0:T(2,128)(2,1)S(1)}, u32[]{:S(2)}, u32[]{:S(2)}) collective-permute-start(bf16[2,32768]{1,0:T(2,128)(2,1)} %bitcast.27), channel_id=1, source_target_pairs={{0,1},{1,0},{2,3},{3,2},{4,5},{5,4},{6,7},{7,6},{8,9},{9,8},{10,11... | collective-permute-start | bytes 393224 | tf_op jit(solution)/shard_map/ppermute | solution.py:165
  4.5 1.6 %collective-permute-start = (bf16[2,32768]{1,0:T(2,128)(2,1)}, bf16[2,32768]{1,0:T(2,128)(2,1)S(1)}, u32[]{:S(2)}, u32[]{:S(2)}) collective-permute-start(bf16[2,32768]{1,0:T(2,128)(2,1)} %bitcast.28), channel_id=1, source_target_pairs={{0,8},{4,12},{8,16},{12,20},{16,24},{20,28},{24,0},{28,4},{1,9},{5... | collective-permute-start | bytes 393224 | tf_op jit(solution)/shard_map/ppermute | solution.py:162
  6.0 0.0 copy-done
  6.0 1.4 %setup.1 = (bf16[512,256]{1,0:T(8,128)(2,1)S(1)}, bf16[256,256]{1,0:T(8,128)(2,1)S(1)}, bf16[256,256]{1,0:T(8,128)(2,1)S(1)}, f32[512,128]{1,0:T(8,128)S(1)}, f32[256,128]{1,0:T(8,128)S(1)}) custom-call(s32[3,8]{1,0:T(4,128)S(1)} %bitcast.25), custom_call_target="tpu_custom_call" | custom-call | tf_op jit(solution)/shard_map/setup/pallas_call | solution.py:174
  7.4 0.0 collective-permute-done.2
  7.5 0.7 %collective-permute-done.1 = bf16[2,32768]{1,0:T(2,128)(2,1)S(1)} collective-permute-done((bf16[2,32768]{1,0:T(2,128)(2,1)}, bf16[2,32768]{1,0:T(2,128)(2,1)S(1)}, u32[]{:S(2)}, u32[]{:S(2)}) %collective-permute-start.1) | collective-permute-done | bytes 131104 | tf_op jit(solution)/shard_map/ppermute | solution.py:165
  8.1 3.3 %collective-permute-done = bf16[2,32768]{1,0:T(2,128)(2,1)S(1)} collective-permute-done((bf16[2,32768]{1,0:T(2,128)(2,1)}, bf16[2,32768]{1,0:T(2,128)(2,1)S(1)}, u32[]{:S(2)}, u32[]{:S(2)}) %collective-permute-start) | collective-permute-done | bytes 131104 | tf_op jit(solution)/shard_map/ppermute | solution.py:162
  11.4 1.1 %exchange.1 = (bf16[512,128]{1,0:T(8,128)(2,1)S(1)}, bf16[512,128]{1,0:T(8,128)(2,1)S(1)}, bf16[512,128]{1,0:T(8,128)(2,1)S(1)}) custom-call(bf16[512,128]{1,0:T(8,128)(2,1)S(1)} %bitcast.24, bf16[512,128]{1,0:T(8,128)(2,1)S(1)} %bitcast.23, bf16[512,128]{1,0:T(8,128)(2,1)S(1)} %bitcast.22, bf16[512,256]{1,0:T(8,128)(2,1)S(1)} %get-tuple-element.13.refs_3_, ...), custom_call_target="tpu_custom_call" | custom-call | tf_op jit(solution)/shard_map/exchange/pallas_call | solution.py:189
  12.5 1.9 %collective-permute-start.3 = (bf16[512,128]{1,0:T(8,128)(2,1)S(1)}, bf16[512,128]{1,0:T(8,128)(2,1)S(1)}, u32[]{:S(2)}, u32[]{:S(2)}) collective-permute-start(bf16[512,128]{1,0:T(8,128)(2,1)S(1)} %get-tuple-element.18), channel_id=1, source_target_pairs={{0,24},{4,28},{8,0},{12,4},{16,8},{20,12},{24,16},{28,20},{1,25},{... | collective-permute-start | bytes 393224 | tf_op jit(solution)/shard_map/ppermute | solution.py:162
  14.4 0.5 %collective-permute-start.4 = (bf16[512,128]{1,0:T(8,128)(2,1)S(1)}, bf16[512,128]{1,0:T(8,128)(2,1)S(1)}, u32[]{:S(2)}, u32[]{:S(2)}) collective-permute-start(bf16[512,128]{1,0:T(8,128)(2,1)S(1)} %get-tuple-element.19), channel_id=1, source_target_pairs={{0,1},{1,0},{2,3},{3,2},{4,5},{5,4},{6,7},{7,6},{8,9},{9,8},{10,11... | collective-permute-start | bytes 393224 | tf_op jit(solution)/shard_map/ppermute | solution.py:165
  14.9 0.5 %collective-permute-start.5 = (bf16[512,128]{1,0:T(8,128)(2,1)S(1)}, bf16[512,128]{1,0:T(8,128)(2,1)S(1)}, u32[]{:S(2)}, u32[]{:S(2)}) collective-permute-start(bf16[512,128]{1,0:T(8,128)(2,1)S(1)} %get-tuple-element.20), channel_id=1, source_target_pairs={{0,2},{1,3},{2,0},{3,1},{4,6},{5,7},{6,4},{7,5},{8,10},{9,11},{10,... | collective-permute-start | bytes 393224 | tf_op jit(solution)/shard_map/ppermute | solution.py:165
  15.4 2.1 %collective-permute-done.3.refs_0_ = bf16[512,128]{1,0:T(8,128)(2,1)S(1)} collective-permute-done((bf16[512,128]{1,0:T(8,128)(2,1)S(1)}, bf16[512,128]{1,0:T(8,128)(2,1)S(1)}, u32[]{:S(2)}, u32[]{:S(2)}) %collective-permute-start.3) | collective-permute-done | bytes 131104 | tf_op jit(solution)/shard_map/ppermute | solution.py:162
  17.5 1.8 %collective-permute-done.4.refs_1_ = bf16[512,128]{1,0:T(8,128)(2,1)S(1)} collective-permute-done((bf16[512,128]{1,0:T(8,128)(2,1)S(1)}, bf16[512,128]{1,0:T(8,128)(2,1)S(1)}, u32[]{:S(2)}, u32[]{:S(2)}) %collective-permute-start.4) | collective-permute-done | bytes 131104 | tf_op jit(solution)/shard_map/ppermute | solution.py:165
  19.3 0.5 %collective-permute-done.5.refs_2_ = bf16[512,128]{1,0:T(8,128)(2,1)S(1)} collective-permute-done((bf16[512,128]{1,0:T(8,128)(2,1)S(1)}, bf16[512,128]{1,0:T(8,128)(2,1)S(1)}, u32[]{:S(2)}, u32[]{:S(2)}) %collective-permute-start.5) | collective-permute-done | bytes 131104 | tf_op jit(solution)/shard_map/ppermute | solution.py:165
  19.9 0.7 %total.1 = f32[512,128]{1,0:T(8,128)} custom-call(bf16[512,128]{1,0:T(8,128)(2,1)S(1)} %collective-permute-done.3.refs_0_, bf16[512,128]{1,0:T(8,128)(2,1)S(1)} %collective-permute-done.4.refs_1_, bf16[512,128]{1,0:T(8,128)(2,1)S(1)} %collective-permute-done.5.refs_2_), custom_call_target="tpu_custom_call" | custom-call | tf_op jit(solution)/shard_map/total/pallas_call | solution.py:200
Async XLA Ops:
  0.0 6.0 %copy-start = (s32[8,3]{0,1:T(4,128)S(1)}, s32[8,3]{0,1:T(4,128)}, u32[]{:S(2)}) copy-start(s32[8,3]{0,1:T(4,128)} %param.3) | copy-start | bytes 292
  0.0 7.4 %collective-permute-start.2 = (bf16[2,32768]{1,0:T(2,128)(2,1)}, bf16[2,32768]{1,0:T(2,128)(2,1)S(1)}, u32[]{:S(2)}, u32[]{:S(2)}) collective-permute-start(bf16[2,32768]{1,0:T(2,128)(2,1)} %bitcast.26), channel_id=1, source_target_pairs={{0,2},{1,3},{2,0},{3,1},{4,6},{5,7},{6,4},{7,5},{8,10},{9,11},{10,... | collective-permute-start | bytes 393224 | tf_op jit(solution)/shard_map/ppermute | solution.py:165
  3.0 5.2 %collective-permute-start.1 = (bf16[2,32768]{1,0:T(2,128)(2,1)}, bf16[2,32768]{1,0:T(2,128)(2,1)S(1)}, u32[]{:S(2)}, u32[]{:S(2)}) collective-permute-start(bf16[2,32768]{1,0:T(2,128)(2,1)} %bitcast.27), channel_id=1, source_target_pairs={{0,1},{1,0},{2,3},{3,2},{4,5},{5,4},{6,7},{7,6},{8,9},{9,8},{10,11... | collective-permute-start | bytes 393224 | tf_op jit(solution)/shard_map/ppermute | solution.py:165
  4.5 7.0 %collective-permute-start = (bf16[2,32768]{1,0:T(2,128)(2,1)}, bf16[2,32768]{1,0:T(2,128)(2,1)S(1)}, u32[]{:S(2)}, u32[]{:S(2)}) collective-permute-start(bf16[2,32768]{1,0:T(2,128)(2,1)} %bitcast.28), channel_id=1, source_target_pairs={{0,8},{4,12},{8,16},{12,20},{16,24},{20,28},{24,0},{28,4},{1,9},{5... | collective-permute-start | bytes 393224 | tf_op jit(solution)/shard_map/ppermute | solution.py:162
  12.5 5.0 %collective-permute-start.3 = (bf16[512,128]{1,0:T(8,128)(2,1)S(1)}, bf16[512,128]{1,0:T(8,128)(2,1)S(1)}, u32[]{:S(2)}, u32[]{:S(2)}) collective-permute-start(bf16[512,128]{1,0:T(8,128)(2,1)S(1)} %get-tuple-element.18), channel_id=1, source_target_pairs={{0,24},{4,28},{8,0},{12,4},{16,8},{20,12},{24,16},{28,20},{1,25},{... | collective-permute-start | bytes 393224 | tf_op jit(solution)/shard_map/ppermute | solution.py:162
  14.4 5.0 %collective-permute-start.4 = (bf16[512,128]{1,0:T(8,128)(2,1)S(1)}, bf16[512,128]{1,0:T(8,128)(2,1)S(1)}, u32[]{:S(2)}, u32[]{:S(2)}) collective-permute-start(bf16[512,128]{1,0:T(8,128)(2,1)S(1)} %get-tuple-element.19), channel_id=1, source_target_pairs={{0,1},{1,0},{2,3},{3,2},{4,5},{5,4},{6,7},{7,6},{8,9},{9,8},{10,11... | collective-permute-start | bytes 393224 | tf_op jit(solution)/shard_map/ppermute | solution.py:165
  14.9 5.0 %collective-permute-start.5 = (bf16[512,128]{1,0:T(8,128)(2,1)S(1)}, bf16[512,128]{1,0:T(8,128)(2,1)S(1)}, u32[]{:S(2)}, u32[]{:S(2)}) collective-permute-start(bf16[512,128]{1,0:T(8,128)(2,1)S(1)} %get-tuple-element.20), channel_id=1, source_target_pairs={{0,2},{1,3},{2,0},{3,1},{4,6},{5,7},{6,4},{7,5},{8,10},{9,11},{10,... | collective-permute-start | bytes 393224 | tf_op jit(solution)/shard_map/ppermute | solution.py:165

commit v3 on v2

--- a/solution.py
+++ b/solution.py
@@ -82,8 +82,7 @@
 
 
 def exchange_kernel(rows, matches, *refs):
-    source_ref, refs = refs[0], refs[1:]
-    target_refs, refs = refs[:matches], refs[matches:]
+    target_refs, source_ref, refs = refs[:matches], refs[matches], refs[matches + 1 :]
     rows_ref, forward_ref, inverse_ref, twiddle_ref, coulomb_ref = refs[:5]
     own_refs, return_ref = refs[5 : 5 + matches], refs[5 + matches]
     scratch = refs[6 + matches :]
@@ -194,9 +193,9 @@
         scratch_shapes=[pltpu.VMEM((2 * rows, LANES), jnp.float32)] * (matches + 1),
         compiler_params=limits,
         name="exchange",
-    )(interleaved(source, lay), *[interleaved(t, lay) for t in targets], *tables)
-    arrived = [shifted(outs[matches], -steps)]
-    arrived += [partner(outs[j], j) for j in range(matches)]
+    )(*[interleaved(t, lay) for t in targets], interleaved(source, lay), *tables)
+    arrived = [partner(outs[j], j) for j in range(matches)]
+    arrived += [shifted(outs[matches], -steps)]
     total = pl.pallas_call(
         lambda *refs: sum_kernel(rows, *refs),
         out_shape=shape(2 * rows, LANES, dtype=jnp.float32),

time: 20.7 us -> 18.8 us (0.908)
  waiting for transfers between devices: 8.45 us -> 5.06 us
  starting transfers between devices: 8.92 us -> 10.3 us
    ppermute x2, waiting for transfers between devices: 5.42 us -> 1.87 us  [shifted(): lax.ppermute(value, 'ka', [(k, (k + by) % kpoints) for k in range(kpoints)])]
    ppermute x2, starting transfers between devices: 3.43 us -> 5.21 us  [shifted(): lax.ppermute(value, 'ka', [(k, (k + by) % kpoints) for k in range(kpoints)])]
    ppermute x4, starting transfers between devices: 5.49 us -> 5.13 us  [partner(): lax.ppermute(value, 'ba', [(b, b ^ 2 ** apart) for b in range(groups)])]
  transfers between devices with their start and end apart: 6 -> 6, of which waited for: 5 -> 5; matrix products, arithmetic and copies ran while one was open for 0% -> 0% of each run, Pallas kernels for 7% -> 8%
where the time goes in v3:
time: 18.8 us; the launch traced here: 18.6 us
  starting transfers between devices  10.3 us (55%)
  waiting for transfers between devices  5.06 us (27%)
  Pallas kernels  3.19 us (17%)
    ppermute x2, starting transfers between devices, shifted(): lax.ppermute(value, 'ka', [(k, (k + by) % kpoints) for k in range(kpoints)])  5.21 us
    ppermute x4, starting transfers between devices, partner(): lax.ppermute(value, 'ba', [(b, b ^ 2 ** apart) for b in range(groups)])  5.13 us
    ppermute x4, waiting for transfers between devices, partner(): lax.ppermute(value, 'ba', [(b, b ^ 2 ** apart) for b in range(groups)])  3.19 us
    ppermute x2, waiting for transfers between devices, shifted(): lax.ppermute(value, 'ka', [(k, (k + by) % kpoints) for k in range(kpoints)])  1.87 us
    pallas_call x1, Pallas kernels, per_device(): pl.pallas_call(lambda *refs: setup_kernel(lay, steps, *refs), out_shape=[...  1.4 us
    pallas_call x1, Pallas kernels, per_device(): pl.pallas_call(lambda *refs: exchange_kernel(rows, matches, *refs), out_s...  1.05 us
    pallas_call x1, Pallas kernels, per_device(): pl.pallas_call(lambda *refs: sum_kernel(rows, *refs), out_shape=shape(2 *...  0.75 us
  transfers between devices with their start and end apart: 6, of which 5 were waited for; matrix products, arithmetic and copies ran while one was open for 0% of the time, Pallas kernels for 8%

profile of v3, /device:TPU:0, one launch (start us, length us, event | category | flops | bytes accessed | tf_op | source)
XLA Modules:
  0.0 18.6 jit_solution(17065798380987673371)
XLA Ops:
  0.0 0.0 copy-start
  0.0 3.0 %collective-permute-start.2 = (bf16[2,32768]{1,0:T(2,128)(2,1)}, bf16[2,32768]{1,0:T(2,128)(2,1)S(1)}, u32[]{:S(2)}, u32[]{:S(2)}) collective-permute-start(bf16[2,32768]{1,0:T(2,128)(2,1)} %bitcast.26), channel_id=1, source_target_pairs={{0,8},{4,12},{8,16},{12,20},{16,24},{20,28},{24,0},{28,4},{1,9},{5... | collective-permute-start | bytes 393224 | tf_op jit(solution)/shard_map/ppermute | solution.py:161
  3.0 1.5 %collective-permute-start.1 = (bf16[2,32768]{1,0:T(2,128)(2,1)}, bf16[2,32768]{1,0:T(2,128)(2,1)S(1)}, u32[]{:S(2)}, u32[]{:S(2)}) collective-permute-start(bf16[2,32768]{1,0:T(2,128)(2,1)} %bitcast.27), channel_id=1, source_target_pairs={{0,2},{1,3},{2,0},{3,1},{4,6},{5,7},{6,4},{7,5},{8,10},{9,11},{10,... | collective-permute-start | bytes 393224 | tf_op jit(solution)/shard_map/ppermute | solution.py:164
  4.5 1.5 %collective-permute-start = (bf16[2,32768]{1,0:T(2,128)(2,1)}, bf16[2,32768]{1,0:T(2,128)(2,1)S(1)}, u32[]{:S(2)}, u32[]{:S(2)}) collective-permute-start(bf16[2,32768]{1,0:T(2,128)(2,1)} %bitcast.28), channel_id=1, source_target_pairs={{0,1},{1,0},{2,3},{3,2},{4,5},{5,4},{6,7},{7,6},{8,9},{9,8},{10,11... | collective-permute-start | bytes 393224 | tf_op jit(solution)/shard_map/ppermute | solution.py:164
  6.0 0.0 copy-done
  6.0 1.4 %setup.1 = (bf16[512,256]{1,0:T(8,128)(2,1)S(1)}, bf16[256,256]{1,0:T(8,128)(2,1)S(1)}, bf16[256,256]{1,0:T(8,128)(2,1)S(1)}, f32[512,128]{1,0:T(8,128)S(1)}, f32[256,128]{1,0:T(8,128)S(1)}) custom-call(s32[3,8]{1,0:T(4,128)S(1)} %bitcast.25), custom_call_target="tpu_custom_call" | custom-call | tf_op jit(solution)/shard_map/setup/pallas_call | solution.py:173
  7.4 1.3 %collective-permute-done.2 = bf16[2,32768]{1,0:T(2,128)(2,1)S(1)} collective-permute-done((bf16[2,32768]{1,0:T(2,128)(2,1)}, bf16[2,32768]{1,0:T(2,128)(2,1)S(1)}, u32[]{:S(2)}, u32[]{:S(2)}) %collective-permute-start.2) | collective-permute-done | bytes 131104 | tf_op jit(solution)/shard_map/ppermute | solution.py:161
  8.8 0.0 collective-permute-done.1
  8.8 1.0 %collective-permute-done = bf16[2,32768]{1,0:T(2,128)(2,1)S(1)} collective-permute-done((bf16[2,32768]{1,0:T(2,128)(2,1)}, bf16[2,32768]{1,0:T(2,128)(2,1)S(1)}, u32[]{:S(2)}, u32[]{:S(2)}) %collective-permute-start) | collective-permute-done | bytes 131104 | tf_op jit(solution)/shard_map/ppermute | solution.py:164
  9.7 1.0 %exchange.1 = (bf16[512,128]{1,0:T(8,128)(2,1)S(1)}, bf16[512,128]{1,0:T(8,128)(2,1)S(1)}, bf16[512,128]{1,0:T(8,128)(2,1)S(1)}) custom-call(bf16[512,128]{1,0:T(8,128)(2,1)S(1)} %bitcast.24, bf16[512,128]{1,0:T(8,128)(2,1)S(1)} %bitcast.23, bf16[512,128]{1,0:T(8,128)(2,1)S(1)} %bitcast.22, bf16[512,256]{1,0:T(8,128)(2,1)S(1)} %get-tuple-element.13.refs_3_, ...), custom_call_target="tpu_custom_call" | custom-call | tf_op jit(solution)/shard_map/exchange/pallas_call | solution.py:188
  10.8 1.6 %collective-permute-start.3 = (bf16[512,128]{1,0:T(8,128)(2,1)S(1)}, bf16[512,128]{1,0:T(8,128)(2,1)S(1)}, u32[]{:S(2)}, u32[]{:S(2)}) collective-permute-start(bf16[512,128]{1,0:T(8,128)(2,1)S(1)} %get-tuple-element.18), channel_id=1, source_target_pairs={{0,1},{1,0},{2,3},{3,2},{4,5},{5,4},{6,7},{7,6},{8,9},{9,8},{10,11... | collective-permute-start | bytes 393224 | tf_op jit(solution)/shard_map/ppermute | solution.py:164
  12.3 0.6 %collective-permute-start.4 = (bf16[512,128]{1,0:T(8,128)(2,1)S(1)}, bf16[512,128]{1,0:T(8,128)(2,1)S(1)}, u32[]{:S(2)}, u32[]{:S(2)}) collective-permute-start(bf16[512,128]{1,0:T(8,128)(2,1)S(1)} %get-tuple-element.19), channel_id=1, source_target_pairs={{0,2},{1,3},{2,0},{3,1},{4,6},{5,7},{6,4},{7,5},{8,10},{9,11},{10,... | collective-permute-start | bytes 393224 | tf_op jit(solution)/shard_map/ppermute | solution.py:164
  12.9 2.2 %collective-permute-start.5 = (bf16[512,128]{1,0:T(8,128)(2,1)S(1)}, bf16[512,128]{1,0:T(8,128)(2,1)S(1)}, u32[]{:S(2)}, u32[]{:S(2)}) collective-permute-start(bf16[512,128]{1,0:T(8,128)(2,1)S(1)} %get-tuple-element.20), channel_id=1, source_target_pairs={{0,24},{4,28},{8,0},{12,4},{16,8},{20,12},{24,16},{28,20},{1,25},{... | collective-permute-start | bytes 393224 | tf_op jit(solution)/shard_map/ppermute | solution.py:161
  15.1 0.7 %collective-permute-done.3.refs_0_ = bf16[512,128]{1,0:T(8,128)(2,1)S(1)} collective-permute-done((bf16[512,128]{1,0:T(8,128)(2,1)S(1)}, bf16[512,128]{1,0:T(8,128)(2,1)S(1)}, u32[]{:S(2)}, u32[]{:S(2)}) %collective-permute-start.3) | collective-permute-done | bytes 131104 | tf_op jit(solution)/shard_map/ppermute | solution.py:164
  15.8 1.5 %collective-permute-done.4.refs_1_ = bf16[512,128]{1,0:T(8,128)(2,1)S(1)} collective-permute-done((bf16[512,128]{1,0:T(8,128)(2,1)S(1)}, bf16[512,128]{1,0:T(8,128)(2,1)S(1)}, u32[]{:S(2)}, u32[]{:S(2)}) %collective-permute-start.4) | collective-permute-done | bytes 131104 | tf_op jit(solution)/shard_map/ppermute | solution.py:164
  17.3 0.6 %collective-permute-done.5.refs_2_ = bf16[512,128]{1,0:T(8,128)(2,1)S(1)} collective-permute-done((bf16[512,128]{1,0:T(8,128)(2,1)S(1)}, bf16[512,128]{1,0:T(8,128)(2,1)S(1)}, u32[]{:S(2)}, u32[]{:S(2)}) %collective-permute-start.5) | collective-permute-done | bytes 131104 | tf_op jit(solution)/shard_map/ppermute | solution.py:161
  17.9 0.7 %total.1 = f32[512,128]{1,0:T(8,128)} custom-call(bf16[512,128]{1,0:T(8,128)(2,1)S(1)} %collective-permute-done.3.refs_0_, bf16[512,128]{1,0:T(8,128)(2,1)S(1)} %collective-permute-done.4.refs_1_, bf16[512,128]{1,0:T(8,128)(2,1)S(1)} %collective-permute-done.5.refs_2_), custom_call_target="tpu_custom_call" | custom-call | tf_op jit(solution)/shard_map/total/pallas_call | solution.py:199
Async XLA Ops:
  0.0 6.0 %copy-start = (s32[8,3]{0,1:T(4,128)S(1)}, s32[8,3]{0,1:T(4,128)}, u32[]{:S(2)}) copy-start(s32[8,3]{0,1:T(4,128)} %param.3) | copy-start | bytes 292
  0.0 8.8 %collective-permute-start.2 = (bf16[2,32768]{1,0:T(2,128)(2,1)}, bf16[2,32768]{1,0:T(2,128)(2,1)S(1)}, u32[]{:S(2)}, u32[]{:S(2)}) collective-permute-start(bf16[2,32768]{1,0:T(2,128)(2,1)} %bitcast.26), channel_id=1, source_target_pairs={{0,8},{4,12},{8,16},{12,20},{16,24},{20,28},{24,0},{28,4},{1,9},{5... | collective-permute-start | bytes 393224 | tf_op jit(solution)/shard_map/ppermute | solution.py:161
  3.0 5.7 %collective-permute-start.1 = (bf16[2,32768]{1,0:T(2,128)(2,1)}, bf16[2,32768]{1,0:T(2,128)(2,1)S(1)}, u32[]{:S(2)}, u32[]{:S(2)}) collective-permute-start(bf16[2,32768]{1,0:T(2,128)(2,1)} %bitcast.27), channel_id=1, source_target_pairs={{0,2},{1,3},{2,0},{3,1},{4,6},{5,7},{6,4},{7,5},{8,10},{9,11},{10,... | collective-permute-start | bytes 393224 | tf_op jit(solution)/shard_map/ppermute | solution.py:164
  4.5 5.2 %collective-permute-start = (bf16[2,32768]{1,0:T(2,128)(2,1)}, bf16[2,32768]{1,0:T(2,128)(2,1)S(1)}, u32[]{:S(2)}, u32[]{:S(2)}) collective-permute-start(bf16[2,32768]{1,0:T(2,128)(2,1)} %bitcast.28), channel_id=1, source_target_pairs={{0,1},{1,0},{2,3},{3,2},{4,5},{5,4},{6,7},{7,6},{8,9},{9,8},{10,11... | collective-permute-start | bytes 393224 | tf_op jit(solution)/shard_map/ppermute | solution.py:164
  10.8 5.0 %collective-permute-start.3 = (bf16[512,128]{1,0:T(8,128)(2,1)S(1)}, bf16[512,128]{1,0:T(8,128)(2,1)S(1)}, u32[]{:S(2)}, u32[]{:S(2)}) collective-permute-start(bf16[512,128]{1,0:T(8,128)(2,1)S(1)} %get-tuple-element.18), channel_id=1, source_target_pairs={{0,1},{1,0},{2,3},{3,2},{4,5},{5,4},{6,7},{7,6},{8,9},{9,8},{10,11... | collective-permute-start | bytes 393224 | tf_op jit(solution)/shard_map/ppermute | solution.py:164
  12.3 5.0 %collective-permute-start.4 = (bf16[512,128]{1,0:T(8,128)(2,1)S(1)}, bf16[512,128]{1,0:T(8,128)(2,1)S(1)}, u32[]{:S(2)}, u32[]{:S(2)}) collective-permute-start(bf16[512,128]{1,0:T(8,128)(2,1)S(1)} %get-tuple-element.19), channel_id=1, source_target_pairs={{0,2},{1,3},{2,0},{3,1},{4,6},{5,7},{6,4},{7,5},{8,10},{9,11},{10,... | collective-permute-start | bytes 393224 | tf_op jit(solution)/shard_map/ppermute | solution.py:164
  12.9 5.0 %collective-permute-start.5 = (bf16[512,128]{1,0:T(8,128)(2,1)S(1)}, bf16[512,128]{1,0:T(8,128)(2,1)S(1)}, u32[]{:S(2)}, u32[]{:S(2)}) collective-permute-start(bf16[512,128]{1,0:T(8,128)(2,1)S(1)} %get-tuple-element.20), channel_id=1, source_target_pairs={{0,24},{4,28},{8,0},{12,4},{16,8},{20,12},{24,16},{28,20},{1,25},{... | collective-permute-start | bytes 393224 | tf_op jit(solution)/shard_map/ppermute | solution.py:161

commit v4 on v3

--- a/solution.py
+++ b/solution.py
@@ -95,44 +95,52 @@
     targets = [split_parts(target_refs[j], scratch[1 + j], rows) for j in range(matches)]
     coulomb = coulomb_ref[...]
     coulomb = jnp.concatenate([coulomb, coulomb], axis=1)
-    tw_cos, tw_sin = twiddle_ref[:rows], twiddle_ref[rows:]
-
-    stage = []
+
+    pairs = []
     for t_real, t_imag in targets:
         real = s_real * t_real + s_imag * t_imag
         imag = s_real * t_imag - s_imag * t_real
-        stage.append(jnp.concatenate([real.astype(bf16), imag.astype(bf16)], axis=1))
-    stage = [dot(rows_ref[...], pair) for pair in stage]
-    after = []
-    for both in stage:
-        real = both[:rows, :LANES] + both[rows:, LANES:]
-        imag = both[:rows, LANES:] - both[rows:, :LANES]
-        turned_real = real * tw_cos + imag * tw_sin
-        turned_imag = imag * tw_cos - real * tw_sin
-        after.append(jnp.concatenate([turned_real.astype(bf16), turned_imag.astype(bf16)], axis=1))
-    stage = [dot(field, forward_ref[...]) for field in after]
-    stage = [(field * coulomb).astype(bf16) for field in stage]
-    stage = [dot(field, inverse_ref[...]) for field in stage]
-    after = []
-    for both in stage:
-        real, imag = both[:, :LANES], both[:, LANES:]
-        turned_real = real * tw_cos - imag * tw_sin
-        turned_imag = imag * tw_cos + real * tw_sin
-        after.append(jnp.concatenate([turned_real.astype(bf16), turned_imag.astype(bf16)], axis=1))
-    stage = [dot(rows_ref[...], field) for field in after]
-    total_real, total_imag = None, None
-    for j, both in enumerate(stage):
-        v_real = both[:rows, :LANES] - both[rows:, LANES:]
-        v_imag = both[:rows, LANES:] + both[rows:, :LANES]
-        t_real, t_imag = targets[j]
-        own_refs[j][:rows] = (s_imag * v_imag - s_real * v_real).astype(bf16)
-        own_refs[j][rows:] = (-(s_real * v_imag + s_imag * v_real)).astype(bf16)
-        real = -(t_real * v_real + t_imag * v_imag)
-        imag = t_real * v_imag - t_imag * v_real
-        total_real = real if total_real is None else total_real + real
-        total_imag = imag if total_imag is None else total_imag + imag
-    return_ref[:rows] = total_real.astype(bf16)
-    return_ref[rows:] = total_imag.astype(bf16)
+        pairs.append(jnp.concatenate([real.astype(bf16), imag.astype(bf16)], axis=1))
+
+    def turned(real, imag, cos, sin):
+        return jnp.concatenate([(real * cos + imag * sin).astype(bf16), (imag * cos - real * sin).astype(bf16)], axis=1)
+
+    chunk = rows
+    spans = [slice(at, at + chunk) for at in range(0, rows, chunk)]
+    tables = []
+    for span in spans:
+        lower = slice(rows + span.start, rows + span.stop)
+        tables.append((rows_ref[span], rows_ref[lower], twiddle_ref[span], twiddle_ref[lower]))
+
+    fields = [[] for _ in pairs]
+    for span, (row_cos, row_sin, tw_cos, tw_sin) in zip(spans, tables):
+        both = [(dot(row_cos, pair), dot(row_sin, pair)) for pair in pairs]
+        stage = [
+            turned(c[:, :LANES] + s[:, LANES:], c[:, LANES:] - s[:, :LANES], tw_cos, tw_sin) for c, s in both
+        ]
+        stage = [dot(field, forward_ref[...]) for field in stage]
+        stage = [(field * coulomb[span]).astype(bf16) for field in stage]
+        stage = [dot(field, inverse_ref[...]) for field in stage]
+        for j, field in enumerate(stage):
+            fields[j].append(turned(field[:, :LANES], field[:, LANES:], tw_cos, -tw_sin))
+    fields = [jnp.concatenate(parts, axis=0) for parts in fields]
+    for span, (row_cos, row_sin, _, _) in zip(spans, tables):
+        lower = slice(rows + span.start, rows + span.stop)
+        total_real, total_imag = None, None
+        for j, field in enumerate(fields):
+            c, s = dot(row_cos, field), dot(row_sin, field)
+            v_real = c[:, :LANES] - s[:, LANES:]
+            v_imag = c[:, LANES:] + s[:, :LANES]
+            (t_real, t_imag), a, b = targets[j], s_real[span], s_imag[span]
+            t_real, t_imag = t_real[span], t_imag[span]
+            own_refs[j][span] = (b * v_imag - a * v_real).astype(bf16)
+            own_refs[j][lower] = (-(a * v_imag + b * v_real)).astype(bf16)
+            real = t_real * v_real + t_imag * v_imag
+            imag = t_real * v_imag - t_imag * v_real
+            total_real = real if total_real is None else total_real + real
+            total_imag = imag if total_imag is None else total_imag + imag
+        return_ref[span] = (-total_real).astype(bf16)
+        return_ref[lower] = total_imag.astype(bf16)
 
 
 def sum_kernel(rows, *refs):

time: 18.8 us -> 18.6 us (0.989)
  Pallas kernels: 3.19 us -> 2.99 us
    pallas_call x1, Pallas kernels: 1.05 us -> 0.85 us  [per_device(): pl.pallas_call(lambda *refs: exchange_kernel(rows, matches, *refs), out_s...]
where the time goes in v4:
time: 18.6 us; the launch traced here: 18.4 us
  starting transfers between devices  10.3 us (55%)
  waiting for transfers between devices  5.05 us (27%)
  Pallas kernels  2.99 us (16%)
    ppermute x2, starting transfers between devices, shifted(): lax.ppermute(value, 'ka', [(k, (k + by) % kpoints) for k in range(kpoints)])  5.22 us
    ppermute x4, starting transfers between devices, partner(): lax.ppermute(value, 'ba', [(b, b ^ 2 ** apart) for b in range(groups)])  5.13 us
    ppermute x4, waiting for transfers between devices, partner(): lax.ppermute(value, 'ba', [(b, b ^ 2 ** apart) for b in range(groups)])  3.18 us
    ppermute x2, waiting for transfers between devices, shifted(): lax.ppermute(value, 'ka', [(k, (k + by) % kpoints) for k in range(kpoints)])  1.87 us
    pallas_call x1, Pallas kernels, per_device(): pl.pallas_call(lambda *refs: setup_kernel(lay, steps, *refs), out_shape=[...  1.4 us
    pallas_call x1, Pallas kernels, per_device(): pl.pallas_call(lambda *refs: exchange_kernel(rows, matches, *refs), out_s...  0.85 us
    pallas_call x1, Pallas kernels, per_device(): pl.pallas_call(lambda *refs: sum_kernel(rows, *refs), out_shape=shape(2 *...  0.75 us
  transfers between devices with their start and end apart: 6, of which 5 were waited for; matrix products, arithmetic and copies ran while one was open for 0% of the time, Pallas kernels for 8%

profile of v4, /device:TPU:0, one launch (start us, length us, event | category | flops | bytes accessed | tf_op | source)
XLA Modules:
  0.0 18.4 jit_solution(15584802760434279663)
XLA Ops:
  0.0 0.0 copy-start
  0.0 3.0 %collective-permute-start.2 = (bf16[2,32768]{1,0:T(2,128)(2,1)}, bf16[2,32768]{1,0:T(2,128)(2,1)S(1)}, u32[]{:S(2)}, u32[]{:S(2)}) collective-permute-start(bf16[2,32768]{1,0:T(2,128)(2,1)} %bitcast.26), channel_id=1, source_target_pairs={{0,8},{4,12},{8,16},{12,20},{16,24},{20,28},{24,0},{28,4},{1,9},{5... | collective-permute-start | bytes 393224 | tf_op jit(solution)/shard_map/ppermute | solution.py:169
  3.0 1.5 %collective-permute-start.1 = (bf16[2,32768]{1,0:T(2,128)(2,1)}, bf16[2,32768]{1,0:T(2,128)(2,1)S(1)}, u32[]{:S(2)}, u32[]{:S(2)}) collective-permute-start(bf16[2,32768]{1,0:T(2,128)(2,1)} %bitcast.27), channel_id=1, source_target_pairs={{0,2},{1,3},{2,0},{3,1},{4,6},{5,7},{6,4},{7,5},{8,10},{9,11},{10,... | collective-permute-start | bytes 393224 | tf_op jit(solution)/shard_map/ppermute | solution.py:172
  4.5 1.5 %collective-permute-start = (bf16[2,32768]{1,0:T(2,128)(2,1)}, bf16[2,32768]{1,0:T(2,128)(2,1)S(1)}, u32[]{:S(2)}, u32[]{:S(2)}) collective-permute-start(bf16[2,32768]{1,0:T(2,128)(2,1)} %bitcast.28), channel_id=1, source_target_pairs={{0,1},{1,0},{2,3},{3,2},{4,5},{5,4},{6,7},{7,6},{8,9},{9,8},{10,11... | collective-permute-start | bytes 393224 | tf_op jit(solution)/shard_map/ppermute | solution.py:172
  6.0 0.0 copy-done
  6.0 1.4 %setup.1 = (bf16[512,256]{1,0:T(8,128)(2,1)S(1)}, bf16[256,256]{1,0:T(8,128)(2,1)S(1)}, bf16[256,256]{1,0:T(8,128)(2,1)S(1)}, f32[512,128]{1,0:T(8,128)S(1)}, f32[256,128]{1,0:T(8,128)S(1)}) custom-call(s32[3,8]{1,0:T(4,128)S(1)} %bitcast.25), custom_call_target="tpu_custom_call" | custom-call | tf_op jit(solution)/shard_map/setup/pallas_call | solution.py:181
  7.4 1.3 %collective-permute-done.2 = bf16[2,32768]{1,0:T(2,128)(2,1)S(1)} collective-permute-done((bf16[2,32768]{1,0:T(2,128)(2,1)}, bf16[2,32768]{1,0:T(2,128)(2,1)S(1)}, u32[]{:S(2)}, u32[]{:S(2)}) %collective-permute-start.2) | collective-permute-done | bytes 131104 | tf_op jit(solution)/shard_map/ppermute | solution.py:169
  8.8 0.0 collective-permute-done.1
  8.8 1.0 %collective-permute-done = bf16[2,32768]{1,0:T(2,128)(2,1)S(1)} collective-permute-done((bf16[2,32768]{1,0:T(2,128)(2,1)}, bf16[2,32768]{1,0:T(2,128)(2,1)S(1)}, u32[]{:S(2)}, u32[]{:S(2)}) %collective-permute-start) | collective-permute-done | bytes 131104 | tf_op jit(solution)/shard_map/ppermute | solution.py:172
  9.7 0.8 %exchange.1 = (bf16[512,128]{1,0:T(8,128)(2,1)S(1)}, bf16[512,128]{1,0:T(8,128)(2,1)S(1)}, bf16[512,128]{1,0:T(8,128)(2,1)S(1)}) custom-call(bf16[512,128]{1,0:T(8,128)(2,1)S(1)} %bitcast.24, bf16[512,128]{1,0:T(8,128)(2,1)S(1)} %bitcast.23, bf16[512,128]{1,0:T(8,128)(2,1)S(1)} %bitcast.22, bf16[512,256]{1,0:T(8,128)(2,1)S(1)} %get-tuple-element.13.refs_3_, ...), custom_call_target="tpu_custom_call" | custom-call | tf_op jit(solution)/shard_map/exchange/pallas_call | solution.py:196
  10.6 1.6 %collective-permute-start.3 = (bf16[512,128]{1,0:T(8,128)(2,1)S(1)}, bf16[512,128]{1,0:T(8,128)(2,1)S(1)}, u32[]{:S(2)}, u32[]{:S(2)}) collective-permute-start(bf16[512,128]{1,0:T(8,128)(2,1)S(1)} %get-tuple-element.18), channel_id=1, source_target_pairs={{0,1},{1,0},{2,3},{3,2},{4,5},{5,4},{6,7},{7,6},{8,9},{9,8},{10,11... | collective-permute-start | bytes 393224 | tf_op jit(solution)/shard_map/ppermute | solution.py:172
  12.1 0.6 %collective-permute-start.4 = (bf16[512,128]{1,0:T(8,128)(2,1)S(1)}, bf16[512,128]{1,0:T(8,128)(2,1)S(1)}, u32[]{:S(2)}, u32[]{:S(2)}) collective-permute-start(bf16[512,128]{1,0:T(8,128)(2,1)S(1)} %get-tuple-element.19), channel_id=1, source_target_pairs={{0,2},{1,3},{2,0},{3,1},{4,6},{5,7},{6,4},{7,5},{8,10},{9,11},{10,... | collective-permute-start | bytes 393224 | tf_op jit(solution)/shard_map/ppermute | solution.py:172
  12.7 2.2 %collective-permute-start.5 = (bf16[512,128]{1,0:T(8,128)(2,1)S(1)}, bf16[512,128]{1,0:T(8,128)(2,1)S(1)}, u32[]{:S(2)}, u32[]{:S(2)}) collective-permute-start(bf16[512,128]{1,0:T(8,128)(2,1)S(1)} %get-tuple-element.20), channel_id=1, source_target_pairs={{0,24},{4,28},{8,0},{12,4},{16,8},{20,12},{24,16},{28,20},{1,25},{... | collective-permute-start | bytes 393224 | tf_op jit(solution)/shard_map/ppermute | solution.py:169
  14.9 0.7 %collective-permute-done.3.refs_0_ = bf16[512,128]{1,0:T(8,128)(2,1)S(1)} collective-permute-done((bf16[512,128]{1,0:T(8,128)(2,1)S(1)}, bf16[512,128]{1,0:T(8,128)(2,1)S(1)}, u32[]{:S(2)}, u32[]{:S(2)}) %collective-permute-start.3) | collective-permute-done | bytes 131104 | tf_op jit(solution)/shard_map/ppermute | solution.py:172
  15.6 1.5 %collective-permute-done.4.refs_1_ = bf16[512,128]{1,0:T(8,128)(2,1)S(1)} collective-permute-done((bf16[512,128]{1,0:T(8,128)(2,1)S(1)}, bf16[512,128]{1,0:T(8,128)(2,1)S(1)}, u32[]{:S(2)}, u32[]{:S(2)}) %collective-permute-start.4) | collective-permute-done | bytes 131104 | tf_op jit(solution)/shard_map/ppermute | solution.py:172
  17.1 0.6 %collective-permute-done.5.refs_2_ = bf16[512,128]{1,0:T(8,128)(2,1)S(1)} collective-permute-done((bf16[512,128]{1,0:T(8,128)(2,1)S(1)}, bf16[512,128]{1,0:T(8,128)(2,1)S(1)}, u32[]{:S(2)}, u32[]{:S(2)}) %collective-permute-start.5) | collective-permute-done | bytes 131104 | tf_op jit(solution)/shard_map/ppermute | solution.py:169
  17.7 0.7 %total.1 = f32[512,128]{1,0:T(8,128)} custom-call(bf16[512,128]{1,0:T(8,128)(2,1)S(1)} %collective-permute-done.3.refs_0_, bf16[512,128]{1,0:T(8,128)(2,1)S(1)} %collective-permute-done.4.refs_1_, bf16[512,128]{1,0:T(8,128)(2,1)S(1)} %collective-permute-done.5.refs_2_), custom_call_target="tpu_custom_call" | custom-call | tf_op jit(solution)/shard_map/total/pallas_call | solution.py:207
Async XLA Ops:
  0.0 6.0 %copy-start = (s32[8,3]{0,1:T(4,128)S(1)}, s32[8,3]{0,1:T(4,128)}, u32[]{:S(2)}) copy-start(s32[8,3]{0,1:T(4,128)} %param.3) | copy-start | bytes 292
  0.0 8.8 %collective-permute-start.2 = (bf16[2,32768]{1,0:T(2,128)(2,1)}, bf16[2,32768]{1,0:T(2,128)(2,1)S(1)}, u32[]{:S(2)}, u32[]{:S(2)}) collective-permute-start(bf16[2,32768]{1,0:T(2,128)(2,1)} %bitcast.26), channel_id=1, source_target_pairs={{0,8},{4,12},{8,16},{12,20},{16,24},{20,28},{24,0},{28,4},{1,9},{5... | collective-permute-start | bytes 393224 | tf_op jit(solution)/shard_map/ppermute | solution.py:169
  3.0 5.7 %collective-permute-start.1 = (bf16[2,32768]{1,0:T(2,128)(2,1)}, bf16[2,32768]{1,0:T(2,128)(2,1)S(1)}, u32[]{:S(2)}, u32[]{:S(2)}) collective-permute-start(bf16[2,32768]{1,0:T(2,128)(2,1)} %bitcast.27), channel_id=1, source_target_pairs={{0,2},{1,3},{2,0},{3,1},{4,6},{5,7},{6,4},{7,5},{8,10},{9,11},{10,... | collective-permute-start | bytes 393224 | tf_op jit(solution)/shard_map/ppermute | solution.py:172
  4.5 5.2 %collective-permute-start = (bf16[2,32768]{1,0:T(2,128)(2,1)}, bf16[2,32768]{1,0:T(2,128)(2,1)S(1)}, u32[]{:S(2)}, u32[]{:S(2)}) collective-permute-start(bf16[2,32768]{1,0:T(2,128)(2,1)} %bitcast.28), channel_id=1, source_target_pairs={{0,1},{1,0},{2,3},{3,2},{4,5},{5,4},{6,7},{7,6},{8,9},{9,8},{10,11... | collective-permute-start | bytes 393224 | tf_op jit(solution)/shard_map/ppermute | solution.py:172
  10.6 5.0 %collective-permute-start.3 = (bf16[512,128]{1,0:T(8,128)(2,1)S(1)}, bf16[512,128]{1,0:T(8,128)(2,1)S(1)}, u32[]{:S(2)}, u32[]{:S(2)}) collective-permute-start(bf16[512,128]{1,0:T(8,128)(2,1)S(1)} %get-tuple-element.18), channel_id=1, source_target_pairs={{0,1},{1,0},{2,3},{3,2},{4,5},{5,4},{6,7},{7,6},{8,9},{9,8},{10,11... | collective-permute-start | bytes 393224 | tf_op jit(solution)/shard_map/ppermute | solution.py:172
  12.1 5.0 %collective-permute-start.4 = (bf16[512,128]{1,0:T(8,128)(2,1)S(1)}, bf16[512,128]{1,0:T(8,128)(2,1)S(1)}, u32[]{:S(2)}, u32[]{:S(2)}) collective-permute-start(bf16[512,128]{1,0:T(8,128)(2,1)S(1)} %get-tuple-element.19), channel_id=1, source_target_pairs={{0,2},{1,3},{2,0},{3,1},{4,6},{5,7},{6,4},{7,5},{8,10},{9,11},{10,... | collective-permute-start | bytes 393224 | tf_op jit(solution)/shard_map/ppermute | solution.py:172
  12.7 5.0 %collective-permute-start.5 = (bf16[512,128]{1,0:T(8,128)(2,1)S(1)}, bf16[512,128]{1,0:T(8,128)(2,1)S(1)}, u32[]{:S(2)}, u32[]{:S(2)}) collective-permute-start(bf16[512,128]{1,0:T(8,128)(2,1)S(1)} %get-tuple-element.20), channel_id=1, source_target_pairs={{0,24},{4,28},{8,0},{12,4},{16,8},{20,12},{24,16},{28,20},{1,25},{... | collective-permute-start | bytes 393224 | tf_op jit(solution)/shard_map/ppermute | solution.py:169

commit v5 on v3

--- a/solution.py
+++ b/solution.py
@@ -58,7 +58,7 @@
     twiddle_ref[rows:] = sine(steps, grid)
 
     kpoints = coords_ref.shape[1]
-    here = lax.axis_index("ka")
+    here = worker(lax.axis_index("ka"))
     there = lax.rem(here + kpoints - by, kpoints)
     offset = [(coords_ref[d, here] - coords_ref[d, there]).astype(jnp.float32) / 4.0 for d in range(3)]
 
@@ -76,16 +76,21 @@
     return field.reshape(2, lay.rows, LANES).transpose(1, 0, 2).reshape(2 * lay.rows, LANES)
 
 
+def worker(device):
+    return device ^ 1
+
+
 def split_parts(ref, scratch, rows):
     scratch[...] = ref[...].astype(jnp.float32)
     return scratch[pl.ds(0, rows, 2), :], scratch[pl.ds(1, rows, 2), :]
 
 
-def exchange_kernel(rows, matches, *refs):
+def exchange_kernel(rows, slots, *refs):
+    matches = len(slots[0]) - 1
     target_refs, source_ref, refs = refs[:matches], refs[matches], refs[matches + 1 :]
     rows_ref, forward_ref, inverse_ref, twiddle_ref, coulomb_ref = refs[:5]
-    own_refs, return_ref = refs[5 : 5 + matches], refs[5 + matches]
-    scratch = refs[6 + matches :]
+    out_refs, scratch = refs[5 : 6 + matches], refs[6 + matches :]
+    odd = lax.rem(worker(lax.axis_index("ka")), 2) == 1
     f32, bf16 = jnp.float32, jnp.bfloat16
 
     def dot(a, b):
@@ -95,44 +100,44 @@
     targets = [split_parts(target_refs[j], scratch[1 + j], rows) for j in range(matches)]
     coulomb = coulomb_ref[...]
     coulomb = jnp.concatenate([coulomb, coulomb], axis=1)
-    tw_cos, tw_sin = twiddle_ref[:rows], twiddle_ref[rows:]
-
-    stage = []
+
+    pairs = []
     for t_real, t_imag in targets:
         real = s_real * t_real + s_imag * t_imag
         imag = s_real * t_imag - s_imag * t_real
-        stage.append(jnp.concatenate([real.astype(bf16), imag.astype(bf16)], axis=1))
-    stage = [dot(rows_ref[...], pair) for pair in stage]
-    after = []
-    for both in stage:
-        real = both[:rows, :LANES] + both[rows:, LANES:]
-        imag = both[:rows, LANES:] - both[rows:, :LANES]
-        turned_real = real * tw_cos + imag * tw_sin
-        turned_imag = imag * tw_cos - real * tw_sin
-        after.append(jnp.concatenate([turned_real.astype(bf16), turned_imag.astype(bf16)], axis=1))
-    stage = [dot(field, forward_ref[...]) for field in after]
+        pairs.append(jnp.concatenate([real.astype(bf16), imag.astype(bf16)], axis=1))
+
+    def turned(real, imag, cos, sin):
+        return jnp.concatenate([(real * cos + imag * sin).astype(bf16), (imag * cos - real * sin).astype(bf16)], axis=1)
+
+    row_cos, row_sin = rows_ref[:rows], rows_ref[rows:]
+    tw_cos, tw_sin = twiddle_ref[:rows], twiddle_ref[rows:]
+    both = [(dot(row_cos, pair), dot(row_sin, pair)) for pair in pairs]
+    stage = [turned(c[:, :LANES] + s[:, LANES:], c[:, LANES:] - s[:, :LANES], tw_cos, tw_sin) for c, s in both]
+    stage = [dot(field, forward_ref[...]) for field in stage]
     stage = [(field * coulomb).astype(bf16) for field in stage]
     stage = [dot(field, inverse_ref[...]) for field in stage]
-    after = []
-    for both in stage:
-        real, imag = both[:, :LANES], both[:, LANES:]
-        turned_real = real * tw_cos - imag * tw_sin
-        turned_imag = imag * tw_cos + real * tw_sin
-        after.append(jnp.concatenate([turned_real.astype(bf16), turned_imag.astype(bf16)], axis=1))
-    stage = [dot(rows_ref[...], field) for field in after]
+    stage = [turned(field[:, :LANES], field[:, LANES:], tw_cos, -tw_sin) for field in stage]
+    results = []
     total_real, total_imag = None, None
-    for j, both in enumerate(stage):
-        v_real = both[:rows, :LANES] - both[rows:, LANES:]
-        v_imag = both[:rows, LANES:] + both[rows:, :LANES]
-        t_real, t_imag = targets[j]
-        own_refs[j][:rows] = (s_imag * v_imag - s_real * v_real).astype(bf16)
-        own_refs[j][rows:] = (-(s_real * v_imag + s_imag * v_real)).astype(bf16)
-        real = -(t_real * v_real + t_imag * v_imag)
+    for (t_real, t_imag), field in zip(targets, stage):
+        c, s = dot(row_cos, field), dot(row_sin, field)
+        v_real = c[:, :LANES] - s[:, LANES:]
+        v_imag = c[:, LANES:] + s[:, :LANES]
+        real = s_imag * v_imag - s_real * v_real
+        imag = -(s_real * v_imag + s_imag * v_real)
+        results.append((real.astype(bf16), imag.astype(bf16)))
+        real = t_real * v_real + t_imag * v_imag
         imag = t_real * v_imag - t_imag * v_real
         total_real = real if total_real is None else total_real + real
         total_imag = imag if total_imag is None else total_imag + imag
-    return_ref[:rows] = total_real.astype(bf16)
-    return_ref[rows:] = total_imag.astype(bf16)
+    results.append(((-total_real).astype(bf16), total_imag.astype(bf16)))
+    for out_ref, even_slot, odd_slot in zip(out_refs, *slots):
+        for part, span in enumerate((slice(0, rows), slice(rows, 2 * rows))):
+            value = results[even_slot][part]
+            if even_slot != odd_slot:
+                value = jnp.where(odd, results[odd_slot][part], value)
+            out_ref[span] = value
 
 
 def sum_kernel(rows, *refs):
@@ -157,14 +162,22 @@
     steps = kpoints // 4
     matches = min(3, groups // 4 + 1)
 
-    def shifted(value, by):
-        return lax.ppermute(value, "ka", [(k, (k + by) % kpoints) for k in range(kpoints)])
-
-    def partner(value, apart):
-        return lax.ppermute(value, "ba", [(b, b ^ 2**apart) for b in range(groups)])
-
-    source = shifted(own, steps)
-    targets = [partner(own, j) for j in range(matches)]
+    def moved(value, step, order, back):
+        pairs = []
+        for k in range(kpoints):
+            for b in range(groups):
+                part = order[k % 2][step]
+                if part == matches:
+                    home = (k - steps) % kpoints * groups + b
+                else:
+                    home = k * groups + (b ^ 2 ** ((part + k) % matches))
+                away = worker(k) * groups + b
+                pairs.append((away, home) if back else (home, away))
+        return lax.ppermute(value, ("ka", "ba"), pairs)
+
+    straight = list(range(matches + 1))
+    arrivals = [moved(own, step, (straight, straight), False) for step in straight]
+    slots = (straight[:matches][::-1] + straight[matches:], straight[matches:] + straight[:matches])
 
     def shape(*dims, dtype=jnp.bfloat16):
         return jax.ShapeDtypeStruct(dims, dtype)
@@ -186,16 +199,15 @@
     )(kpoint_coords.T)
 
     outs = pl.pallas_call(
-        lambda *refs: exchange_kernel(rows, matches, *refs),
+        lambda *refs: exchange_kernel(rows, slots, *refs),
         out_shape=[shape(2 * rows, LANES)] * (matches + 1),
         in_specs=in_vmem(matches + 6),
         out_specs=in_vmem(matches + 1),
         scratch_shapes=[pltpu.VMEM((2 * rows, LANES), jnp.float32)] * (matches + 1),
         compiler_params=limits,
         name="exchange",
-    )(*[interleaved(t, lay) for t in targets], interleaved(source, lay), *tables)
-    arrived = [partner(outs[j], j) for j in range(matches)]
-    arrived += [shifted(outs[matches], -steps)]
+    )(*[interleaved(arrival, lay) for arrival in arrivals], *tables)
+    returned = [moved(outs[step], step, slots, True) for step in straight]
     total = pl.pallas_call(
         lambda *refs: sum_kernel(rows, *refs),
         out_shape=shape(2 * rows, LANES, dtype=jnp.float32),
@@ -203,7 +215,7 @@
         out_specs=in_vmem(1)[0],
         compiler_params=limits,
         name="total",
-    )(*arrived)
+    )(*returned)
     return total.reshape(rows, 2, LANES).transpose(1, 0, 2).reshape(1, 1, 2, cells)
 
 

time: 18.8 us -> 18.2 us (0.968)
  the two profiles are of different devices: /device:TPU:0 before, /device:TPU:1 now
where the time goes in v5:
time: 18.2 us; the launch traced here: 18.1 us
  starting transfers between devices  8.49 us (47%)
  waiting for transfers between devices  6.53 us (36%)
  Pallas kernels  3.03 us (17%)
    ppermute x6, starting transfers between devices, moved(): return lax.ppermute(value, ('ka', 'ba'), pairs)  8.49 us
    ppermute x6, waiting for transfers between devices, moved(): return lax.ppermute(value, ('ka', 'ba'), pairs)  6.53 us
    pallas_call x1, Pallas kernels, per_device(): pl.pallas_call(lambda *refs: setup_kernel(lay, steps, *refs), out_shape=[...  1.4 us
    pallas_call x1, Pallas kernels, per_device(): pl.pallas_call(lambda *refs: exchange_kernel(rows, slots, *refs), out_sha...  0.88 us
    pallas_call x1, Pallas kernels, per_device(): pl.pallas_call(lambda *refs: sum_kernel(rows, *refs), out_shape=shape(2 *...  0.75 us
  transfers between devices with their start and end apart: 6, of which 5 were waited for; matrix products, arithmetic and copies ran while one was open for 0% of the time, Pallas kernels for 8%

profile of v5, /device:TPU:1, one launch (start us, length us, event | category | flops | bytes accessed | tf_op | source)
XLA Modules:
  0.0 18.1 jit_solution(14353571589888664582)
XLA Ops:
  0.0 0.0 copy-start
  0.0 2.7 %collective-permute-start.2 = (bf16[2,32768]{1,0:T(2,128)(2,1)}, bf16[2,32768]{1,0:T(2,128)(2,1)S(1)}, u32[]{:S(2)}, u32[]{:S(2)}) collective-permute-start(bf16[2,32768]{1,0:T(2,128)(2,1)} %bitcast.26), channel_id=1, source_target_pairs={{24,4},{25,5},{26,6},{27,7},{28,0},{29,1},{30,2},{31,3},{0,12},{1,... | collective-permute-start | bytes 393224 | tf_op jit(solution)/shard_map/ppermute | solution.py:176
  2.7 0.9 %collective-permute-start.1 = (bf16[2,32768]{1,0:T(2,128)(2,1)}, bf16[2,32768]{1,0:T(2,128)(2,1)S(1)}, u32[]{:S(2)}, u32[]{:S(2)}) collective-permute-start(bf16[2,32768]{1,0:T(2,128)(2,1)} %bitcast.27), channel_id=1, source_target_pairs={{2,4},{3,5},{0,6},{1,7},{5,0},{4,1},{7,2},{6,3},{10,12},{11,13},{8... | collective-permute-start | bytes 393224 | tf_op jit(solution)/shard_map/ppermute | solution.py:176
  3.6 0.8 %collective-permute-start = (bf16[2,32768]{1,0:T(2,128)(2,1)}, bf16[2,32768]{1,0:T(2,128)(2,1)S(1)}, u32[]{:S(2)}, u32[]{:S(2)}) collective-permute-start(bf16[2,32768]{1,0:T(2,128)(2,1)} %bitcast.28), channel_id=1, source_target_pairs={{1,4},{0,5},{3,6},{2,7},{6,0},{7,1},{4,2},{5,3},{9,12},{8,13},{11,... | collective-permute-start | bytes 393224 | tf_op jit(solution)/shard_map/ppermute | solution.py:176
  4.4 0.0 copy-done
  4.4 1.4 %setup.1 = (bf16[512,256]{1,0:T(8,128)(2,1)S(1)}, bf16[256,256]{1,0:T(8,128)(2,1)S(1)}, bf16[256,256]{1,0:T(8,128)(2,1)S(1)}, f32[512,128]{1,0:T(8,128)S(1)}, f32[256,128]{1,0:T(8,128)S(1)}) custom-call(s32[3,8]{1,0:T(4,128)S(1)} %bitcast.25), custom_call_target="tpu_custom_call" | custom-call | tf_op jit(solution)/shard_map/setup/pallas_call | solution.py:186
  5.8 2.3 %collective-permute-done.2 = bf16[2,32768]{1,0:T(2,128)(2,1)S(1)} collective-permute-done((bf16[2,32768]{1,0:T(2,128)(2,1)}, bf16[2,32768]{1,0:T(2,128)(2,1)S(1)}, u32[]{:S(2)}, u32[]{:S(2)}) %collective-permute-start.2) | collective-permute-done | bytes 131104 | tf_op jit(solution)/shard_map/ppermute | solution.py:176
  8.1 0.0 collective-permute-done.1
  8.1 0.5 %collective-permute-done = bf16[2,32768]{1,0:T(2,128)(2,1)S(1)} collective-permute-done((bf16[2,32768]{1,0:T(2,128)(2,1)}, bf16[2,32768]{1,0:T(2,128)(2,1)S(1)}, u32[]{:S(2)}, u32[]{:S(2)}) %collective-permute-start) | collective-permute-done | bytes 131104 | tf_op jit(solution)/shard_map/ppermute | solution.py:176
  8.6 0.9 %exchange.1 = (bf16[512,128]{1,0:T(8,128)(2,1)S(1)}, bf16[512,128]{1,0:T(8,128)(2,1)S(1)}, bf16[512,128]{1,0:T(8,128)(2,1)S(1)}) custom-call(bf16[512,128]{1,0:T(8,128)(2,1)S(1)} %bitcast.24, bf16[512,128]{1,0:T(8,128)(2,1)S(1)} %bitcast.23, bf16[512,128]{1,0:T(8,128)(2,1)S(1)} %bitcast.22, bf16[512,256]{1,0:T(8,128)(2,1)S(1)} %get-tuple-element.13.refs_3_, ...), custom_call_target="tpu_custom_call" | custom-call | tf_op jit(solution)/shard_map/exchange/pallas_call | solution.py:201
  9.5 1.8 %collective-permute-start.3 = (bf16[512,128]{1,0:T(8,128)(2,1)S(1)}, bf16[512,128]{1,0:T(8,128)(2,1)S(1)}, u32[]{:S(2)}, u32[]{:S(2)}) collective-permute-start(bf16[512,128]{1,0:T(8,128)(2,1)S(1)} %get-tuple-element.18), channel_id=1, source_target_pairs={{4,2},{5,3},{6,0},{7,1},{0,28},{1,29},{2,30},{3,31},{12,10},{13,11... | collective-permute-start | bytes 393224 | tf_op jit(solution)/shard_map/ppermute | solution.py:176
  11.3 1.6 %collective-permute-start.4 = (bf16[512,128]{1,0:T(8,128)(2,1)S(1)}, bf16[512,128]{1,0:T(8,128)(2,1)S(1)}, u32[]{:S(2)}, u32[]{:S(2)}) collective-permute-start(bf16[512,128]{1,0:T(8,128)(2,1)S(1)} %get-tuple-element.19), channel_id=1, source_target_pairs={{4,1},{5,0},{6,3},{7,2},{0,6},{1,7},{2,4},{3,5},{12,9},{13,8},{14,... | collective-permute-start | bytes 393224 | tf_op jit(solution)/shard_map/ppermute | solution.py:176
  12.9 0.6 %collective-permute-start.5 = (bf16[512,128]{1,0:T(8,128)(2,1)S(1)}, bf16[512,128]{1,0:T(8,128)(2,1)S(1)}, u32[]{:S(2)}, u32[]{:S(2)}) collective-permute-start(bf16[512,128]{1,0:T(8,128)(2,1)S(1)} %get-tuple-element.20), channel_id=1, source_target_pairs={{4,24},{5,25},{6,26},{7,27},{0,5},{1,4},{2,7},{3,6},{12,0},{13,1},... | collective-permute-start | bytes 393224 | tf_op jit(solution)/shard_map/ppermute | solution.py:176
  13.6 0.8 %collective-permute-done.3.refs_0_ = bf16[512,128]{1,0:T(8,128)(2,1)S(1)} collective-permute-done((bf16[512,128]{1,0:T(8,128)(2,1)S(1)}, bf16[512,128]{1,0:T(8,128)(2,1)S(1)}, u32[]{:S(2)}, u32[]{:S(2)}) %collective-permute-start.3) | collective-permute-done | bytes 131104 | tf_op jit(solution)/shard_map/ppermute | solution.py:176
  14.3 1.7 %collective-permute-done.4.refs_1_ = bf16[512,128]{1,0:T(8,128)(2,1)S(1)} collective-permute-done((bf16[512,128]{1,0:T(8,128)(2,1)S(1)}, bf16[512,128]{1,0:T(8,128)(2,1)S(1)}, u32[]{:S(2)}, u32[]{:S(2)}) %collective-permute-start.4) | collective-permute-done | bytes 131104 | tf_op jit(solution)/shard_map/ppermute | solution.py:176
  16.0 1.3 %collective-permute-done.5.refs_2_ = bf16[512,128]{1,0:T(8,128)(2,1)S(1)} collective-permute-done((bf16[512,128]{1,0:T(8,128)(2,1)S(1)}, bf16[512,128]{1,0:T(8,128)(2,1)S(1)}, u32[]{:S(2)}, u32[]{:S(2)}) %collective-permute-start.5) | collective-permute-done | bytes 131104 | tf_op jit(solution)/shard_map/ppermute | solution.py:176
  17.3 0.7 %total.1 = f32[512,128]{1,0:T(8,128)} custom-call(bf16[512,128]{1,0:T(8,128)(2,1)S(1)} %collective-permute-done.3.refs_0_, bf16[512,128]{1,0:T(8,128)(2,1)S(1)} %collective-permute-done.4.refs_1_, bf16[512,128]{1,0:T(8,128)(2,1)S(1)} %collective-permute-done.5.refs_2_), custom_call_target="tpu_custom_call" | custom-call | tf_op jit(solution)/shard_map/total/pallas_call | solution.py:211
Async XLA Ops:
  0.0 4.4 %copy-start = (s32[8,3]{0,1:T(4,128)S(1)}, s32[8,3]{0,1:T(4,128)}, u32[]{:S(2)}) copy-start(s32[8,3]{0,1:T(4,128)} %param.3) | copy-start | bytes 292
  0.0 8.1 %collective-permute-start.2 = (bf16[2,32768]{1,0:T(2,128)(2,1)}, bf16[2,32768]{1,0:T(2,128)(2,1)S(1)}, u32[]{:S(2)}, u32[]{:S(2)}) collective-permute-start(bf16[2,32768]{1,0:T(2,128)(2,1)} %bitcast.26), channel_id=1, source_target_pairs={{24,4},{25,5},{26,6},{27,7},{28,0},{29,1},{30,2},{31,3},{0,12},{1,... | collective-permute-start | bytes 393224 | tf_op jit(solution)/shard_map/ppermute | solution.py:176
  2.7 5.4 %collective-permute-start.1 = (bf16[2,32768]{1,0:T(2,128)(2,1)}, bf16[2,32768]{1,0:T(2,128)(2,1)S(1)}, u32[]{:S(2)}, u32[]{:S(2)}) collective-permute-start(bf16[2,32768]{1,0:T(2,128)(2,1)} %bitcast.27), channel_id=1, source_target_pairs={{2,4},{3,5},{0,6},{1,7},{5,0},{4,1},{7,2},{6,3},{10,12},{11,13},{8... | collective-permute-start | bytes 393224 | tf_op jit(solution)/shard_map/ppermute | solution.py:176
  3.6 5.0 %collective-permute-start = (bf16[2,32768]{1,0:T(2,128)(2,1)}, bf16[2,32768]{1,0:T(2,128)(2,1)S(1)}, u32[]{:S(2)}, u32[]{:S(2)}) collective-permute-start(bf16[2,32768]{1,0:T(2,128)(2,1)} %bitcast.28), channel_id=1, source_target_pairs={{1,4},{0,5},{3,6},{2,7},{6,0},{7,1},{4,2},{5,3},{9,12},{8,13},{11,... | collective-permute-start | bytes 393224 | tf_op jit(solution)/shard_map/ppermute | solution.py:176
  9.5 4.8 %collective-permute-start.3 = (bf16[512,128]{1,0:T(8,128)(2,1)S(1)}, bf16[512,128]{1,0:T(8,128)(2,1)S(1)}, u32[]{:S(2)}, u32[]{:S(2)}) collective-permute-start(bf16[512,128]{1,0:T(8,128)(2,1)S(1)} %get-tuple-element.18), channel_id=1, source_target_pairs={{4,2},{5,3},{6,0},{7,1},{0,28},{1,29},{2,30},{3,31},{12,10},{13,11... | collective-permute-start | bytes 393224 | tf_op jit(solution)/shard_map/ppermute | solution.py:176
  11.3 4.7 %collective-permute-start.4 = (bf16[512,128]{1,0:T(8,128)(2,1)S(1)}, bf16[512,128]{1,0:T(8,128)(2,1)S(1)}, u32[]{:S(2)}, u32[]{:S(2)}) collective-permute-start(bf16[512,128]{1,0:T(8,128)(2,1)S(1)} %get-tuple-element.19), channel_id=1, source_target_pairs={{4,1},{5,0},{6,3},{7,2},{0,6},{1,7},{2,4},{3,5},{12,9},{13,8},{14,... | collective-permute-start | bytes 393224 | tf_op jit(solution)/shard_map/ppermute | solution.py:176
  12.9 4.4 %collective-permute-start.5 = (bf16[512,128]{1,0:T(8,128)(2,1)S(1)}, bf16[512,128]{1,0:T(8,128)(2,1)S(1)}, u32[]{:S(2)}, u32[]{:S(2)}) collective-permute-start(bf16[512,128]{1,0:T(8,128)(2,1)S(1)} %get-tuple-element.20), channel_id=1, source_target_pairs={{4,24},{5,25},{6,26},{7,27},{0,5},{1,4},{2,7},{3,6},{12,0},{13,1},... | collective-permute-start | bytes 393224 | tf_op jit(solution)/shard_map/ppermute | solution.py:176

commit v6 on v5

--- a/solution.py
+++ b/solution.py
@@ -58,7 +58,7 @@
     twiddle_ref[rows:] = sine(steps, grid)
 
     kpoints = coords_ref.shape[1]
-    here = worker(lax.axis_index("ka"))
+    here = worker(lax.axis_index("ka"), kpoints)
     there = lax.rem(here + kpoints - by, kpoints)
     offset = [(coords_ref[d, here] - coords_ref[d, there]).astype(jnp.float32) / 4.0 for d in range(3)]
 
@@ -76,8 +76,12 @@
     return field.reshape(2, lay.rows, LANES).transpose(1, 0, 2).reshape(2 * lay.rows, LANES)
 
 
-def worker(device):
-    return device ^ 1
+def parity(k, kpoints):
+    return k % 2 if kpoints % 8 == 0 else 0 * k
+
+
+def worker(k, kpoints):
+    return k + 1 - 2 * parity(k, kpoints) if kpoints % 8 == 0 else k
 
 
 def split_parts(ref, scratch, rows):
@@ -90,7 +94,8 @@
     target_refs, source_ref, refs = refs[:matches], refs[matches], refs[matches + 1 :]
     rows_ref, forward_ref, inverse_ref, twiddle_ref, coulomb_ref = refs[:5]
     out_refs, scratch = refs[5 : 6 + matches], refs[6 + matches :]
-    odd = lax.rem(worker(lax.axis_index("ka")), 2) == 1
+    kpoints = lax.axis_size("ka")
+    odd = parity(worker(lax.axis_index("ka"), kpoints), kpoints) == 1
     f32, bf16 = jnp.float32, jnp.bfloat16
 
     def dot(a, b):
@@ -166,12 +171,12 @@
         pairs = []
         for k in range(kpoints):
             for b in range(groups):
-                part = order[k % 2][step]
+                part = order[parity(k, kpoints)][step]
                 if part == matches:
                     home = (k - steps) % kpoints * groups + b
                 else:
-                    home = k * groups + (b ^ 2 ** ((part + k) % matches))
-                away = worker(k) * groups + b
+                    home = k * groups + (b ^ 2 ** ((part + parity(k, kpoints)) % matches))
+                away = worker(k, kpoints) * groups + b
                 pairs.append((away, home) if back else (home, away))
         return lax.ppermute(value, ("ka", "ba"), pairs)
 

time: 18.2 us -> 18.2 us (level)
  no operation moved by 1% of the time
where the time goes in v6:
time: 18.2 us; the launch traced here: 18.1 us
  starting transfers between devices  8.49 us (47%)
  waiting for transfers between devices  6.53 us (36%)
  Pallas kernels  3.03 us (17%)
    ppermute x6, starting transfers between devices, moved(): return lax.ppermute(value, ('ka', 'ba'), pairs)  8.49 us
    ppermute x6, waiting for transfers between devices, moved(): return lax.ppermute(value, ('ka', 'ba'), pairs)  6.53 us
    pallas_call x1, Pallas kernels, per_device(): pl.pallas_call(lambda *refs: setup_kernel(lay, steps, *refs), out_shape=[...  1.4 us
    pallas_call x1, Pallas kernels, per_device(): pl.pallas_call(lambda *refs: exchange_kernel(rows, slots, *refs), out_sha...  0.88 us
    pallas_call x1, Pallas kernels, per_device(): pl.pallas_call(lambda *refs: sum_kernel(rows, *refs), out_shape=shape(2 *...  0.75 us
  transfers between devices with their start and end apart: 6, of which 5 were waited for; matrix products, arithmetic and copies ran while one was open for 0% of the time, Pallas kernels for 8%

profile of v6, /device:TPU:1, one launch (start us, length us, event | category | flops | bytes accessed | tf_op | source)
XLA Modules:
  0.0 18.1 jit_solution(2490767929563197454)
XLA Ops:
  0.0 0.0 copy-start
  0.0 2.7 %collective-permute-start.2 = (bf16[2,32768]{1,0:T(2,128)(2,1)}, bf16[2,32768]{1,0:T(2,128)(2,1)S(1)}, u32[]{:S(2)}, u32[]{:S(2)}) collective-permute-start(bf16[2,32768]{1,0:T(2,128)(2,1)} %bitcast.26), channel_id=1, source_target_pairs={{24,4},{25,5},{26,6},{27,7},{28,0},{29,1},{30,2},{31,3},{0,12},{1,... | collective-permute-start | bytes 393224 | tf_op jit(solution)/shard_map/ppermute | solution.py:181
  2.7 0.9 %collective-permute-start.1 = (bf16[2,32768]{1,0:T(2,128)(2,1)}, bf16[2,32768]{1,0:T(2,128)(2,1)S(1)}, u32[]{:S(2)}, u32[]{:S(2)}) collective-permute-start(bf16[2,32768]{1,0:T(2,128)(2,1)} %bitcast.27), channel_id=1, source_target_pairs={{2,4},{3,5},{0,6},{1,7},{5,0},{4,1},{7,2},{6,3},{10,12},{11,13},{8... | collective-permute-start | bytes 393224 | tf_op jit(solution)/shard_map/ppermute | solution.py:181
  3.6 0.8 %collective-permute-start = (bf16[2,32768]{1,0:T(2,128)(2,1)}, bf16[2,32768]{1,0:T(2,128)(2,1)S(1)}, u32[]{:S(2)}, u32[]{:S(2)}) collective-permute-start(bf16[2,32768]{1,0:T(2,128)(2,1)} %bitcast.28), channel_id=1, source_target_pairs={{1,4},{0,5},{3,6},{2,7},{6,0},{7,1},{4,2},{5,3},{9,12},{8,13},{11,... | collective-permute-start | bytes 393224 | tf_op jit(solution)/shard_map/ppermute | solution.py:181
  4.4 0.0 copy-done
  4.4 1.4 %setup.1 = (bf16[512,256]{1,0:T(8,128)(2,1)S(1)}, bf16[256,256]{1,0:T(8,128)(2,1)S(1)}, bf16[256,256]{1,0:T(8,128)(2,1)S(1)}, f32[512,128]{1,0:T(8,128)S(1)}, f32[256,128]{1,0:T(8,128)S(1)}) custom-call(s32[3,8]{1,0:T(4,128)S(1)} %bitcast.25), custom_call_target="tpu_custom_call" | custom-call | tf_op jit(solution)/shard_map/setup/pallas_call | solution.py:191
  5.8 2.3 %collective-permute-done.2 = bf16[2,32768]{1,0:T(2,128)(2,1)S(1)} collective-permute-done((bf16[2,32768]{1,0:T(2,128)(2,1)}, bf16[2,32768]{1,0:T(2,128)(2,1)S(1)}, u32[]{:S(2)}, u32[]{:S(2)}) %collective-permute-start.2) | collective-permute-done | bytes 131104 | tf_op jit(solution)/shard_map/ppermute | solution.py:181
  8.1 0.0 collective-permute-done.1
  8.1 0.5 %collective-permute-done = bf16[2,32768]{1,0:T(2,128)(2,1)S(1)} collective-permute-done((bf16[2,32768]{1,0:T(2,128)(2,1)}, bf16[2,32768]{1,0:T(2,128)(2,1)S(1)}, u32[]{:S(2)}, u32[]{:S(2)}) %collective-permute-start) | collective-permute-done | bytes 131104 | tf_op jit(solution)/shard_map/ppermute | solution.py:181
  8.6 0.9 %exchange.1 = (bf16[512,128]{1,0:T(8,128)(2,1)S(1)}, bf16[512,128]{1,0:T(8,128)(2,1)S(1)}, bf16[512,128]{1,0:T(8,128)(2,1)S(1)}) custom-call(bf16[512,128]{1,0:T(8,128)(2,1)S(1)} %bitcast.24, bf16[512,128]{1,0:T(8,128)(2,1)S(1)} %bitcast.23, bf16[512,128]{1,0:T(8,128)(2,1)S(1)} %bitcast.22, bf16[512,256]{1,0:T(8,128)(2,1)S(1)} %get-tuple-element.13.refs_3_, ...), custom_call_target="tpu_custom_call" | custom-call | tf_op jit(solution)/shard_map/exchange/pallas_call | solution.py:206
  9.5 1.8 %collective-permute-start.3 = (bf16[512,128]{1,0:T(8,128)(2,1)S(1)}, bf16[512,128]{1,0:T(8,128)(2,1)S(1)}, u32[]{:S(2)}, u32[]{:S(2)}) collective-permute-start(bf16[512,128]{1,0:T(8,128)(2,1)S(1)} %get-tuple-element.18), channel_id=1, source_target_pairs={{4,2},{5,3},{6,0},{7,1},{0,28},{1,29},{2,30},{3,31},{12,10},{13,11... | collective-permute-start | bytes 393224 | tf_op jit(solution)/shard_map/ppermute | solution.py:181
  11.3 1.6 %collective-permute-start.4 = (bf16[512,128]{1,0:T(8,128)(2,1)S(1)}, bf16[512,128]{1,0:T(8,128)(2,1)S(1)}, u32[]{:S(2)}, u32[]{:S(2)}) collective-permute-start(bf16[512,128]{1,0:T(8,128)(2,1)S(1)} %get-tuple-element.19), channel_id=1, source_target_pairs={{4,1},{5,0},{6,3},{7,2},{0,6},{1,7},{2,4},{3,5},{12,9},{13,8},{14,... | collective-permute-start | bytes 393224 | tf_op jit(solution)/shard_map/ppermute | solution.py:181
  12.9 0.6 %collective-permute-start.5 = (bf16[512,128]{1,0:T(8,128)(2,1)S(1)}, bf16[512,128]{1,0:T(8,128)(2,1)S(1)}, u32[]{:S(2)}, u32[]{:S(2)}) collective-permute-start(bf16[512,128]{1,0:T(8,128)(2,1)S(1)} %get-tuple-element.20), channel_id=1, source_target_pairs={{4,24},{5,25},{6,26},{7,27},{0,5},{1,4},{2,7},{3,6},{12,0},{13,1},... | collective-permute-start | bytes 393224 | tf_op jit(solution)/shard_map/ppermute | solution.py:181
  13.6 0.8 %collective-permute-done.3.refs_0_ = bf16[512,128]{1,0:T(8,128)(2,1)S(1)} collective-permute-done((bf16[512,128]{1,0:T(8,128)(2,1)S(1)}, bf16[512,128]{1,0:T(8,128)(2,1)S(1)}, u32[]{:S(2)}, u32[]{:S(2)}) %collective-permute-start.3) | collective-permute-done | bytes 131104 | tf_op jit(solution)/shard_map/ppermute | solution.py:181
  14.3 1.7 %collective-permute-done.4.refs_1_ = bf16[512,128]{1,0:T(8,128)(2,1)S(1)} collective-permute-done((bf16[512,128]{1,0:T(8,128)(2,1)S(1)}, bf16[512,128]{1,0:T(8,128)(2,1)S(1)}, u32[]{:S(2)}, u32[]{:S(2)}) %collective-permute-start.4) | collective-permute-done | bytes 131104 | tf_op jit(solution)/shard_map/ppermute | solution.py:181
  16.0 1.3 %collective-permute-done.5.refs_2_ = bf16[512,128]{1,0:T(8,128)(2,1)S(1)} collective-permute-done((bf16[512,128]{1,0:T(8,128)(2,1)S(1)}, bf16[512,128]{1,0:T(8,128)(2,1)S(1)}, u32[]{:S(2)}, u32[]{:S(2)}) %collective-permute-start.5) | collective-permute-done | bytes 131104 | tf_op jit(solution)/shard_map/ppermute | solution.py:181
  17.3 0.7 %total.1 = f32[512,128]{1,0:T(8,128)} custom-call(bf16[512,128]{1,0:T(8,128)(2,1)S(1)} %collective-permute-done.3.refs_0_, bf16[512,128]{1,0:T(8,128)(2,1)S(1)} %collective-permute-done.4.refs_1_, bf16[512,128]{1,0:T(8,128)(2,1)S(1)} %collective-permute-done.5.refs_2_), custom_call_target="tpu_custom_call" | custom-call | tf_op jit(solution)/shard_map/total/pallas_call | solution.py:216
Async XLA Ops:
  0.0 4.4 %copy-start = (s32[8,3]{0,1:T(4,128)S(1)}, s32[8,3]{0,1:T(4,128)}, u32[]{:S(2)}) copy-start(s32[8,3]{0,1:T(4,128)} %param.3) | copy-start | bytes 292
  0.0 8.1 %collective-permute-start.2 = (bf16[2,32768]{1,0:T(2,128)(2,1)}, bf16[2,32768]{1,0:T(2,128)(2,1)S(1)}, u32[]{:S(2)}, u32[]{:S(2)}) collective-permute-start(bf16[2,32768]{1,0:T(2,128)(2,1)} %bitcast.26), channel_id=1, source_target_pairs={{24,4},{25,5},{26,6},{27,7},{28,0},{29,1},{30,2},{31,3},{0,12},{1,... | collective-permute-start | bytes 393224 | tf_op jit(solution)/shard_map/ppermute | solution.py:181
  2.7 5.4 %collective-permute-start.1 = (bf16[2,32768]{1,0:T(2,128)(2,1)}, bf16[2,32768]{1,0:T(2,128)(2,1)S(1)}, u32[]{:S(2)}, u32[]{:S(2)}) collective-permute-start(bf16[2,32768]{1,0:T(2,128)(2,1)} %bitcast.27), channel_id=1, source_target_pairs={{2,4},{3,5},{0,6},{1,7},{5,0},{4,1},{7,2},{6,3},{10,12},{11,13},{8... | collective-permute-start | bytes 393224 | tf_op jit(solution)/shard_map/ppermute | solution.py:181
  3.6 5.0 %collective-permute-start = (bf16[2,32768]{1,0:T(2,128)(2,1)}, bf16[2,32768]{1,0:T(2,128)(2,1)S(1)}, u32[]{:S(2)}, u32[]{:S(2)}) collective-permute-start(bf16[2,32768]{1,0:T(2,128)(2,1)} %bitcast.28), channel_id=1, source_target_pairs={{1,4},{0,5},{3,6},{2,7},{6,0},{7,1},{4,2},{5,3},{9,12},{8,13},{11,... | collective-permute-start | bytes 393224 | tf_op jit(solution)/shard_map/ppermute | solution.py:181
  9.5 4.8 %collective-permute-start.3 = (bf16[512,128]{1,0:T(8,128)(2,1)S(1)}, bf16[512,128]{1,0:T(8,128)(2,1)S(1)}, u32[]{:S(2)}, u32[]{:S(2)}) collective-permute-start(bf16[512,128]{1,0:T(8,128)(2,1)S(1)} %get-tuple-element.18), channel_id=1, source_target_pairs={{4,2},{5,3},{6,0},{7,1},{0,28},{1,29},{2,30},{3,31},{12,10},{13,11... | collective-permute-start | bytes 393224 | tf_op jit(solution)/shard_map/ppermute | solution.py:181
  11.3 4.7 %collective-permute-start.4 = (bf16[512,128]{1,0:T(8,128)(2,1)S(1)}, bf16[512,128]{1,0:T(8,128)(2,1)S(1)}, u32[]{:S(2)}, u32[]{:S(2)}) collective-permute-start(bf16[512,128]{1,0:T(8,128)(2,1)S(1)} %get-tuple-element.19), channel_id=1, source_target_pairs={{4,1},{5,0},{6,3},{7,2},{0,6},{1,7},{2,4},{3,5},{12,9},{13,8},{14,... | collective-permute-start | bytes 393224 | tf_op jit(solution)/shard_map/ppermute | solution.py:181
  12.9 4.4 %collective-permute-start.5 = (bf16[512,128]{1,0:T(8,128)(2,1)S(1)}, bf16[512,128]{1,0:T(8,128)(2,1)S(1)}, u32[]{:S(2)}, u32[]{:S(2)}) collective-permute-start(bf16[512,128]{1,0:T(8,128)(2,1)S(1)} %get-tuple-element.20), channel_id=1, source_target_pairs={{4,24},{5,25},{6,26},{7,27},{0,5},{1,4},{2,7},{3,6},{12,0},{13,1},... | collective-permute-start | bytes 393224 | tf_op jit(solution)/shard_map/ppermute | solution.py:181

commit v7 on v6

--- a/solution.py
+++ b/solution.py
@@ -81,7 +81,7 @@
 
 
 def worker(k, kpoints):
-    return k + 1 - 2 * parity(k, kpoints) if kpoints % 8 == 0 else k
+    return k ^ (k // 2 != 0) if kpoints % 8 == 0 else k
 
 
 def split_parts(ref, scratch, rows):

time: 18.2 us -> 18.3 us (level)
  the two profiles are of different devices: /device:TPU:1 before, /device:TPU:0 now
where the time goes in v7:
time: 18.3 us; the launch traced here: 18.1 us
  starting transfers between devices  9.5 us (52%)
  waiting for transfers between devices  5.57 us (30%)
  Pallas kernels  3.03 us (17%)
    ppermute x6, starting transfers between devices, moved(): return lax.ppermute(value, ('ka', 'ba'), pairs)  9.5 us
    ppermute x6, waiting for transfers between devices, moved(): return lax.ppermute(value, ('ka', 'ba'), pairs)  5.57 us
    pallas_call x1, Pallas kernels, per_device(): pl.pallas_call(lambda *refs: setup_kernel(lay, steps, *refs), out_shape=[...  1.4 us
    pallas_call x1, Pallas kernels, per_device(): pl.pallas_call(lambda *refs: exchange_kernel(rows, slots, *refs), out_sha...  0.88 us
    pallas_call x1, Pallas kernels, per_device(): pl.pallas_call(lambda *refs: sum_kernel(rows, *refs), out_shape=shape(2 *...  0.75 us
  transfers between devices with their start and end apart: 6, of which 5 were waited for; matrix products, arithmetic and copies ran while one was open for 0% of the time, Pallas kernels for 8%

profile of v7, /device:TPU:0, one launch (start us, length us, event | category | flops | bytes accessed | tf_op | source)
XLA Modules:
  0.0 18.1 jit_solution(10215841396885587785)
XLA Ops:
  0.0 0.0 copy-start
  0.0 2.5 %collective-permute-start.2 = (bf16[2,32768]{1,0:T(2,128)(2,1)}, bf16[2,32768]{1,0:T(2,128)(2,1)S(1)}, u32[]{:S(2)}, u32[]{:S(2)}) collective-permute-start(bf16[2,32768]{1,0:T(2,128)(2,1)} %bitcast.26), channel_id=1, source_target_pairs={{24,0},{25,1},{26,2},{27,3},{28,4},{29,5},{30,6},{31,7},{0,12},{1,... | collective-permute-start | bytes 393224 | tf_op jit(solution)/shard_map/ppermute | solution.py:181
  2.5 1.5 %collective-permute-start.1 = (bf16[2,32768]{1,0:T(2,128)(2,1)}, bf16[2,32768]{1,0:T(2,128)(2,1)S(1)}, u32[]{:S(2)}, u32[]{:S(2)}) collective-permute-start(bf16[2,32768]{1,0:T(2,128)(2,1)} %bitcast.27), channel_id=1, source_target_pairs={{2,0},{3,1},{0,2},{1,3},{5,4},{4,5},{7,6},{6,7},{10,12},{11,13},{8... | collective-permute-start | bytes 393224 | tf_op jit(solution)/shard_map/ppermute | solution.py:181
  4.0 1.5 %collective-permute-start = (bf16[2,32768]{1,0:T(2,128)(2,1)}, bf16[2,32768]{1,0:T(2,128)(2,1)S(1)}, u32[]{:S(2)}, u32[]{:S(2)}) collective-permute-start(bf16[2,32768]{1,0:T(2,128)(2,1)} %bitcast.28), channel_id=1, source_target_pairs={{1,0},{0,1},{3,2},{2,3},{6,4},{7,5},{4,6},{5,7},{9,12},{8,13},{11,... | collective-permute-start | bytes 393224 | tf_op jit(solution)/shard_map/ppermute | solution.py:181
  5.5 0.0 copy-done
  5.5 1.4 %setup.1 = (bf16[512,256]{1,0:T(8,128)(2,1)S(1)}, bf16[256,256]{1,0:T(8,128)(2,1)S(1)}, bf16[256,256]{1,0:T(8,128)(2,1)S(1)}, f32[512,128]{1,0:T(8,128)S(1)}, f32[256,128]{1,0:T(8,128)S(1)}) custom-call(s32[3,8]{1,0:T(4,128)S(1)} %bitcast.25), custom_call_target="tpu_custom_call" | custom-call | tf_op jit(solution)/shard_map/setup/pallas_call | solution.py:191
  6.9 1.9 %collective-permute-done.2 = bf16[2,32768]{1,0:T(2,128)(2,1)S(1)} collective-permute-done((bf16[2,32768]{1,0:T(2,128)(2,1)}, bf16[2,32768]{1,0:T(2,128)(2,1)S(1)}, u32[]{:S(2)}, u32[]{:S(2)}) %collective-permute-start.2) | collective-permute-done | bytes 131104 | tf_op jit(solution)/shard_map/ppermute | solution.py:181
  8.8 0.0 collective-permute-done.1
  8.8 0.4 %collective-permute-done = bf16[2,32768]{1,0:T(2,128)(2,1)S(1)} collective-permute-done((bf16[2,32768]{1,0:T(2,128)(2,1)}, bf16[2,32768]{1,0:T(2,128)(2,1)S(1)}, u32[]{:S(2)}, u32[]{:S(2)}) %collective-permute-start) | collective-permute-done | bytes 131104 | tf_op jit(solution)/shard_map/ppermute | solution.py:181
  9.2 0.9 %exchange.1 = (bf16[512,128]{1,0:T(8,128)(2,1)S(1)}, bf16[512,128]{1,0:T(8,128)(2,1)S(1)}, bf16[512,128]{1,0:T(8,128)(2,1)S(1)}) custom-call(bf16[512,128]{1,0:T(8,128)(2,1)S(1)} %bitcast.24, bf16[512,128]{1,0:T(8,128)(2,1)S(1)} %bitcast.23, bf16[512,128]{1,0:T(8,128)(2,1)S(1)} %bitcast.22, bf16[512,256]{1,0:T(8,128)(2,1)S(1)} %get-tuple-element.13.refs_3_, ...), custom_call_target="tpu_custom_call" | custom-call | tf_op jit(solution)/shard_map/exchange/pallas_call | solution.py:206
  10.1 1.2 %collective-permute-start.3 = (bf16[512,128]{1,0:T(8,128)(2,1)S(1)}, bf16[512,128]{1,0:T(8,128)(2,1)S(1)}, u32[]{:S(2)}, u32[]{:S(2)}) collective-permute-start(bf16[512,128]{1,0:T(8,128)(2,1)S(1)} %get-tuple-element.18), channel_id=1, source_target_pairs={{0,2},{1,3},{2,0},{3,1},{4,28},{5,29},{6,30},{7,31},{12,10},{13,11... | collective-permute-start | bytes 393224 | tf_op jit(solution)/shard_map/ppermute | solution.py:181
  11.2 1.7 %collective-permute-start.4 = (bf16[512,128]{1,0:T(8,128)(2,1)S(1)}, bf16[512,128]{1,0:T(8,128)(2,1)S(1)}, u32[]{:S(2)}, u32[]{:S(2)}) collective-permute-start(bf16[512,128]{1,0:T(8,128)(2,1)S(1)} %get-tuple-element.19), channel_id=1, source_target_pairs={{0,1},{1,0},{2,3},{3,2},{4,6},{5,7},{6,4},{7,5},{12,9},{13,8},{14,... | collective-permute-start | bytes 393224 | tf_op jit(solution)/shard_map/ppermute | solution.py:181
  13.0 1.1 %collective-permute-start.5 = (bf16[512,128]{1,0:T(8,128)(2,1)S(1)}, bf16[512,128]{1,0:T(8,128)(2,1)S(1)}, u32[]{:S(2)}, u32[]{:S(2)}) collective-permute-start(bf16[512,128]{1,0:T(8,128)(2,1)S(1)} %get-tuple-element.20), channel_id=1, source_target_pairs={{0,24},{1,25},{2,26},{3,27},{4,5},{5,4},{6,7},{7,6},{12,0},{13,1},... | collective-permute-start | bytes 393224 | tf_op jit(solution)/shard_map/ppermute | solution.py:181
  14.1 1.3 %collective-permute-done.3.refs_0_ = bf16[512,128]{1,0:T(8,128)(2,1)S(1)} collective-permute-done((bf16[512,128]{1,0:T(8,128)(2,1)S(1)}, bf16[512,128]{1,0:T(8,128)(2,1)S(1)}, u32[]{:S(2)}, u32[]{:S(2)}) %collective-permute-start.3) | collective-permute-done | bytes 131104 | tf_op jit(solution)/shard_map/ppermute | solution.py:181
  15.4 1.0 %collective-permute-done.4.refs_1_ = bf16[512,128]{1,0:T(8,128)(2,1)S(1)} collective-permute-done((bf16[512,128]{1,0:T(8,128)(2,1)S(1)}, bf16[512,128]{1,0:T(8,128)(2,1)S(1)}, u32[]{:S(2)}, u32[]{:S(2)}) %collective-permute-start.4) | collective-permute-done | bytes 131104 | tf_op jit(solution)/shard_map/ppermute | solution.py:181
  16.4 1.0 %collective-permute-done.5.refs_2_ = bf16[512,128]{1,0:T(8,128)(2,1)S(1)} collective-permute-done((bf16[512,128]{1,0:T(8,128)(2,1)S(1)}, bf16[512,128]{1,0:T(8,128)(2,1)S(1)}, u32[]{:S(2)}, u32[]{:S(2)}) %collective-permute-start.5) | collective-permute-done | bytes 131104 | tf_op jit(solution)/shard_map/ppermute | solution.py:181
  17.4 0.7 %total.1 = f32[512,128]{1,0:T(8,128)} custom-call(bf16[512,128]{1,0:T(8,128)(2,1)S(1)} %collective-permute-done.3.refs_0_, bf16[512,128]{1,0:T(8,128)(2,1)S(1)} %collective-permute-done.4.refs_1_, bf16[512,128]{1,0:T(8,128)(2,1)S(1)} %collective-permute-done.5.refs_2_), custom_call_target="tpu_custom_call" | custom-call | tf_op jit(solution)/shard_map/total/pallas_call | solution.py:216
Async XLA Ops:
  0.0 5.5 %copy-start = (s32[8,3]{0,1:T(4,128)S(1)}, s32[8,3]{0,1:T(4,128)}, u32[]{:S(2)}) copy-start(s32[8,3]{0,1:T(4,128)} %param.3) | copy-start | bytes 292
  0.0 8.8 %collective-permute-start.2 = (bf16[2,32768]{1,0:T(2,128)(2,1)}, bf16[2,32768]{1,0:T(2,128)(2,1)S(1)}, u32[]{:S(2)}, u32[]{:S(2)}) collective-permute-start(bf16[2,32768]{1,0:T(2,128)(2,1)} %bitcast.26), channel_id=1, source_target_pairs={{24,0},{25,1},{26,2},{27,3},{28,4},{29,5},{30,6},{31,7},{0,12},{1,... | collective-permute-start | bytes 393224 | tf_op jit(solution)/shard_map/ppermute | solution.py:181
  2.5 6.3 %collective-permute-start.1 = (bf16[2,32768]{1,0:T(2,128)(2,1)}, bf16[2,32768]{1,0:T(2,128)(2,1)S(1)}, u32[]{:S(2)}, u32[]{:S(2)}) collective-permute-start(bf16[2,32768]{1,0:T(2,128)(2,1)} %bitcast.27), channel_id=1, source_target_pairs={{2,0},{3,1},{0,2},{1,3},{5,4},{4,5},{7,6},{6,7},{10,12},{11,13},{8... | collective-permute-start | bytes 393224 | tf_op jit(solution)/shard_map/ppermute | solution.py:181
  4.0 5.2 %collective-permute-start = (bf16[2,32768]{1,0:T(2,128)(2,1)}, bf16[2,32768]{1,0:T(2,128)(2,1)S(1)}, u32[]{:S(2)}, u32[]{:S(2)}) collective-permute-start(bf16[2,32768]{1,0:T(2,128)(2,1)} %bitcast.28), channel_id=1, source_target_pairs={{1,0},{0,1},{3,2},{2,3},{6,4},{7,5},{4,6},{5,7},{9,12},{8,13},{11,... | collective-permute-start | bytes 393224 | tf_op jit(solution)/shard_map/ppermute | solution.py:181
  10.1 5.3 %collective-permute-start.3 = (bf16[512,128]{1,0:T(8,128)(2,1)S(1)}, bf16[512,128]{1,0:T(8,128)(2,1)S(1)}, u32[]{:S(2)}, u32[]{:S(2)}) collective-permute-start(bf16[512,128]{1,0:T(8,128)(2,1)S(1)} %get-tuple-element.18), channel_id=1, source_target_pairs={{0,2},{1,3},{2,0},{3,1},{4,28},{5,29},{6,30},{7,31},{12,10},{13,11... | collective-permute-start | bytes 393224 | tf_op jit(solution)/shard_map/ppermute | solution.py:181
  11.2 5.2 %collective-permute-start.4 = (bf16[512,128]{1,0:T(8,128)(2,1)S(1)}, bf16[512,128]{1,0:T(8,128)(2,1)S(1)}, u32[]{:S(2)}, u32[]{:S(2)}) collective-permute-start(bf16[512,128]{1,0:T(8,128)(2,1)S(1)} %get-tuple-element.19), channel_id=1, source_target_pairs={{0,1},{1,0},{2,3},{3,2},{4,6},{5,7},{6,4},{7,5},{12,9},{13,8},{14,... | collective-permute-start | bytes 393224 | tf_op jit(solution)/shard_map/ppermute | solution.py:181
  13.0 4.4 %collective-permute-start.5 = (bf16[512,128]{1,0:T(8,128)(2,1)S(1)}, bf16[512,128]{1,0:T(8,128)(2,1)S(1)}, u32[]{:S(2)}, u32[]{:S(2)}) collective-permute-start(bf16[512,128]{1,0:T(8,128)(2,1)S(1)} %get-tuple-element.20), channel_id=1, source_target_pairs={{0,24},{1,25},{2,26},{3,27},{4,5},{5,4},{6,7},{7,6},{12,0},{13,1},... | collective-permute-start | bytes 393224 | tf_op jit(solution)/shard_map/ppermute | solution.py:181

commit v8 on v6

--- a/solution.py
+++ b/solution.py
@@ -146,12 +146,22 @@
 
 
 def sum_kernel(rows, *refs):
-    out_ref = refs[-1]
-    total = refs[0][...].astype(jnp.float32)
-    for ref in refs[1:-1]:
-        total = total + ref[...].astype(jnp.float32)
-    out_ref[pl.ds(0, rows, 2), :] = total[:rows]
-    out_ref[pl.ds(1, rows, 2), :] = total[rows:]
+    in_refs, out_ref, total_ref, sems = refs[:-3], refs[-3], refs[-2], refs[-1]
+    count = sems.shape[0]
+    size = rows // count
+    copies = []
+    for piece in range(count):
+        for part in range(2):
+            here = slice(part * rows + piece * size, part * rows + (piece + 1) * size)
+            total = in_refs[0][here].astype(jnp.float32)
+            for ref in in_refs[1:]:
+                total = total + ref[here].astype(jnp.float32)
+            total_ref[pl.ds(2 * piece * size + part, size, 2), :] = total
+        span = pl.ds(2 * piece * size, 2 * size)
+        copies.append(pltpu.make_async_copy(total_ref.at[span], out_ref.at[span], sems.at[piece]))
+        copies[-1].start()
+    for copy in copies:
+        copy.wait()
 
 
 def in_vmem(count):
@@ -217,7 +227,8 @@
         lambda *refs: sum_kernel(rows, *refs),
         out_shape=shape(2 * rows, LANES, dtype=jnp.float32),
         in_specs=in_vmem(matches + 1),
-        out_specs=in_vmem(1)[0],
+        out_specs=pl.BlockSpec(memory_space=pl.ANY),
+        scratch_shapes=[pltpu.VMEM((2 * rows, LANES), jnp.float32), pltpu.SemaphoreType.DMA((4,))],
         compiler_params=limits,
         name="total",
     )(*returned)

time: 18.2 us -> 18.2 us (level)
  no operation moved by 1% of the time
where the time goes in v8:
time: 18.2 us; the launch traced here: 18.1 us
  starting transfers between devices  8.49 us (47%)
  waiting for transfers between devices  6.53 us (36%)
  Pallas kernels  3.02 us (17%)
    ppermute x6, starting transfers between devices, moved(): return lax.ppermute(value, ('ka', 'ba'), pairs)  8.49 us
    ppermute x6, waiting for transfers between devices, moved(): return lax.ppermute(value, ('ka', 'ba'), pairs)  6.53 us
    pallas_call x1, Pallas kernels, per_device(): pl.pallas_call(lambda *refs: setup_kernel(lay, steps, *refs), out_shape=[...  1.4 us
    pallas_call x1, Pallas kernels, per_device(): pl.pallas_call(lambda *refs: exchange_kernel(rows, slots, *refs), out_sha...  0.88 us
    pallas_call x1, Pallas kernels, per_device(): pl.pallas_call(lambda *refs: sum_kernel(rows, *refs), out_shape=shape(2 *...  0.74 us
  transfers between devices with their start and end apart: 6, of which 5 were waited for; matrix products, arithmetic and copies ran while one was open for 0% of the time, Pallas kernels for 8%

profile of v8, /device:TPU:1, one launch (start us, length us, event | category | flops | bytes accessed | tf_op | source)
XLA Modules:
  0.0 18.1 jit_solution(3013077017160212009)
XLA Ops:
  0.0 0.0 copy-start
  0.0 2.7 %collective-permute-start.2 = (bf16[2,32768]{1,0:T(2,128)(2,1)}, bf16[2,32768]{1,0:T(2,128)(2,1)S(1)}, u32[]{:S(2)}, u32[]{:S(2)}) collective-permute-start(bf16[2,32768]{1,0:T(2,128)(2,1)} %bitcast.26), channel_id=1, source_target_pairs={{24,4},{25,5},{26,6},{27,7},{28,0},{29,1},{30,2},{31,3},{0,12},{1,... | collective-permute-start | bytes 393224 | tf_op jit(solution)/shard_map/ppermute | solution.py:191
  2.7 0.9 %collective-permute-start.1 = (bf16[2,32768]{1,0:T(2,128)(2,1)}, bf16[2,32768]{1,0:T(2,128)(2,1)S(1)}, u32[]{:S(2)}, u32[]{:S(2)}) collective-permute-start(bf16[2,32768]{1,0:T(2,128)(2,1)} %bitcast.27), channel_id=1, source_target_pairs={{2,4},{3,5},{0,6},{1,7},{5,0},{4,1},{7,2},{6,3},{10,12},{11,13},{8... | collective-permute-start | bytes 393224 | tf_op jit(solution)/shard_map/ppermute | solution.py:191
  3.6 0.8 %collective-permute-start = (bf16[2,32768]{1,0:T(2,128)(2,1)}, bf16[2,32768]{1,0:T(2,128)(2,1)S(1)}, u32[]{:S(2)}, u32[]{:S(2)}) collective-permute-start(bf16[2,32768]{1,0:T(2,128)(2,1)} %bitcast.28), channel_id=1, source_target_pairs={{1,4},{0,5},{3,6},{2,7},{6,0},{7,1},{4,2},{5,3},{9,12},{8,13},{11,... | collective-permute-start | bytes 393224 | tf_op jit(solution)/shard_map/ppermute | solution.py:191
  4.4 0.0 copy-done
  4.4 1.4 %setup.1 = (bf16[512,256]{1,0:T(8,128)(2,1)S(1)}, bf16[256,256]{1,0:T(8,128)(2,1)S(1)}, bf16[256,256]{1,0:T(8,128)(2,1)S(1)}, f32[512,128]{1,0:T(8,128)S(1)}, f32[256,128]{1,0:T(8,128)S(1)}) custom-call(s32[3,8]{1,0:T(4,128)S(1)} %bitcast.25), custom_call_target="tpu_custom_call" | custom-call | tf_op jit(solution)/shard_map/setup/pallas_call | solution.py:201
  5.8 2.3 %collective-permute-done.2 = bf16[2,32768]{1,0:T(2,128)(2,1)S(1)} collective-permute-done((bf16[2,32768]{1,0:T(2,128)(2,1)}, bf16[2,32768]{1,0:T(2,128)(2,1)S(1)}, u32[]{:S(2)}, u32[]{:S(2)}) %collective-permute-start.2) | collective-permute-done | bytes 131104 | tf_op jit(solution)/shard_map/ppermute | solution.py:191
  8.1 0.0 collective-permute-done.1
  8.1 0.5 %collective-permute-done = bf16[2,32768]{1,0:T(2,128)(2,1)S(1)} collective-permute-done((bf16[2,32768]{1,0:T(2,128)(2,1)}, bf16[2,32768]{1,0:T(2,128)(2,1)S(1)}, u32[]{:S(2)}, u32[]{:S(2)}) %collective-permute-start) | collective-permute-done | bytes 131104 | tf_op jit(solution)/shard_map/ppermute | solution.py:191
  8.6 0.9 %exchange.1 = (bf16[512,128]{1,0:T(8,128)(2,1)S(1)}, bf16[512,128]{1,0:T(8,128)(2,1)S(1)}, bf16[512,128]{1,0:T(8,128)(2,1)S(1)}) custom-call(bf16[512,128]{1,0:T(8,128)(2,1)S(1)} %bitcast.24, bf16[512,128]{1,0:T(8,128)(2,1)S(1)} %bitcast.23, bf16[512,128]{1,0:T(8,128)(2,1)S(1)} %bitcast.22, bf16[512,256]{1,0:T(8,128)(2,1)S(1)} %get-tuple-element.13.refs_3_, ...), custom_call_target="tpu_custom_call" | custom-call | tf_op jit(solution)/shard_map/exchange/pallas_call | solution.py:216
  9.5 1.8 %collective-permute-start.3 = (bf16[512,128]{1,0:T(8,128)(2,1)S(1)}, bf16[512,128]{1,0:T(8,128)(2,1)S(1)}, u32[]{:S(2)}, u32[]{:S(2)}) collective-permute-start(bf16[512,128]{1,0:T(8,128)(2,1)S(1)} %get-tuple-element.18), channel_id=1, source_target_pairs={{4,2},{5,3},{6,0},{7,1},{0,28},{1,29},{2,30},{3,31},{12,10},{13,11... | collective-permute-start | bytes 393224 | tf_op jit(solution)/shard_map/ppermute | solution.py:191
  11.3 1.6 %collective-permute-start.4 = (bf16[512,128]{1,0:T(8,128)(2,1)S(1)}, bf16[512,128]{1,0:T(8,128)(2,1)S(1)}, u32[]{:S(2)}, u32[]{:S(2)}) collective-permute-start(bf16[512,128]{1,0:T(8,128)(2,1)S(1)} %get-tuple-element.19), channel_id=1, source_target_pairs={{4,1},{5,0},{6,3},{7,2},{0,6},{1,7},{2,4},{3,5},{12,9},{13,8},{14,... | collective-permute-start | bytes 393224 | tf_op jit(solution)/shard_map/ppermute | solution.py:191
  12.9 0.6 %collective-permute-start.5 = (bf16[512,128]{1,0:T(8,128)(2,1)S(1)}, bf16[512,128]{1,0:T(8,128)(2,1)S(1)}, u32[]{:S(2)}, u32[]{:S(2)}) collective-permute-start(bf16[512,128]{1,0:T(8,128)(2,1)S(1)} %get-tuple-element.20), channel_id=1, source_target_pairs={{4,24},{5,25},{6,26},{7,27},{0,5},{1,4},{2,7},{3,6},{12,0},{13,1},... | collective-permute-start | bytes 393224 | tf_op jit(solution)/shard_map/ppermute | solution.py:191
  13.6 0.8 %collective-permute-done.3.refs_0_ = bf16[512,128]{1,0:T(8,128)(2,1)S(1)} collective-permute-done((bf16[512,128]{1,0:T(8,128)(2,1)S(1)}, bf16[512,128]{1,0:T(8,128)(2,1)S(1)}, u32[]{:S(2)}, u32[]{:S(2)}) %collective-permute-start.3) | collective-permute-done | bytes 131104 | tf_op jit(solution)/shard_map/ppermute | solution.py:191
  14.3 1.7 %collective-permute-done.4.refs_1_ = bf16[512,128]{1,0:T(8,128)(2,1)S(1)} collective-permute-done((bf16[512,128]{1,0:T(8,128)(2,1)S(1)}, bf16[512,128]{1,0:T(8,128)(2,1)S(1)}, u32[]{:S(2)}, u32[]{:S(2)}) %collective-permute-start.4) | collective-permute-done | bytes 131104 | tf_op jit(solution)/shard_map/ppermute | solution.py:191
  16.0 1.3 %collective-permute-done.5.refs_2_ = bf16[512,128]{1,0:T(8,128)(2,1)S(1)} collective-permute-done((bf16[512,128]{1,0:T(8,128)(2,1)S(1)}, bf16[512,128]{1,0:T(8,128)(2,1)S(1)}, u32[]{:S(2)}, u32[]{:S(2)}) %collective-permute-start.5) | collective-permute-done | bytes 131104 | tf_op jit(solution)/shard_map/ppermute | solution.py:191
  17.3 0.7 %total.1 = f32[512,128]{1,0:T(8,128)} custom-call(bf16[512,128]{1,0:T(8,128)(2,1)S(1)} %collective-permute-done.3.refs_0_, bf16[512,128]{1,0:T(8,128)(2,1)S(1)} %collective-permute-done.4.refs_1_, bf16[512,128]{1,0:T(8,128)(2,1)S(1)} %collective-permute-done.5.refs_2_), custom_call_target="tpu_custom_call" | custom-call | tf_op jit(solution)/shard_map/total/pallas_call | solution.py:226
Async XLA Ops:
  0.0 4.4 %copy-start = (s32[8,3]{0,1:T(4,128)S(1)}, s32[8,3]{0,1:T(4,128)}, u32[]{:S(2)}) copy-start(s32[8,3]{0,1:T(4,128)} %param.3) | copy-start | bytes 292
  0.0 8.1 %collective-permute-start.2 = (bf16[2,32768]{1,0:T(2,128)(2,1)}, bf16[2,32768]{1,0:T(2,128)(2,1)S(1)}, u32[]{:S(2)}, u32[]{:S(2)}) collective-permute-start(bf16[2,32768]{1,0:T(2,128)(2,1)} %bitcast.26), channel_id=1, source_target_pairs={{24,4},{25,5},{26,6},{27,7},{28,0},{29,1},{30,2},{31,3},{0,12},{1,... | collective-permute-start | bytes 393224 | tf_op jit(solution)/shard_map/ppermute | solution.py:191
  2.7 5.4 %collective-permute-start.1 = (bf16[2,32768]{1,0:T(2,128)(2,1)}, bf16[2,32768]{1,0:T(2,128)(2,1)S(1)}, u32[]{:S(2)}, u32[]{:S(2)}) collective-permute-start(bf16[2,32768]{1,0:T(2,128)(2,1)} %bitcast.27), channel_id=1, source_target_pairs={{2,4},{3,5},{0,6},{1,7},{5,0},{4,1},{7,2},{6,3},{10,12},{11,13},{8... | collective-permute-start | bytes 393224 | tf_op jit(solution)/shard_map/ppermute | solution.py:191
  3.6 5.0 %collective-permute-start = (bf16[2,32768]{1,0:T(2,128)(2,1)}, bf16[2,32768]{1,0:T(2,128)(2,1)S(1)}, u32[]{:S(2)}, u32[]{:S(2)}) collective-permute-start(bf16[2,32768]{1,0:T(2,128)(2,1)} %bitcast.28), channel_id=1, source_target_pairs={{1,4},{0,5},{3,6},{2,7},{6,0},{7,1},{4,2},{5,3},{9,12},{8,13},{11,... | collective-permute-start | bytes 393224 | tf_op jit(solution)/shard_map/ppermute | solution.py:191
  9.5 4.8 %collective-permute-start.3 = (bf16[512,128]{1,0:T(8,128)(2,1)S(1)}, bf16[512,128]{1,0:T(8,128)(2,1)S(1)}, u32[]{:S(2)}, u32[]{:S(2)}) collective-permute-start(bf16[512,128]{1,0:T(8,128)(2,1)S(1)} %get-tuple-element.18), channel_id=1, source_target_pairs={{4,2},{5,3},{6,0},{7,1},{0,28},{1,29},{2,30},{3,31},{12,10},{13,11... | collective-permute-start | bytes 393224 | tf_op jit(solution)/shard_map/ppermute | solution.py:191
  11.3 4.7 %collective-permute-start.4 = (bf16[512,128]{1,0:T(8,128)(2,1)S(1)}, bf16[512,128]{1,0:T(8,128)(2,1)S(1)}, u32[]{:S(2)}, u32[]{:S(2)}) collective-permute-start(bf16[512,128]{1,0:T(8,128)(2,1)S(1)} %get-tuple-element.19), channel_id=1, source_target_pairs={{4,1},{5,0},{6,3},{7,2},{0,6},{1,7},{2,4},{3,5},{12,9},{13,8},{14,... | collective-permute-start | bytes 393224 | tf_op jit(solution)/shard_map/ppermute | solution.py:191
  12.9 4.4 %collective-permute-start.5 = (bf16[512,128]{1,0:T(8,128)(2,1)S(1)}, bf16[512,128]{1,0:T(8,128)(2,1)S(1)}, u32[]{:S(2)}, u32[]{:S(2)}) collective-permute-start(bf16[512,128]{1,0:T(8,128)(2,1)S(1)} %get-tuple-element.20), channel_id=1, source_target_pairs={{4,24},{5,25},{6,26},{7,27},{0,5},{1,4},{2,7},{3,6},{12,0},{13,1},... | collective-permute-start | bytes 393224 | tf_op jit(solution)/shard_map/ppermute | solution.py:191

commit v9 on v6

--- a/solution.py
+++ b/solution.py
@@ -182,7 +182,7 @@
 
     straight = list(range(matches + 1))
     arrivals = [moved(own, step, (straight, straight), False) for step in straight]
-    slots = (straight[:matches][::-1] + straight[matches:], straight[matches:] + straight[:matches])
+    slots = (straight[1:] + straight[:1], straight[:matches][::-1] + straight[matches:])
 
     def shape(*dims, dtype=jnp.bfloat16):
         return jax.ShapeDtypeStruct(dims, dtype)

time: 18.2 us -> 18.2 us (level)
  starting transfers between devices: 8.49 us -> 8.1 us
  waiting for transfers between devices: 6.53 us -> 6.91 us
    ppermute x6, waiting for transfers between devices: 6.53 us -> 6.91 us  [moved(): return lax.ppermute(value, ('ka', 'ba'), pairs)]
    ppermute x6, starting transfers between devices: 8.49 us -> 8.1 us  [moved(): return lax.ppermute(value, ('ka', 'ba'), pairs)]
where the time goes in v9:
time: 18.2 us; the launch traced here: 18.1 us
  starting transfers between devices  8.1 us (45%)
  waiting for transfers between devices  6.91 us (38%)
  Pallas kernels  3.03 us (17%)
    ppermute x6, starting transfers between devices, moved(): return lax.ppermute(value, ('ka', 'ba'), pairs)  8.1 us
    ppermute x6, waiting for transfers between devices, moved(): return lax.ppermute(value, ('ka', 'ba'), pairs)  6.91 us
    pallas_call x1, Pallas kernels, per_device(): pl.pallas_call(lambda *refs: setup_kernel(lay, steps, *refs), out_shape=[...  1.4 us
    pallas_call x1, Pallas kernels, per_device(): pl.pallas_call(lambda *refs: exchange_kernel(rows, slots, *refs), out_sha...  0.88 us
    pallas_call x1, Pallas kernels, per_device(): pl.pallas_call(lambda *refs: sum_kernel(rows, *refs), out_shape=shape(2 *...  0.75 us
  transfers between devices with their start and end apart: 6, of which 5 were waited for; matrix products, arithmetic and copies ran while one was open for 0% of the time, Pallas kernels for 8%

profile of v9, /device:TPU:1, one launch (start us, length us, event | category | flops | bytes accessed | tf_op | source)
XLA Modules:
  0.0 18.1 jit_solution(13336296688582492454)
XLA Ops:
  0.0 0.0 copy-start
  0.0 2.7 %collective-permute-start.2 = (bf16[2,32768]{1,0:T(2,128)(2,1)}, bf16[2,32768]{1,0:T(2,128)(2,1)S(1)}, u32[]{:S(2)}, u32[]{:S(2)}) collective-permute-start(bf16[2,32768]{1,0:T(2,128)(2,1)} %bitcast.26), channel_id=1, source_target_pairs={{24,4},{25,5},{26,6},{27,7},{28,0},{29,1},{30,2},{31,3},{0,12},{1,... | collective-permute-start | bytes 393224 | tf_op jit(solution)/shard_map/ppermute | solution.py:181
  2.7 0.9 %collective-permute-start.1 = (bf16[2,32768]{1,0:T(2,128)(2,1)}, bf16[2,32768]{1,0:T(2,128)(2,1)S(1)}, u32[]{:S(2)}, u32[]{:S(2)}) collective-permute-start(bf16[2,32768]{1,0:T(2,128)(2,1)} %bitcast.27), channel_id=1, source_target_pairs={{2,4},{3,5},{0,6},{1,7},{5,0},{4,1},{7,2},{6,3},{10,12},{11,13},{8... | collective-permute-start | bytes 393224 | tf_op jit(solution)/shard_map/ppermute | solution.py:181
  3.6 0.8 %collective-permute-start = (bf16[2,32768]{1,0:T(2,128)(2,1)}, bf16[2,32768]{1,0:T(2,128)(2,1)S(1)}, u32[]{:S(2)}, u32[]{:S(2)}) collective-permute-start(bf16[2,32768]{1,0:T(2,128)(2,1)} %bitcast.28), channel_id=1, source_target_pairs={{1,4},{0,5},{3,6},{2,7},{6,0},{7,1},{4,2},{5,3},{9,12},{8,13},{11,... | collective-permute-start | bytes 393224 | tf_op jit(solution)/shard_map/ppermute | solution.py:181
  4.4 0.0 copy-done
  4.4 1.4 %setup.1 = (bf16[512,256]{1,0:T(8,128)(2,1)S(1)}, bf16[256,256]{1,0:T(8,128)(2,1)S(1)}, bf16[256,256]{1,0:T(8,128)(2,1)S(1)}, f32[512,128]{1,0:T(8,128)S(1)}, f32[256,128]{1,0:T(8,128)S(1)}) custom-call(s32[3,8]{1,0:T(4,128)S(1)} %bitcast.25), custom_call_target="tpu_custom_call" | custom-call | tf_op jit(solution)/shard_map/setup/pallas_call | solution.py:191
  5.8 2.3 %collective-permute-done.2 = bf16[2,32768]{1,0:T(2,128)(2,1)S(1)} collective-permute-done((bf16[2,32768]{1,0:T(2,128)(2,1)}, bf16[2,32768]{1,0:T(2,128)(2,1)S(1)}, u32[]{:S(2)}, u32[]{:S(2)}) %collective-permute-start.2) | collective-permute-done | bytes 131104 | tf_op jit(solution)/shard_map/ppermute | solution.py:181
  8.1 0.0 collective-permute-done.1
  8.1 0.5 %collective-permute-done = bf16[2,32768]{1,0:T(2,128)(2,1)S(1)} collective-permute-done((bf16[2,32768]{1,0:T(2,128)(2,1)}, bf16[2,32768]{1,0:T(2,128)(2,1)S(1)}, u32[]{:S(2)}, u32[]{:S(2)}) %collective-permute-start) | collective-permute-done | bytes 131104 | tf_op jit(solution)/shard_map/ppermute | solution.py:181
  8.6 0.9 %exchange.1 = (bf16[512,128]{1,0:T(8,128)(2,1)S(1)}, bf16[512,128]{1,0:T(8,128)(2,1)S(1)}, bf16[512,128]{1,0:T(8,128)(2,1)S(1)}) custom-call(bf16[512,128]{1,0:T(8,128)(2,1)S(1)} %bitcast.24, bf16[512,128]{1,0:T(8,128)(2,1)S(1)} %bitcast.23, bf16[512,128]{1,0:T(8,128)(2,1)S(1)} %bitcast.22, bf16[512,256]{1,0:T(8,128)(2,1)S(1)} %get-tuple-element.13.refs_3_, ...), custom_call_target="tpu_custom_call" | custom-call | tf_op jit(solution)/shard_map/exchange/pallas_call | solution.py:206
  9.5 1.8 %collective-permute-start.3 = (bf16[512,128]{1,0:T(8,128)(2,1)S(1)}, bf16[512,128]{1,0:T(8,128)(2,1)S(1)}, u32[]{:S(2)}, u32[]{:S(2)}) collective-permute-start(bf16[512,128]{1,0:T(8,128)(2,1)S(1)} %get-tuple-element.18), channel_id=1, source_target_pairs={{4,2},{5,3},{6,0},{7,1},{0,5},{1,4},{2,7},{3,6},{12,10},{13,11},{1... | collective-permute-start | bytes 393224 | tf_op jit(solution)/shard_map/ppermute | solution.py:181
  11.3 1.6 %collective-permute-start.4 = (bf16[512,128]{1,0:T(8,128)(2,1)S(1)}, bf16[512,128]{1,0:T(8,128)(2,1)S(1)}, u32[]{:S(2)}, u32[]{:S(2)}) collective-permute-start(bf16[512,128]{1,0:T(8,128)(2,1)S(1)} %get-tuple-element.19), channel_id=1, source_target_pairs={{4,24},{5,25},{6,26},{7,27},{0,6},{1,7},{2,4},{3,5},{12,0},{13,1},... | collective-permute-start | bytes 393224 | tf_op jit(solution)/shard_map/ppermute | solution.py:181
  12.9 0.2 %collective-permute-start.5 = (bf16[512,128]{1,0:T(8,128)(2,1)S(1)}, bf16[512,128]{1,0:T(8,128)(2,1)S(1)}, u32[]{:S(2)}, u32[]{:S(2)}) collective-permute-start(bf16[512,128]{1,0:T(8,128)(2,1)S(1)} %get-tuple-element.20), channel_id=1, source_target_pairs={{4,1},{5,0},{6,3},{7,2},{0,28},{1,29},{2,30},{3,31},{12,9},{13,8},... | collective-permute-start | bytes 393224 | tf_op jit(solution)/shard_map/ppermute | solution.py:181
  13.2 1.2 %collective-permute-done.3.refs_0_ = bf16[512,128]{1,0:T(8,128)(2,1)S(1)} collective-permute-done((bf16[512,128]{1,0:T(8,128)(2,1)S(1)}, bf16[512,128]{1,0:T(8,128)(2,1)S(1)}, u32[]{:S(2)}, u32[]{:S(2)}) %collective-permute-start.3) | collective-permute-done | bytes 131104 | tf_op jit(solution)/shard_map/ppermute | solution.py:181
  14.4 1.6 %collective-permute-done.4.refs_1_ = bf16[512,128]{1,0:T(8,128)(2,1)S(1)} collective-permute-done((bf16[512,128]{1,0:T(8,128)(2,1)S(1)}, bf16[512,128]{1,0:T(8,128)(2,1)S(1)}, u32[]{:S(2)}, u32[]{:S(2)}) %collective-permute-start.4) | collective-permute-done | bytes 131104 | tf_op jit(solution)/shard_map/ppermute | solution.py:181
  16.0 1.3 %collective-permute-done.5.refs_2_ = bf16[512,128]{1,0:T(8,128)(2,1)S(1)} collective-permute-done((bf16[512,128]{1,0:T(8,128)(2,1)S(1)}, bf16[512,128]{1,0:T(8,128)(2,1)S(1)}, u32[]{:S(2)}, u32[]{:S(2)}) %collective-permute-start.5) | collective-permute-done | bytes 131104 | tf_op jit(solution)/shard_map/ppermute | solution.py:181
  17.3 0.7 %total.1 = f32[512,128]{1,0:T(8,128)} custom-call(bf16[512,128]{1,0:T(8,128)(2,1)S(1)} %collective-permute-done.3.refs_0_, bf16[512,128]{1,0:T(8,128)(2,1)S(1)} %collective-permute-done.4.refs_1_, bf16[512,128]{1,0:T(8,128)(2,1)S(1)} %collective-permute-done.5.refs_2_), custom_call_target="tpu_custom_call" | custom-call | tf_op jit(solution)/shard_map/total/pallas_call | solution.py:216
Async XLA Ops:
  0.0 4.4 %copy-start = (s32[8,3]{0,1:T(4,128)S(1)}, s32[8,3]{0,1:T(4,128)}, u32[]{:S(2)}) copy-start(s32[8,3]{0,1:T(4,128)} %param.3) | copy-start | bytes 292
  0.0 8.1 %collective-permute-start.2 = (bf16[2,32768]{1,0:T(2,128)(2,1)}, bf16[2,32768]{1,0:T(2,128)(2,1)S(1)}, u32[]{:S(2)}, u32[]{:S(2)}) collective-permute-start(bf16[2,32768]{1,0:T(2,128)(2,1)} %bitcast.26), channel_id=1, source_target_pairs={{24,4},{25,5},{26,6},{27,7},{28,0},{29,1},{30,2},{31,3},{0,12},{1,... | collective-permute-start | bytes 393224 | tf_op jit(solution)/shard_map/ppermute | solution.py:181
  2.7 5.4 %collective-permute-start.1 = (bf16[2,32768]{1,0:T(2,128)(2,1)}, bf16[2,32768]{1,0:T(2,128)(2,1)S(1)}, u32[]{:S(2)}, u32[]{:S(2)}) collective-permute-start(bf16[2,32768]{1,0:T(2,128)(2,1)} %bitcast.27), channel_id=1, source_target_pairs={{2,4},{3,5},{0,6},{1,7},{5,0},{4,1},{7,2},{6,3},{10,12},{11,13},{8... | collective-permute-start | bytes 393224 | tf_op jit(solution)/shard_map/ppermute | solution.py:181
  3.6 5.0 %collective-permute-start = (bf16[2,32768]{1,0:T(2,128)(2,1)}, bf16[2,32768]{1,0:T(2,128)(2,1)S(1)}, u32[]{:S(2)}, u32[]{:S(2)}) collective-permute-start(bf16[2,32768]{1,0:T(2,128)(2,1)} %bitcast.28), channel_id=1, source_target_pairs={{1,4},{0,5},{3,6},{2,7},{6,0},{7,1},{4,2},{5,3},{9,12},{8,13},{11,... | collective-permute-start | bytes 393224 | tf_op jit(solution)/shard_map/ppermute | solution.py:181
  9.5 4.9 %collective-permute-start.3 = (bf16[512,128]{1,0:T(8,128)(2,1)S(1)}, bf16[512,128]{1,0:T(8,128)(2,1)S(1)}, u32[]{:S(2)}, u32[]{:S(2)}) collective-permute-start(bf16[512,128]{1,0:T(8,128)(2,1)S(1)} %get-tuple-element.18), channel_id=1, source_target_pairs={{4,2},{5,3},{6,0},{7,1},{0,5},{1,4},{2,7},{3,6},{12,10},{13,11},{1... | collective-permute-start | bytes 393224 | tf_op jit(solution)/shard_map/ppermute | solution.py:181
  11.3 4.7 %collective-permute-start.4 = (bf16[512,128]{1,0:T(8,128)(2,1)S(1)}, bf16[512,128]{1,0:T(8,128)(2,1)S(1)}, u32[]{:S(2)}, u32[]{:S(2)}) collective-permute-start(bf16[512,128]{1,0:T(8,128)(2,1)S(1)} %get-tuple-element.19), channel_id=1, source_target_pairs={{4,24},{5,25},{6,26},{7,27},{0,6},{1,7},{2,4},{3,5},{12,0},{13,1},... | collective-permute-start | bytes 393224 | tf_op jit(solution)/shard_map/ppermute | solution.py:181
  12.9 4.4 %collective-permute-start.5 = (bf16[512,128]{1,0:T(8,128)(2,1)S(1)}, bf16[512,128]{1,0:T(8,128)(2,1)S(1)}, u32[]{:S(2)}, u32[]{:S(2)}) collective-permute-start(bf16[512,128]{1,0:T(8,128)(2,1)S(1)} %get-tuple-element.20), channel_id=1, source_target_pairs={{4,1},{5,0},{6,3},{7,2},{0,28},{1,29},{2,30},{3,31},{12,9},{13,8},... | collective-permute-start | bytes 393224 | tf_op jit(solution)/shard_map/ppermute | solution.py:181

commit v10 on v9

--- a/solution.py
+++ b/solution.py
@@ -119,9 +119,10 @@
     tw_cos, tw_sin = twiddle_ref[:rows], twiddle_ref[rows:]
     both = [(dot(row_cos, pair), dot(row_sin, pair)) for pair in pairs]
     stage = [turned(c[:, :LANES] + s[:, LANES:], c[:, LANES:] - s[:, :LANES], tw_cos, tw_sin) for c, s in both]
-    stage = [dot(field, forward_ref[...]) for field in stage]
-    stage = [(field * coulomb).astype(bf16) for field in stage]
-    stage = [dot(field, inverse_ref[...]) for field in stage]
+    stacked = dot(jnp.concatenate(stage, axis=0), forward_ref[...])
+    stacked = (stacked * jnp.concatenate([coulomb] * matches, axis=0)).astype(bf16)
+    stacked = dot(stacked, inverse_ref[...])
+    stage = [stacked[j * rows : (j + 1) * rows] for j in range(matches)]
     stage = [turned(field[:, :LANES], field[:, LANES:], tw_cos, -tw_sin) for field in stage]
     results = []
     total_real, total_imag = None, None

time: 18.2 us -> 18.2 us (level)
  no operation moved by 1% of the time
where the time goes in v10:
time: 18.2 us; the launch traced here: 18.1 us
  starting transfers between devices  8.1 us (45%)
  waiting for transfers between devices  6.91 us (38%)
  Pallas kernels  3.03 us (17%)
    ppermute x6, starting transfers between devices, moved(): return lax.ppermute(value, ('ka', 'ba'), pairs)  8.1 us
    ppermute x6, waiting for transfers between devices, moved(): return lax.ppermute(value, ('ka', 'ba'), pairs)  6.91 us
    pallas_call x1, Pallas kernels, per_device(): pl.pallas_call(lambda *refs: setup_kernel(lay, steps, *refs), out_shape=[...  1.4 us
    pallas_call x1, Pallas kernels, per_device(): pl.pallas_call(lambda *refs: exchange_kernel(rows, slots, *refs), out_sha...  0.88 us
    pallas_call x1, Pallas kernels, per_device(): pl.pallas_call(lambda *refs: sum_kernel(rows, *refs), out_shape=shape(2 *...  0.75 us
  transfers between devices with their start and end apart: 6, of which 5 were waited for; matrix products, arithmetic and copies ran while one was open for 0% of the time, Pallas kernels for 8%

profile of v10, /device:TPU:1, one launch (start us, length us, event | category | flops | bytes accessed | tf_op | source)
XLA Modules:
  0.0 18.1 jit_solution(2179578826695005960)
XLA Ops:
  0.0 0.0 copy-start
  0.0 2.7 %collective-permute-start.2 = (bf16[2,32768]{1,0:T(2,128)(2,1)}, bf16[2,32768]{1,0:T(2,128)(2,1)S(1)}, u32[]{:S(2)}, u32[]{:S(2)}) collective-permute-start(bf16[2,32768]{1,0:T(2,128)(2,1)} %bitcast.26), channel_id=1, source_target_pairs={{24,4},{25,5},{26,6},{27,7},{28,0},{29,1},{30,2},{31,3},{0,12},{1,... | collective-permute-start | bytes 393224 | tf_op jit(solution)/shard_map/ppermute | solution.py:182
  2.7 0.9 %collective-permute-start.1 = (bf16[2,32768]{1,0:T(2,128)(2,1)}, bf16[2,32768]{1,0:T(2,128)(2,1)S(1)}, u32[]{:S(2)}, u32[]{:S(2)}) collective-permute-start(bf16[2,32768]{1,0:T(2,128)(2,1)} %bitcast.27), channel_id=1, source_target_pairs={{2,4},{3,5},{0,6},{1,7},{5,0},{4,1},{7,2},{6,3},{10,12},{11,13},{8... | collective-permute-start | bytes 393224 | tf_op jit(solution)/shard_map/ppermute | solution.py:182
  3.6 0.8 %collective-permute-start = (bf16[2,32768]{1,0:T(2,128)(2,1)}, bf16[2,32768]{1,0:T(2,128)(2,1)S(1)}, u32[]{:S(2)}, u32[]{:S(2)}) collective-permute-start(bf16[2,32768]{1,0:T(2,128)(2,1)} %bitcast.28), channel_id=1, source_target_pairs={{1,4},{0,5},{3,6},{2,7},{6,0},{7,1},{4,2},{5,3},{9,12},{8,13},{11,... | collective-permute-start | bytes 393224 | tf_op jit(solution)/shard_map/ppermute | solution.py:182
  4.4 0.0 copy-done
  4.4 1.4 %setup.1 = (bf16[512,256]{1,0:T(8,128)(2,1)S(1)}, bf16[256,256]{1,0:T(8,128)(2,1)S(1)}, bf16[256,256]{1,0:T(8,128)(2,1)S(1)}, f32[512,128]{1,0:T(8,128)S(1)}, f32[256,128]{1,0:T(8,128)S(1)}) custom-call(s32[3,8]{1,0:T(4,128)S(1)} %bitcast.25), custom_call_target="tpu_custom_call" | custom-call | tf_op jit(solution)/shard_map/setup/pallas_call | solution.py:192
  5.8 2.3 %collective-permute-done.2 = bf16[2,32768]{1,0:T(2,128)(2,1)S(1)} collective-permute-done((bf16[2,32768]{1,0:T(2,128)(2,1)}, bf16[2,32768]{1,0:T(2,128)(2,1)S(1)}, u32[]{:S(2)}, u32[]{:S(2)}) %collective-permute-start.2) | collective-permute-done | bytes 131104 | tf_op jit(solution)/shard_map/ppermute | solution.py:182
  8.1 0.0 collective-permute-done.1
  8.1 0.5 %collective-permute-done = bf16[2,32768]{1,0:T(2,128)(2,1)S(1)} collective-permute-done((bf16[2,32768]{1,0:T(2,128)(2,1)}, bf16[2,32768]{1,0:T(2,128)(2,1)S(1)}, u32[]{:S(2)}, u32[]{:S(2)}) %collective-permute-start) | collective-permute-done | bytes 131104 | tf_op jit(solution)/shard_map/ppermute | solution.py:182
  8.6 0.9 %exchange.1 = (bf16[512,128]{1,0:T(8,128)(2,1)S(1)}, bf16[512,128]{1,0:T(8,128)(2,1)S(1)}, bf16[512,128]{1,0:T(8,128)(2,1)S(1)}) custom-call(bf16[512,128]{1,0:T(8,128)(2,1)S(1)} %bitcast.24, bf16[512,128]{1,0:T(8,128)(2,1)S(1)} %bitcast.23, bf16[512,128]{1,0:T(8,128)(2,1)S(1)} %bitcast.22, bf16[512,256]{1,0:T(8,128)(2,1)S(1)} %get-tuple-element.13.refs_3_, ...), custom_call_target="tpu_custom_call" | custom-call | tf_op jit(solution)/shard_map/exchange/pallas_call | solution.py:207
  9.5 1.8 %collective-permute-start.3 = (bf16[512,128]{1,0:T(8,128)(2,1)S(1)}, bf16[512,128]{1,0:T(8,128)(2,1)S(1)}, u32[]{:S(2)}, u32[]{:S(2)}) collective-permute-start(bf16[512,128]{1,0:T(8,128)(2,1)S(1)} %get-tuple-element.18), channel_id=1, source_target_pairs={{4,2},{5,3},{6,0},{7,1},{0,5},{1,4},{2,7},{3,6},{12,10},{13,11},{1... | collective-permute-start | bytes 393224 | tf_op jit(solution)/shard_map/ppermute | solution.py:182
  11.3 1.6 %collective-permute-start.4 = (bf16[512,128]{1,0:T(8,128)(2,1)S(1)}, bf16[512,128]{1,0:T(8,128)(2,1)S(1)}, u32[]{:S(2)}, u32[]{:S(2)}) collective-permute-start(bf16[512,128]{1,0:T(8,128)(2,1)S(1)} %get-tuple-element.19), channel_id=1, source_target_pairs={{4,24},{5,25},{6,26},{7,27},{0,6},{1,7},{2,4},{3,5},{12,0},{13,1},... | collective-permute-start | bytes 393224 | tf_op jit(solution)/shard_map/ppermute | solution.py:182
  12.9 0.2 %collective-permute-start.5 = (bf16[512,128]{1,0:T(8,128)(2,1)S(1)}, bf16[512,128]{1,0:T(8,128)(2,1)S(1)}, u32[]{:S(2)}, u32[]{:S(2)}) collective-permute-start(bf16[512,128]{1,0:T(8,128)(2,1)S(1)} %get-tuple-element.20), channel_id=1, source_target_pairs={{4,1},{5,0},{6,3},{7,2},{0,28},{1,29},{2,30},{3,31},{12,9},{13,8},... | collective-permute-start | bytes 393224 | tf_op jit(solution)/shard_map/ppermute | solution.py:182
  13.2 1.2 %collective-permute-done.3.refs_0_ = bf16[512,128]{1,0:T(8,128)(2,1)S(1)} collective-permute-done((bf16[512,128]{1,0:T(8,128)(2,1)S(1)}, bf16[512,128]{1,0:T(8,128)(2,1)S(1)}, u32[]{:S(2)}, u32[]{:S(2)}) %collective-permute-start.3) | collective-permute-done | bytes 131104 | tf_op jit(solution)/shard_map/ppermute | solution.py:182
  14.4 1.6 %collective-permute-done.4.refs_1_ = bf16[512,128]{1,0:T(8,128)(2,1)S(1)} collective-permute-done((bf16[512,128]{1,0:T(8,128)(2,1)S(1)}, bf16[512,128]{1,0:T(8,128)(2,1)S(1)}, u32[]{:S(2)}, u32[]{:S(2)}) %collective-permute-start.4) | collective-permute-done | bytes 131104 | tf_op jit(solution)/shard_map/ppermute | solution.py:182
  16.0 1.3 %collective-permute-done.5.refs_2_ = bf16[512,128]{1,0:T(8,128)(2,1)S(1)} collective-permute-done((bf16[512,128]{1,0:T(8,128)(2,1)S(1)}, bf16[512,128]{1,0:T(8,128)(2,1)S(1)}, u32[]{:S(2)}, u32[]{:S(2)}) %collective-permute-start.5) | collective-permute-done | bytes 131104 | tf_op jit(solution)/shard_map/ppermute | solution.py:182
  17.3 0.7 %total.1 = f32[512,128]{1,0:T(8,128)} custom-call(bf16[512,128]{1,0:T(8,128)(2,1)S(1)} %collective-permute-done.3.refs_0_, bf16[512,128]{1,0:T(8,128)(2,1)S(1)} %collective-permute-done.4.refs_1_, bf16[512,128]{1,0:T(8,128)(2,1)S(1)} %collective-permute-done.5.refs_2_), custom_call_target="tpu_custom_call" | custom-call | tf_op jit(solution)/shard_map/total/pallas_call | solution.py:217
Async XLA Ops:
  0.0 4.4 %copy-start = (s32[8,3]{0,1:T(4,128)S(1)}, s32[8,3]{0,1:T(4,128)}, u32[]{:S(2)}) copy-start(s32[8,3]{0,1:T(4,128)} %param.3) | copy-start | bytes 292
  0.0 8.1 %collective-permute-start.2 = (bf16[2,32768]{1,0:T(2,128)(2,1)}, bf16[2,32768]{1,0:T(2,128)(2,1)S(1)}, u32[]{:S(2)}, u32[]{:S(2)}) collective-permute-start(bf16[2,32768]{1,0:T(2,128)(2,1)} %bitcast.26), channel_id=1, source_target_pairs={{24,4},{25,5},{26,6},{27,7},{28,0},{29,1},{30,2},{31,3},{0,12},{1,... | collective-permute-start | bytes 393224 | tf_op jit(solution)/shard_map/ppermute | solution.py:182
  2.7 5.4 %collective-permute-start.1 = (bf16[2,32768]{1,0:T(2,128)(2,1)}, bf16[2,32768]{1,0:T(2,128)(2,1)S(1)}, u32[]{:S(2)}, u32[]{:S(2)}) collective-permute-start(bf16[2,32768]{1,0:T(2,128)(2,1)} %bitcast.27), channel_id=1, source_target_pairs={{2,4},{3,5},{0,6},{1,7},{5,0},{4,1},{7,2},{6,3},{10,12},{11,13},{8... | collective-permute-start | bytes 393224 | tf_op jit(solution)/shard_map/ppermute | solution.py:182
  3.6 5.0 %collective-permute-start = (bf16[2,32768]{1,0:T(2,128)(2,1)}, bf16[2,32768]{1,0:T(2,128)(2,1)S(1)}, u32[]{:S(2)}, u32[]{:S(2)}) collective-permute-start(bf16[2,32768]{1,0:T(2,128)(2,1)} %bitcast.28), channel_id=1, source_target_pairs={{1,4},{0,5},{3,6},{2,7},{6,0},{7,1},{4,2},{5,3},{9,12},{8,13},{11,... | collective-permute-start | bytes 393224 | tf_op jit(solution)/shard_map/ppermute | solution.py:182
  9.5 4.9 %collective-permute-start.3 = (bf16[512,128]{1,0:T(8,128)(2,1)S(1)}, bf16[512,128]{1,0:T(8,128)(2,1)S(1)}, u32[]{:S(2)}, u32[]{:S(2)}) collective-permute-start(bf16[512,128]{1,0:T(8,128)(2,1)S(1)} %get-tuple-element.18), channel_id=1, source_target_pairs={{4,2},{5,3},{6,0},{7,1},{0,5},{1,4},{2,7},{3,6},{12,10},{13,11},{1... | collective-permute-start | bytes 393224 | tf_op jit(solution)/shard_map/ppermute | solution.py:182
  11.3 4.7 %collective-permute-start.4 = (bf16[512,128]{1,0:T(8,128)(2,1)S(1)}, bf16[512,128]{1,0:T(8,128)(2,1)S(1)}, u32[]{:S(2)}, u32[]{:S(2)}) collective-permute-start(bf16[512,128]{1,0:T(8,128)(2,1)S(1)} %get-tuple-element.19), channel_id=1, source_target_pairs={{4,24},{5,25},{6,26},{7,27},{0,6},{1,7},{2,4},{3,5},{12,0},{13,1},... | collective-permute-start | bytes 393224 | tf_op jit(solution)/shard_map/ppermute | solution.py:182
  12.9 4.4 %collective-permute-start.5 = (bf16[512,128]{1,0:T(8,128)(2,1)S(1)}, bf16[512,128]{1,0:T(8,128)(2,1)S(1)}, u32[]{:S(2)}, u32[]{:S(2)}) collective-permute-start(bf16[512,128]{1,0:T(8,128)(2,1)S(1)} %get-tuple-element.20), channel_id=1, source_target_pairs={{4,1},{5,0},{6,3},{7,2},{0,28},{1,29},{2,30},{3,31},{12,9},{13,8},... | collective-permute-start | bytes 393224 | tf_op jit(solution)/shard_map/ppermute | solution.py:182

commit v11 on v6

--- a/solution.py
+++ b/solution.py
@@ -89,6 +89,10 @@
     return scratch[pl.ds(0, rows, 2), :], scratch[pl.ds(1, rows, 2), :]
 
 
+def early_kernel(rows, in_ref, out_ref, scratch):
+    out_ref[:rows], out_ref[rows:] = split_parts(in_ref, scratch, rows)
+
+
 def exchange_kernel(rows, slots, *refs):
     matches = len(slots[0]) - 1
     target_refs, source_ref, refs = refs[:matches], refs[matches], refs[matches + 1 :]
@@ -101,8 +105,11 @@
     def dot(a, b):
         return jnp.dot(a, b, preferred_element_type=f32)
 
-    s_real, s_imag = split_parts(source_ref, scratch[0], rows)
-    targets = [split_parts(target_refs[j], scratch[1 + j], rows) for j in range(matches)]
+    fields = []
+    for ref, space in zip([*target_refs, source_ref], scratch):
+        ready = ref.dtype == f32
+        fields.append((ref[:rows], ref[rows:]) if ready else split_parts(ref, space, rows))
+    targets, (s_real, s_imag) = fields[:matches], fields[matches]
     coulomb = coulomb_ref[...]
     coulomb = jnp.concatenate([coulomb, coulomb], axis=1)
 
@@ -203,6 +210,17 @@
         name="setup",
     )(kpoint_coords.T)
 
+    inputs = [interleaved(arrival, lay) for arrival in arrivals]
+    for early in [matches]:
+        inputs[early] = pl.pallas_call(
+            lambda *refs: early_kernel(rows, *refs),
+            out_shape=shape(2 * rows, LANES, dtype=jnp.float32),
+            in_specs=in_vmem(1),
+            out_specs=in_vmem(1)[0],
+            scratch_shapes=[pltpu.VMEM((2 * rows, LANES), jnp.float32)],
+            compiler_params=limits,
+            name="early",
+        )(inputs[early])
     outs = pl.pallas_call(
         lambda *refs: exchange_kernel(rows, slots, *refs),
         out_shape=[shape(2 * rows, LANES)] * (matches + 1),
@@ -211,7 +229,7 @@
         scratch_shapes=[pltpu.VMEM((2 * rows, LANES), jnp.float32)] * (matches + 1),
         compiler_params=limits,
         name="exchange",
-    )(*[interleaved(arrival, lay) for arrival in arrivals], *tables)
+    )(*inputs, *tables)
     returned = [moved(outs[step], step, slots, True) for step in straight]
     total = pl.pallas_call(
         lambda *refs: sum_kernel(rows, *refs),

time: 18.2 us -> 18.2 us (level)
  no operation moved by 1% of the time
where the time goes in v11:
time: 18.2 us; the launch traced here: 18.1 us
  starting transfers between devices  8.49 us (47%)
  waiting for transfers between devices  6.5 us (36%)
  Pallas kernels  3.06 us (17%)
    ppermute x6, starting transfers between devices, moved(): return lax.ppermute(value, ('ka', 'ba'), pairs)  8.49 us
    ppermute x6, waiting for transfers between devices, moved(): return lax.ppermute(value, ('ka', 'ba'), pairs)  6.5 us
    pallas_call x1, Pallas kernels, per_device(): pl.pallas_call(lambda *refs: setup_kernel(lay, steps, *refs), out_shape=[...  1.4 us
    pallas_call x1, Pallas kernels, per_device(): pl.pallas_call(lambda *refs: exchange_kernel(rows, slots, *refs), out_sha...  0.87 us
    pallas_call x1, Pallas kernels, per_device(): pl.pallas_call(lambda *refs: sum_kernel(rows, *refs), out_shape=shape(2 *...  0.75 us
  transfers between devices with their start and end apart: 6, of which 5 were waited for; matrix products, arithmetic and copies ran while one was open for 0% of the time, Pallas kernels for 8%

profile of v11, /device:TPU:1, one launch (start us, length us, event | category | flops | bytes accessed | tf_op | source)
XLA Modules:
  0.0 18.1 jit_solution(11574067237464173615)
XLA Ops:
  0.0 0.0 copy-start
  0.0 2.7 %collective-permute-start.2 = (bf16[2,32768]{1,0:T(2,128)(2,1)}, bf16[2,32768]{1,0:T(2,128)(2,1)S(1)}, u32[]{:S(2)}, u32[]{:S(2)}) collective-permute-start(bf16[2,32768]{1,0:T(2,128)(2,1)} %bitcast.26), channel_id=1, source_target_pairs={{24,4},{25,5},{26,6},{27,7},{28,0},{29,1},{30,2},{31,3},{0,12},{1,... | collective-permute-start | bytes 393224 | tf_op jit(solution)/shard_map/ppermute | solution.py:188
  2.7 0.9 %collective-permute-start.1 = (bf16[2,32768]{1,0:T(2,128)(2,1)}, bf16[2,32768]{1,0:T(2,128)(2,1)S(1)}, u32[]{:S(2)}, u32[]{:S(2)}) collective-permute-start(bf16[2,32768]{1,0:T(2,128)(2,1)} %bitcast.27), channel_id=1, source_target_pairs={{2,4},{3,5},{0,6},{1,7},{5,0},{4,1},{7,2},{6,3},{10,12},{11,13},{8... | collective-permute-start | bytes 393224 | tf_op jit(solution)/shard_map/ppermute | solution.py:188
  3.6 0.8 %collective-permute-start = (bf16[2,32768]{1,0:T(2,128)(2,1)}, bf16[2,32768]{1,0:T(2,128)(2,1)S(1)}, u32[]{:S(2)}, u32[]{:S(2)}) collective-permute-start(bf16[2,32768]{1,0:T(2,128)(2,1)} %bitcast.28), channel_id=1, source_target_pairs={{1,4},{0,5},{3,6},{2,7},{6,0},{7,1},{4,2},{5,3},{9,12},{8,13},{11,... | collective-permute-start | bytes 393224 | tf_op jit(solution)/shard_map/ppermute | solution.py:188
  4.4 0.0 copy-done
  4.4 1.4 %setup.1 = (bf16[512,256]{1,0:T(8,128)(2,1)S(1)}, bf16[256,256]{1,0:T(8,128)(2,1)S(1)}, bf16[256,256]{1,0:T(8,128)(2,1)S(1)}, f32[512,128]{1,0:T(8,128)S(1)}, f32[256,128]{1,0:T(8,128)S(1)}) custom-call(s32[3,8]{1,0:T(4,128)S(1)} %bitcast.25), custom_call_target="tpu_custom_call" | custom-call | tf_op jit(solution)/shard_map/setup/pallas_call | solution.py:198
  5.8 2.3 %collective-permute-done.2 = bf16[2,32768]{1,0:T(2,128)(2,1)S(1)} collective-permute-done((bf16[2,32768]{1,0:T(2,128)(2,1)}, bf16[2,32768]{1,0:T(2,128)(2,1)S(1)}, u32[]{:S(2)}, u32[]{:S(2)}) %collective-permute-start.2) | collective-permute-done | bytes 131104 | tf_op jit(solution)/shard_map/ppermute | solution.py:188
  8.2 0.0 collective-permute-done.1
  8.2 0.4 %collective-permute-done = bf16[2,32768]{1,0:T(2,128)(2,1)S(1)} collective-permute-done((bf16[2,32768]{1,0:T(2,128)(2,1)}, bf16[2,32768]{1,0:T(2,128)(2,1)S(1)}, u32[]{:S(2)}, u32[]{:S(2)}) %collective-permute-start) | collective-permute-done | bytes 131104 | tf_op jit(solution)/shard_map/ppermute | solution.py:188
  8.6 0.9 %exchange.1 = (bf16[512,128]{1,0:T(8,128)(2,1)S(1)}, bf16[512,128]{1,0:T(8,128)(2,1)S(1)}, bf16[512,128]{1,0:T(8,128)(2,1)S(1)}) custom-call(bf16[512,128]{1,0:T(8,128)(2,1)S(1)} %bitcast.24, bf16[512,128]{1,0:T(8,128)(2,1)S(1)} %bitcast.23, f32[512,128]{1,0:T(8,128)S(1)} %early.1.refs_2_, bf16[512,256]{1,0:T(8,128)(2,1)S(1)} %get-tuple-element.13.refs_3_, ...), custom_call_target="tpu_custom_call" | custom-call | tf_op jit(solution)/shard_map/exchange/pallas_call | solution.py:224
  9.5 1.8 %collective-permute-start.3 = (bf16[512,128]{1,0:T(8,128)(2,1)S(1)}, bf16[512,128]{1,0:T(8,128)(2,1)S(1)}, u32[]{:S(2)}, u32[]{:S(2)}) collective-permute-start(bf16[512,128]{1,0:T(8,128)(2,1)S(1)} %get-tuple-element.18), channel_id=1, source_target_pairs={{4,2},{5,3},{6,0},{7,1},{0,28},{1,29},{2,30},{3,31},{12,10},{13,11... | collective-permute-start | bytes 393224 | tf_op jit(solution)/shard_map/ppermute | solution.py:188
  11.3 1.6 %collective-permute-start.4 = (bf16[512,128]{1,0:T(8,128)(2,1)S(1)}, bf16[512,128]{1,0:T(8,128)(2,1)S(1)}, u32[]{:S(2)}, u32[]{:S(2)}) collective-permute-start(bf16[512,128]{1,0:T(8,128)(2,1)S(1)} %get-tuple-element.19), channel_id=1, source_target_pairs={{4,1},{5,0},{6,3},{7,2},{0,6},{1,7},{2,4},{3,5},{12,9},{13,8},{14,... | collective-permute-start | bytes 393224 | tf_op jit(solution)/shard_map/ppermute | solution.py:188
  12.9 0.6 %collective-permute-start.5 = (bf16[512,128]{1,0:T(8,128)(2,1)S(1)}, bf16[512,128]{1,0:T(8,128)(2,1)S(1)}, u32[]{:S(2)}, u32[]{:S(2)}) collective-permute-start(bf16[512,128]{1,0:T(8,128)(2,1)S(1)} %get-tuple-element.20), channel_id=1, source_target_pairs={{4,24},{5,25},{6,26},{7,27},{0,5},{1,4},{2,7},{3,6},{12,0},{13,1},... | collective-permute-start | bytes 393224 | tf_op jit(solution)/shard_map/ppermute | solution.py:188
  13.5 0.8 %collective-permute-done.3.refs_0_ = bf16[512,128]{1,0:T(8,128)(2,1)S(1)} collective-permute-done((bf16[512,128]{1,0:T(8,128)(2,1)S(1)}, bf16[512,128]{1,0:T(8,128)(2,1)S(1)}, u32[]{:S(2)}, u32[]{:S(2)}) %collective-permute-start.3) | collective-permute-done | bytes 131104 | tf_op jit(solution)/shard_map/ppermute | solution.py:188
  14.3 1.7 %collective-permute-done.4.refs_1_ = bf16[512,128]{1,0:T(8,128)(2,1)S(1)} collective-permute-done((bf16[512,128]{1,0:T(8,128)(2,1)S(1)}, bf16[512,128]{1,0:T(8,128)(2,1)S(1)}, u32[]{:S(2)}, u32[]{:S(2)}) %collective-permute-start.4) | collective-permute-done | bytes 131104 | tf_op jit(solution)/shard_map/ppermute | solution.py:188
  16.0 1.3 %collective-permute-done.5.refs_2_ = bf16[512,128]{1,0:T(8,128)(2,1)S(1)} collective-permute-done((bf16[512,128]{1,0:T(8,128)(2,1)S(1)}, bf16[512,128]{1,0:T(8,128)(2,1)S(1)}, u32[]{:S(2)}, u32[]{:S(2)}) %collective-permute-start.5) | collective-permute-done | bytes 131104 | tf_op jit(solution)/shard_map/ppermute | solution.py:188
  17.3 0.7 %total.1 = f32[512,128]{1,0:T(8,128)} custom-call(bf16[512,128]{1,0:T(8,128)(2,1)S(1)} %collective-permute-done.3.refs_0_, bf16[512,128]{1,0:T(8,128)(2,1)S(1)} %collective-permute-done.4.refs_1_, bf16[512,128]{1,0:T(8,128)(2,1)S(1)} %collective-permute-done.5.refs_2_), custom_call_target="tpu_custom_call" | custom-call | tf_op jit(solution)/shard_map/total/pallas_call | solution.py:234
  (1 shorter events, 0.0 us)
Async XLA Ops:
  0.0 4.4 %copy-start = (s32[8,3]{0,1:T(4,128)S(1)}, s32[8,3]{0,1:T(4,128)}, u32[]{:S(2)}) copy-start(s32[8,3]{0,1:T(4,128)} %param.3) | copy-start | bytes 292
  0.0 8.1 %collective-permute-start.2 = (bf16[2,32768]{1,0:T(2,128)(2,1)}, bf16[2,32768]{1,0:T(2,128)(2,1)S(1)}, u32[]{:S(2)}, u32[]{:S(2)}) collective-permute-start(bf16[2,32768]{1,0:T(2,128)(2,1)} %bitcast.26), channel_id=1, source_target_pairs={{24,4},{25,5},{26,6},{27,7},{28,0},{29,1},{30,2},{31,3},{0,12},{1,... | collective-permute-start | bytes 393224 | tf_op jit(solution)/shard_map/ppermute | solution.py:188
  2.7 5.5 %collective-permute-start.1 = (bf16[2,32768]{1,0:T(2,128)(2,1)}, bf16[2,32768]{1,0:T(2,128)(2,1)S(1)}, u32[]{:S(2)}, u32[]{:S(2)}) collective-permute-start(bf16[2,32768]{1,0:T(2,128)(2,1)} %bitcast.27), channel_id=1, source_target_pairs={{2,4},{3,5},{0,6},{1,7},{5,0},{4,1},{7,2},{6,3},{10,12},{11,13},{8... | collective-permute-start | bytes 393224 | tf_op jit(solution)/shard_map/ppermute | solution.py:188
  3.6 5.0 %collective-permute-start = (bf16[2,32768]{1,0:T(2,128)(2,1)}, bf16[2,32768]{1,0:T(2,128)(2,1)S(1)}, u32[]{:S(2)}, u32[]{:S(2)}) collective-permute-start(bf16[2,32768]{1,0:T(2,128)(2,1)} %bitcast.28), channel_id=1, source_target_pairs={{1,4},{0,5},{3,6},{2,7},{6,0},{7,1},{4,2},{5,3},{9,12},{8,13},{11,... | collective-permute-start | bytes 393224 | tf_op jit(solution)/shard_map/ppermute | solution.py:188
  9.5 4.8 %collective-permute-start.3 = (bf16[512,128]{1,0:T(8,128)(2,1)S(1)}, bf16[512,128]{1,0:T(8,128)(2,1)S(1)}, u32[]{:S(2)}, u32[]{:S(2)}) collective-permute-start(bf16[512,128]{1,0:T(8,128)(2,1)S(1)} %get-tuple-element.18), channel_id=1, source_target_pairs={{4,2},{5,3},{6,0},{7,1},{0,28},{1,29},{2,30},{3,31},{12,10},{13,11... | collective-permute-start | bytes 393224 | tf_op jit(solution)/shard_map/ppermute | solution.py:188
  11.3 4.7 %collective-permute-start.4 = (bf16[512,128]{1,0:T(8,128)(2,1)S(1)}, bf16[512,128]{1,0:T(8,128)(2,1)S(1)}, u32[]{:S(2)}, u32[]{:S(2)}) collective-permute-start(bf16[512,128]{1,0:T(8,128)(2,1)S(1)} %get-tuple-element.19), channel_id=1, source_target_pairs={{4,1},{5,0},{6,3},{7,2},{0,6},{1,7},{2,4},{3,5},{12,9},{13,8},{14,... | collective-permute-start | bytes 393224 | tf_op jit(solution)/shard_map/ppermute | solution.py:188
  12.9 4.4 %collective-permute-start.5 = (bf16[512,128]{1,0:T(8,128)(2,1)S(1)}, bf16[512,128]{1,0:T(8,128)(2,1)S(1)}, u32[]{:S(2)}, u32[]{:S(2)}) collective-permute-start(bf16[512,128]{1,0:T(8,128)(2,1)S(1)} %get-tuple-element.20), channel_id=1, source_target_pairs={{4,24},{5,25},{6,26},{7,27},{0,5},{1,4},{2,7},{3,6},{12,0},{13,1},... | collective-permute-start | bytes 393224 | tf_op jit(solution)/shard_map/ppermute | solution.py:188

commit v12 on v9

--- a/solution.py
+++ b/solution.py
@@ -175,7 +175,7 @@
                 if part == matches:
                     home = (k - steps) % kpoints * groups + b
                 else:
-                    home = k * groups + (b ^ 2 ** ((part + parity(k, kpoints)) % matches))
+                    home = k * groups + (b ^ 2 ** ((part + parity(k, kpoints) + 1) % matches))
                 away = worker(k, kpoints) * groups + b
                 pairs.append((away, home) if back else (home, away))
         return lax.ppermute(value, ("ka", "ba"), pairs)

time: 18.2 us -> 18.2 us (level)
  no operation moved by 1% of the time
where the time goes in v12:
time: 18.2 us; the launch traced here: 18.1 us
  starting transfers between devices  8.13 us (45%)
  waiting for transfers between devices  6.92 us (38%)
  Pallas kernels  3.03 us (17%)
    ppermute x6, starting transfers between devices, moved(): return lax.ppermute(value, ('ka', 'ba'), pairs)  8.13 us
    ppermute x6, waiting for transfers between devices, moved(): return lax.ppermute(value, ('ka', 'ba'), pairs)  6.92 us
    pallas_call x1, Pallas kernels, per_device(): pl.pallas_call(lambda *refs: setup_kernel(lay, steps, *refs), out_shape=[...  1.4 us
    pallas_call x1, Pallas kernels, per_device(): pl.pallas_call(lambda *refs: exchange_kernel(rows, slots, *refs), out_sha...  0.88 us
    pallas_call x1, Pallas kernels, per_device(): pl.pallas_call(lambda *refs: sum_kernel(rows, *refs), out_shape=shape(2 *...  0.75 us
  transfers between devices with their start and end apart: 6, of which 5 were waited for; matrix products, arithmetic and copies ran while one was open for 0% of the time, Pallas kernels for 8%

profile of v12, /device:TPU:1, one launch (start us, length us, event | category | flops | bytes accessed | tf_op | source)
XLA Modules:
  0.0 18.1 jit_solution(375066340410754694)
XLA Ops:
  0.0 0.0 copy-start
  0.0 2.7 %collective-permute-start.2 = (bf16[2,32768]{1,0:T(2,128)(2,1)}, bf16[2,32768]{1,0:T(2,128)(2,1)S(1)}, u32[]{:S(2)}, u32[]{:S(2)}) collective-permute-start(bf16[2,32768]{1,0:T(2,128)(2,1)} %bitcast.26), channel_id=1, source_target_pairs={{24,4},{25,5},{26,6},{27,7},{28,0},{29,1},{30,2},{31,3},{0,12},{1,... | collective-permute-start | bytes 393224 | tf_op jit(solution)/shard_map/ppermute | solution.py:181
  2.7 1.0 %collective-permute-start.1 = (bf16[2,32768]{1,0:T(2,128)(2,1)}, bf16[2,32768]{1,0:T(2,128)(2,1)S(1)}, u32[]{:S(2)}, u32[]{:S(2)}) collective-permute-start(bf16[2,32768]{1,0:T(2,128)(2,1)} %bitcast.27), channel_id=1, source_target_pairs={{1,4},{0,5},{3,6},{2,7},{6,0},{7,1},{4,2},{5,3},{9,12},{8,13},{11,... | collective-permute-start | bytes 393224 | tf_op jit(solution)/shard_map/ppermute | solution.py:181
  3.6 0.8 %collective-permute-start = (bf16[2,32768]{1,0:T(2,128)(2,1)}, bf16[2,32768]{1,0:T(2,128)(2,1)S(1)}, u32[]{:S(2)}, u32[]{:S(2)}) collective-permute-start(bf16[2,32768]{1,0:T(2,128)(2,1)} %bitcast.28), channel_id=1, source_target_pairs={{2,4},{3,5},{0,6},{1,7},{5,0},{4,1},{7,2},{6,3},{10,12},{11,13},{8... | collective-permute-start | bytes 393224 | tf_op jit(solution)/shard_map/ppermute | solution.py:181
  4.4 0.0 copy-done
  4.4 1.4 %setup.1 = (bf16[512,256]{1,0:T(8,128)(2,1)S(1)}, bf16[256,256]{1,0:T(8,128)(2,1)S(1)}, bf16[256,256]{1,0:T(8,128)(2,1)S(1)}, f32[512,128]{1,0:T(8,128)S(1)}, f32[256,128]{1,0:T(8,128)S(1)}) custom-call(s32[3,8]{1,0:T(4,128)S(1)} %bitcast.25), custom_call_target="tpu_custom_call" | custom-call | tf_op jit(solution)/shard_map/setup/pallas_call | solution.py:191
  5.8 2.3 %collective-permute-done.2 = bf16[2,32768]{1,0:T(2,128)(2,1)S(1)} collective-permute-done((bf16[2,32768]{1,0:T(2,128)(2,1)}, bf16[2,32768]{1,0:T(2,128)(2,1)S(1)}, u32[]{:S(2)}, u32[]{:S(2)}) %collective-permute-start.2) | collective-permute-done | bytes 131104 | tf_op jit(solution)/shard_map/ppermute | solution.py:181
  8.1 0.0 collective-permute-done.1
  8.1 0.5 %collective-permute-done = bf16[2,32768]{1,0:T(2,128)(2,1)S(1)} collective-permute-done((bf16[2,32768]{1,0:T(2,128)(2,1)}, bf16[2,32768]{1,0:T(2,128)(2,1)S(1)}, u32[]{:S(2)}, u32[]{:S(2)}) %collective-permute-start) | collective-permute-done | bytes 131104 | tf_op jit(solution)/shard_map/ppermute | solution.py:181
  8.6 0.9 %exchange.1 = (bf16[512,128]{1,0:T(8,128)(2,1)S(1)}, bf16[512,128]{1,0:T(8,128)(2,1)S(1)}, bf16[512,128]{1,0:T(8,128)(2,1)S(1)}) custom-call(bf16[512,128]{1,0:T(8,128)(2,1)S(1)} %bitcast.24, bf16[512,128]{1,0:T(8,128)(2,1)S(1)} %bitcast.23, bf16[512,128]{1,0:T(8,128)(2,1)S(1)} %bitcast.22, bf16[512,256]{1,0:T(8,128)(2,1)S(1)} %get-tuple-element.13.refs_3_, ...), custom_call_target="tpu_custom_call" | custom-call | tf_op jit(solution)/shard_map/exchange/pallas_call | solution.py:206
  9.5 1.8 %collective-permute-start.3 = (bf16[512,128]{1,0:T(8,128)(2,1)S(1)}, bf16[512,128]{1,0:T(8,128)(2,1)S(1)}, u32[]{:S(2)}, u32[]{:S(2)}) collective-permute-start(bf16[512,128]{1,0:T(8,128)(2,1)S(1)} %get-tuple-element.18), channel_id=1, source_target_pairs={{4,1},{5,0},{6,3},{7,2},{0,6},{1,7},{2,4},{3,5},{12,9},{13,8},{14,... | collective-permute-start | bytes 393224 | tf_op jit(solution)/shard_map/ppermute | solution.py:181
  11.3 1.6 %collective-permute-start.4 = (bf16[512,128]{1,0:T(8,128)(2,1)S(1)}, bf16[512,128]{1,0:T(8,128)(2,1)S(1)}, u32[]{:S(2)}, u32[]{:S(2)}) collective-permute-start(bf16[512,128]{1,0:T(8,128)(2,1)S(1)} %get-tuple-element.19), channel_id=1, source_target_pairs={{4,24},{5,25},{6,26},{7,27},{0,5},{1,4},{2,7},{3,6},{12,0},{13,1},... | collective-permute-start | bytes 393224 | tf_op jit(solution)/shard_map/ppermute | solution.py:181
  13.0 0.2 %collective-permute-start.5 = (bf16[512,128]{1,0:T(8,128)(2,1)S(1)}, bf16[512,128]{1,0:T(8,128)(2,1)S(1)}, u32[]{:S(2)}, u32[]{:S(2)}) collective-permute-start(bf16[512,128]{1,0:T(8,128)(2,1)S(1)} %get-tuple-element.20), channel_id=1, source_target_pairs={{4,2},{5,3},{6,0},{7,1},{0,28},{1,29},{2,30},{3,31},{12,10},{13,11... | collective-permute-start | bytes 393224 | tf_op jit(solution)/shard_map/ppermute | solution.py:181
  13.2 1.2 %collective-permute-done.3.refs_0_ = bf16[512,128]{1,0:T(8,128)(2,1)S(1)} collective-permute-done((bf16[512,128]{1,0:T(8,128)(2,1)S(1)}, bf16[512,128]{1,0:T(8,128)(2,1)S(1)}, u32[]{:S(2)}, u32[]{:S(2)}) %collective-permute-start.3) | collective-permute-done | bytes 131104 | tf_op jit(solution)/shard_map/ppermute | solution.py:181
  14.4 1.6 %collective-permute-done.4.refs_1_ = bf16[512,128]{1,0:T(8,128)(2,1)S(1)} collective-permute-done((bf16[512,128]{1,0:T(8,128)(2,1)S(1)}, bf16[512,128]{1,0:T(8,128)(2,1)S(1)}, u32[]{:S(2)}, u32[]{:S(2)}) %collective-permute-start.4) | collective-permute-done | bytes 131104 | tf_op jit(solution)/shard_map/ppermute | solution.py:181
  16.0 1.3 %collective-permute-done.5.refs_2_ = bf16[512,128]{1,0:T(8,128)(2,1)S(1)} collective-permute-done((bf16[512,128]{1,0:T(8,128)(2,1)S(1)}, bf16[512,128]{1,0:T(8,128)(2,1)S(1)}, u32[]{:S(2)}, u32[]{:S(2)}) %collective-permute-start.5) | collective-permute-done | bytes 131104 | tf_op jit(solution)/shard_map/ppermute | solution.py:181
  17.4 0.7 %total.1 = f32[512,128]{1,0:T(8,128)} custom-call(bf16[512,128]{1,0:T(8,128)(2,1)S(1)} %collective-permute-done.3.refs_0_, bf16[512,128]{1,0:T(8,128)(2,1)S(1)} %collective-permute-done.4.refs_1_, bf16[512,128]{1,0:T(8,128)(2,1)S(1)} %collective-permute-done.5.refs_2_), custom_call_target="tpu_custom_call" | custom-call | tf_op jit(solution)/shard_map/total/pallas_call | solution.py:216
Async XLA Ops:
  0.0 4.4 %copy-start = (s32[8,3]{0,1:T(4,128)S(1)}, s32[8,3]{0,1:T(4,128)}, u32[]{:S(2)}) copy-start(s32[8,3]{0,1:T(4,128)} %param.3) | copy-start | bytes 292
  0.0 8.1 %collective-permute-start.2 = (bf16[2,32768]{1,0:T(2,128)(2,1)}, bf16[2,32768]{1,0:T(2,128)(2,1)S(1)}, u32[]{:S(2)}, u32[]{:S(2)}) collective-permute-start(bf16[2,32768]{1,0:T(2,128)(2,1)} %bitcast.26), channel_id=1, source_target_pairs={{24,4},{25,5},{26,6},{27,7},{28,0},{29,1},{30,2},{31,3},{0,12},{1,... | collective-permute-start | bytes 393224 | tf_op jit(solution)/shard_map/ppermute | solution.py:181
  2.7 5.4 %collective-permute-start.1 = (bf16[2,32768]{1,0:T(2,128)(2,1)}, bf16[2,32768]{1,0:T(2,128)(2,1)S(1)}, u32[]{:S(2)}, u32[]{:S(2)}) collective-permute-start(bf16[2,32768]{1,0:T(2,128)(2,1)} %bitcast.27), channel_id=1, source_target_pairs={{1,4},{0,5},{3,6},{2,7},{6,0},{7,1},{4,2},{5,3},{9,12},{8,13},{11,... | collective-permute-start | bytes 393224 | tf_op jit(solution)/shard_map/ppermute | solution.py:181
  3.6 5.0 %collective-permute-start = (bf16[2,32768]{1,0:T(2,128)(2,1)}, bf16[2,32768]{1,0:T(2,128)(2,1)S(1)}, u32[]{:S(2)}, u32[]{:S(2)}) collective-permute-start(bf16[2,32768]{1,0:T(2,128)(2,1)} %bitcast.28), channel_id=1, source_target_pairs={{2,4},{3,5},{0,6},{1,7},{5,0},{4,1},{7,2},{6,3},{10,12},{11,13},{8... | collective-permute-start | bytes 393224 | tf_op jit(solution)/shard_map/ppermute | solution.py:181
  9.5 4.9 %collective-permute-start.3 = (bf16[512,128]{1,0:T(8,128)(2,1)S(1)}, bf16[512,128]{1,0:T(8,128)(2,1)S(1)}, u32[]{:S(2)}, u32[]{:S(2)}) collective-permute-start(bf16[512,128]{1,0:T(8,128)(2,1)S(1)} %get-tuple-element.18), channel_id=1, source_target_pairs={{4,1},{5,0},{6,3},{7,2},{0,6},{1,7},{2,4},{3,5},{12,9},{13,8},{14,... | collective-permute-start | bytes 393224 | tf_op jit(solution)/shard_map/ppermute | solution.py:181
  11.3 4.7 %collective-permute-start.4 = (bf16[512,128]{1,0:T(8,128)(2,1)S(1)}, bf16[512,128]{1,0:T(8,128)(2,1)S(1)}, u32[]{:S(2)}, u32[]{:S(2)}) collective-permute-start(bf16[512,128]{1,0:T(8,128)(2,1)S(1)} %get-tuple-element.19), channel_id=1, source_target_pairs={{4,24},{5,25},{6,26},{7,27},{0,5},{1,4},{2,7},{3,6},{12,0},{13,1},... | collective-permute-start | bytes 393224 | tf_op jit(solution)/shard_map/ppermute | solution.py:181
  13.0 4.4 %collective-permute-start.5 = (bf16[512,128]{1,0:T(8,128)(2,1)S(1)}, bf16[512,128]{1,0:T(8,128)(2,1)S(1)}, u32[]{:S(2)}, u32[]{:S(2)}) collective-permute-start(bf16[512,128]{1,0:T(8,128)(2,1)S(1)} %get-tuple-element.20), channel_id=1, source_target_pairs={{4,2},{5,3},{6,0},{7,1},{0,28},{1,29},{2,30},{3,31},{12,10},{13,11... | collective-permute-start | bytes 393224 | tf_op jit(solution)/shard_map/ppermute | solution.py:181
